TPU v7x, 128 devices: a whole 4x4x4 slice. The times are simulated.
128 devices in a mesh: section: 4 (over x), brick: 32 (over y, z, core).
Axes of the slice: x: 4, y: 4, z: 4, core: 2. Of those that a mesh axis runs over, the one named last changes fastest.
Arguments:
- saved_inputs: bfloat16 [4, 2, 64, 8, 8, 8, 128], P('section', None, 'brick'), may hold values from -6 to 6
- saved_preacts: bfloat16 [4, 2, 64, 8, 8, 8, 128], P('section', None, 'brick'), may hold values from -6 to 6
- supervision: bfloat16 [4, 2, 64, 8, 8, 8, 128], P('section', None, 'brick'), may hold values from -6 to 6
- weights: bfloat16 [4, 3456, 128], P('section'), may hold values from -0.109375 to 0.109375
- trainer: int32 [2, 64], replicated, may hold values from 0 to 31, as said below
- counts: int32 [2, 64], P(None, 'brick'), may hold values from 1 to 512
Outputs:
- skip_grads: bfloat16 [4, 2, 128, 8, 8, 8, 128], P('section', None, 'brick')
- weight_grads: float32 [4, 3456, 128], P('section')
Inputs may be any that keep to these rules, and one draw needn't show every extreme that they name: For each micro-batch, an owner's 2 bricks go to 2 different trainers among the owner itself and the 3 owners after it (owner + 0 to owner + 3, modulo 64 // 2); so no trainer receives more than 4 bricks of one micro-batch, and some trainer receives exactly 4.
All inputs are finite; a program needn't handle non-finite values.
Results may differ from a plain program's by a relative error of at most 0.02.
Values may be sent and summed in bfloat16 or wider, within the bound.
No kernel may reach another device: no remote copies, remote signals or barrier semaphores. Data moves between devices by JAX's collectives and lax.ppermute only.
A program may use at most 128 MiB of HBM per device.

v0:
```python
import math

import jax
import jax.numpy as jnp
from jax import lax
from jax.sharding import PartitionSpec as P


def shifted_2(block, axis, distance):
    devices = range(lax.axis_size(axis))
    route = [((i - distance) % len(devices), i) for i in devices]
    return lax.ppermute(block, axis, route)


def passed_along(shard, axis, by):
    devices = lax.axis_size(axis)
    pairs = [(i, i + by) for i in range(devices) if 0 <= i + by < devices]
    return lax.ppermute(shard, axis, pairs)


def columns(brick):
    brick_edge = brick.shape[0]
    padded = jnp.pad(brick, ((1, 1), (1, 1), (1, 1), (0, 0)))
    shifted = [
        padded[a : a + brick_edge, b : b + brick_edge, c : c + brick_edge, :]
        for a in range(3)
        for b in range(3)
        for c in range(3)
    ]
    return jnp.concatenate(shifted, axis=-1).reshape(brick_edge * brick_edge * brick_edge, -1)


def silu_slope(preacts):
    sigmoid_pre = jax.nn.sigmoid(preacts)
    return sigmoid_pre * (1.0 + preacts * (1.0 - sigmoid_pre))


def slot_backward(flipped, preacts_one, grad_out):
    deltas = (grad_out * silu_slope(preacts_one.astype(jnp.float32))).astype(jnp.bfloat16)
    grad_input = jnp.dot(columns(deltas), flipped, preferred_element_type=jnp.float32)
    return (deltas, grad_input.astype(jnp.bfloat16).reshape(deltas.shape))


def weight_term(inputs_one, deltas):
    flat_deltas = deltas.reshape(-1, deltas.shape[-1])
    return lax.dot_general(
        columns(inputs_one),
        flat_deltas,
        (((0,), (0,)), ((), ())),
        preferred_element_type=jnp.float32,
    )


def by_offset(rows_in, offsets, distance):
    match = (offsets == distance).reshape((-1,) + (1,) * (rows_in.ndim - 1))
    return jnp.sum(jnp.where(match, rows_in, jnp.zeros_like(rows_in)), axis=0)


def shards(saved_inputs, saved_preacts, supervision, weights, trainer, counts):
    peer_count = lax.axis_size("brick")
    my_index = lax.axis_index("brick")
    layer_count = lax.axis_size("section")
    section_index = lax.axis_index("section")
    micro_count = saved_inputs.shape[1]
    own_count = saved_inputs.shape[2]
    channels = saved_inputs.shape[-1]
    voxels = saved_inputs.shape[3] * saved_inputs.shape[4] * saved_inputs.shape[5]
    slot_count = 2 * own_count
    flipped = (
        weights[0]
        .reshape(27, channels, channels)[::-1]
        .transpose(0, 2, 1)
        .reshape(27 * channels, channels)
    )
    label_share = counts.astype(jnp.float32) / voxels
    inputs_own = saved_inputs[0]
    preacts_own = saved_preacts[0]
    weighted = (
        supervision[0].astype(jnp.float32) * label_share[:, :, None, None, None, None]
    ).astype(jnp.bfloat16)
    my_targets = lax.dynamic_slice_in_dim(trainer, my_index * own_count, own_count, 1)
    my_offsets = jnp.mod(my_targets - my_index, peer_count)

    def packed(rows_in, distance):
        return jnp.stack(
            [
                by_offset(rows_in[micro_pos], my_offsets[micro_pos], distance)
                for micro_pos in range(micro_count)
            ]
        )

    slot_inputs = []
    slot_preacts = []
    slot_weighted = []
    for distance in range(slot_count):
        sent_inputs = packed(inputs_own, distance)
        sent_preacts = packed(preacts_own, distance)
        sent_weighted = packed(weighted, distance)
        if distance > 0:
            sent_inputs, sent_preacts, sent_weighted = shifted_2(
                (sent_inputs, sent_preacts, sent_weighted), "brick", distance
            )
        slot_inputs.append(sent_inputs)
        slot_preacts.append(sent_preacts)
        slot_weighted.append(sent_weighted)
    work_inputs = jnp.stack(slot_inputs, axis=1)
    work_preacts = jnp.stack(slot_preacts, axis=1)
    work_weighted = jnp.stack(slot_weighted, axis=1)
    tick_count = layer_count + micro_count - 1
    brick_shape = work_inputs.shape[1:]
    above = jnp.zeros(brick_shape, jnp.bfloat16)
    grad_inputs = jnp.zeros(work_inputs.shape, jnp.bfloat16)
    accumulated = jnp.zeros((27 * channels, channels), jnp.float32)
    for tick_index in range(tick_count):
        micro_pos = tick_index - (layer_count - 1 - section_index)
        active_now = (micro_pos >= 0) & (micro_pos < micro_count)
        clipped = jnp.clip(micro_pos, 0, micro_count - 1)
        inputs_now = lax.dynamic_index_in_dim(work_inputs, clipped, 0, keepdims=False)
        preacts_now = lax.dynamic_index_in_dim(work_preacts, clipped, 0, keepdims=False)
        weighted_now = lax.dynamic_index_in_dim(work_weighted, clipped, 0, keepdims=False)
        grad_now = above.astype(jnp.float32) + weighted_now.astype(jnp.float32)

        def working(operands):

            def visit(running, element):
                deltas, grad_input = slot_backward(flipped, element[1], element[2])
                running = running + weight_term(element[0], deltas)
                return (running, (deltas, grad_input))

            return lax.scan(visit, jnp.zeros_like(accumulated), operands)

        def resting(operands):
            return (
                jnp.zeros_like(accumulated),
                (
                    jnp.zeros(operands[0].shape, jnp.bfloat16),
                    jnp.zeros(operands[0].shape, jnp.bfloat16),
                ),
            )

        partial_sum, step_outs = lax.cond(
            active_now, working, resting, (inputs_now, preacts_now, grad_now)
        )
        grad_step = step_outs[1]
        accumulated = accumulated + partial_sum
        grad_inputs = jnp.where(
            active_now,
            lax.dynamic_update_index_in_dim(grad_inputs, grad_step, clipped, 0),
            grad_inputs,
        )
        if tick_index + 1 < tick_count:
            above = passed_along(grad_step, "section", -1)
    summed = lax.psum(accumulated.astype(jnp.bfloat16), "brick").astype(jnp.float32)
    weight_grads = (summed * (1.0 / math.sqrt(micro_count * own_count * peer_count * voxels)))[None]
    return (grad_inputs[None], weight_grads)


def solution(mesh):
    in_specs = (
        P("section", None, "brick", None, None, None, None),
        P("section", None, "brick", None, None, None, None),
        P("section", None, "brick", None, None, None, None),
        P("section", None, None),
        P(),
        P(None, "brick"),
    )
    out_specs = (P("section", None, "brick", None, None, None, None), P("section", None, None))
    return jax.shard_map(shards, mesh=mesh, in_specs=in_specs, out_specs=out_specs, check_vma=False)
```

profile of v0, /device:TPU:1, one launch (start us, length us, event | category | flops | bytes accessed | tf_op | source)
XLA Modules:
  0.0 496.1 jit_solution(2076499805688644225)
XLA Ops:
  12.5 5.1 %collective-permute-start.2 = (bf16[2,8,8,8,128]{4,3,2,1,0:T(8,128)(2,1)S(1)}, bf16[2,8,8,8,128]{4,3,2,1,0:T(8,128)(2,1)S(1)}, u32[]{:S(2)}, u32[]{:S(2)}) collective-permute-start(bf16[2,8,8,8,128]{4,3,2,1,0:T(8,128)(2,1)S(1)} %pad_maximum_fusion.5), channel_id=1, source_target_pairs={{29,0},{30,1},{31,2},{0,3},{1,4},{2,5},{3,6},{4,7},{5,8},{6,9},{7,... | collective-permute-start | bytes 786440 | tf_op jit(solution)/shard_map/ppermute | solution.py:12
  31.2 3.7 collective-permute-done.1
  37.5 3.5 collective-permute-done.5
  41.0 6.2 %collective-permute-start.6 = (bf16[2,8,8,8,128]{4,3,2,1,0:T(8,128)(2,1)S(1)}, bf16[2,8,8,8,128]{4,3,2,1,0:T(8,128)(2,1)S(1)}, u32[]{:S(2)}, u32[]{:S(2)}) collective-permute-start(bf16[2,8,8,8,128]{4,3,2,1,0:T(8,128)(2,1)S(1)} %copy-done.10), channel_id=1, source_target_pairs={{31,0},{0,1},{1,2},{2,3},{3,4},{4,5},{5,6},{6,7},{7,8},{8,9},{9,10... | collective-permute-start | bytes 786440 | tf_op jit(solution)/shard_map/ppermute | solution.py:12
  48.5 4.2 collective-permute-done.4
  53.9 10.1 %collective-permute-done.7 = bf16[2,8,8,8,128]{4,3,2,1,0:T(8,128)(2,1)S(1)} collective-permute-done((bf16[2,8,8,8,128]{4,3,2,1,0:T(8,128)(2,1)}, bf16[2,8,8,8,128]{4,3,2,1,0:T(8,128)(2,1)S(1)}, u32[]{:S(2)}, u32[]{:S(2)}) %collective-permute-start.7) | collective-permute-done | bytes 262176 | tf_op jit(solution)/shard_map/ppermute | solution.py:12
  64.2 3.8 conditional.5
  69.3 10.8 %collective-permute-done.9 = bf16[4,8,8,8,128]{4,3,2,1,0:T(8,128)(2,1)} collective-permute-done((bf16[4,8,8,8,128]{4,3,2,1,0:T(8,128)(2,1)}, bf16[4,8,8,8,128]{4,3,2,1,0:T(8,128)(2,1)}, u32[]{:S(2)}, u32[]{:S(2)}) %collective-permute-start.9) | collective-permute-done | bytes 524320 | tf_op jit(solution)/shard_map/ppermute | solution.py:18
  86.7 9.9 %collective-permute-done.10 = bf16[4,8,8,8,128]{4,3,2,1,0:T(8,128)(2,1)} collective-permute-done((bf16[4,8,8,8,128]{4,3,2,1,0:T(8,128)(2,1)}, bf16[4,8,8,8,128]{4,3,2,1,0:T(8,128)(2,1)}, u32[]{:S(2)}, u32[]{:S(2)}) %collective-permute-start.10) | collective-permute-done | bytes 524320 | tf_op jit(solution)/shard_map/ppermute | solution.py:18
  98.7 3.3 conditional.7
  103.4 150.8 %collective-permute-done.11 = bf16[4,8,8,8,128]{4,3,2,1,0:T(8,128)(2,1)} collective-permute-done((bf16[4,8,8,8,128]{4,3,2,1,0:T(8,128)(2,1)}, bf16[4,8,8,8,128]{4,3,2,1,0:T(8,128)(2,1)}, u32[]{:S(2)}, u32[]{:S(2)}) %collective-permute-start.11) | collective-permute-done | bytes 524320 | tf_op jit(solution)/shard_map/ppermute | solution.py:18
  256.3 50.2 %conditional.8 = (f32[3456,128]{1,0:T(8,128)}, bf16[4,8,8,8,128]{4,3,2,1,0:T(8,128)(2,1)}, bf16[1,4,8,8,8,128]{5,4,3,2,1,0:T(8,128)(2,1)S(1)}) conditional(s32[]{:T(128)} %convert_element_type.275, () %tuple.167, (bf16[2,4,8,8,8,128]{5,4,3,2,1,0:T(8,128)(2,1)S(1)}, s32[]{:T(128)}, bf16[2,4,8,8,8,128]{5,4,3,2,1,0:T(8,128)(2,1)S(1)}, ...), branch_computations={%region_36.37_spmd, %region_37.40_spmd} | conditional | flops 908099584 | bytes 36274444 | solution.py:141
  259.8 45.7 %while.103 = (s32[]{:T(128)}, f32[3456,128]{1,0:T(8,128)}, bf16[4,8,8,8,128]{4,3,2,1,0:T(8,128)(2,1)}, bf16[4,8,8,8,128]{4,3,2,1,0:T(8,128)(2,1)}, f32[4,8,8,8,1...) while((s32[]{:T(128)}, f32[3456,128]{1,0:T(8,128)}, ...), condition=%wide.region_39.39_spmd.clone, body=%wide.region_38.38_spmd.clone.sunk | while | flops 907575296 | bytes 30507164 | solution.py:130
  274.5 4.3 fusion.718
  286.3 4.3 fusion.718
  298.1 4.3 fusion.718
  309.0 7.6 %collective-permute-done.12 = bf16[4,8,8,8,128]{4,3,2,1,0:T(8,128)(2,1)S(1)} collective-permute-done((bf16[4,8,8,8,128]{4,3,2,1,0:T(8,128)(2,1)}, bf16[4,8,8,8,128]{4,3,2,1,0:T(8,128)(2,1)S(1)}, u32[]{:S(2)}, u32[]{:S(2)}) %collective-permute-start.12) | collective-permute-done | bytes 524320 | tf_op jit(solution)/shard_map/ppermute | solution.py:18
  317.8 48.1 %conditional.9 = (f32[3456,128]{1,0:T(8,128)}, bf16[1,4,8,8,8,128]{5,4,3,2,1,0:T(8,128)(2,1)}) conditional(s32[]{:T(128)} %convert_element_type.277, () %tuple.169, (bf16[2,4,8,8,8,128]{5,4,3,2,1,0:T(8,128)(2,1)S(1)}, s32[]{:T(128)}, bf16[2,4,8,8,8,128]{5,4,3,2,1,0:T(8,128)(2,1)S(1)}, bf16[2,4,8,8,8,128]{5,4,3,2,1,0:T(8,128)(2,1)}, ...), branch_computations={%region_40.41_spmd, %region_41.44_spmd} | conditional | flops 908099584 | bytes 35225860 | solution.py:141
  320.4 45.5 %while.104 = (s32[]{:T(128)}, f32[3456,128]{1,0:T(8,128)}, bf16[4,8,8,8,128]{4,3,2,1,0:T(8,128)(2,1)}, bf16[4,8,8,8,128]{4,3,2,1,0:T(8,128)(2,1)}, f32[4,8,8,8,1...) while((s32[]{:T(128)}, f32[3456,128]{1,0:T(8,128)}, ...), condition=%wide.region_43.43_spmd.clone, body=%wide.region_42.42_spmd.clone.sunk | while | flops 907575296 | bytes 30507164 | solution.py:130
  334.9 4.3 fusion.660
  346.7 4.3 fusion.660
  358.4 4.3 fusion.660
  365.9 4.9 add_convert_fusion
  372.4 114.1 %all-reduce.12.cloned.1.call-done = bf16[3456,128]{1,0:T(8,128)(2,1)} async-done(((bf16[3456,128]{1,0:T(8,128)(2,1)}), bf16[3456,128]{1,0:T(8,128)(2,1)}) %all-reduce.12.cloned.1.call-update) | async-done | bytes 884752 | tf_op jit(solution)/shard_map/psum | solution.py:153
  (567 shorter events, 124.8 us)
Async XLA Ops:
  7.2 479.4 %all-reduce.12.cloned.1.call-start = ((), (), s32[]{:S(2)}) async-start(), calls=%async_computation | async-start | bytes 1769472 | tf_op jit(solution)/shard_map/psum | solution.py:153
  12.4 16.4 %copy-start.4 = (bf16[1,3456,128]{2,1,0:T(8,128)(2,1)S(1)}, bf16[1,3456,128]{2,1,0:T(8,128)(2,1)}, u32[]{:S(2)}) copy-start(bf16[1,3456,128]{2,1,0:T(8,128)(2,1)} %param.29) | copy-start | bytes 2654212
  12.5 15.6 %collective-permute-start.2 = (bf16[2,8,8,8,128]{4,3,2,1,0:T(8,128)(2,1)S(1)}, bf16[2,8,8,8,128]{4,3,2,1,0:T(8,128)(2,1)S(1)}, u32[]{:S(2)}, u32[]{:S(2)}) collective-permute-start(bf16[2,8,8,8,128]{4,3,2,1,0:T(8,128)(2,1)S(1)} %pad_maximum_fusion.5), channel_id=1, source_target_pairs={{29,0},{30,1},{31,2},{0,3},{1,4},{2,5},{3,6},{4,7},{5,8},{6,9},{7,... | collective-permute-start | bytes 786440 | tf_op jit(solution)/shard_map/ppermute | solution.py:12
  18.3 16.6 %collective-permute-start.1 = (bf16[2,8,8,8,128]{4,3,2,1,0:T(8,128)(2,1)}, bf16[2,8,8,8,128]{4,3,2,1,0:T(8,128)(2,1)}, u32[]{:S(2)}, u32[]{:S(2)}) collective-permute-start(bf16[2,8,8,8,128]{4,3,2,1,0:T(8,128)(2,1)} %pad_maximum_fusion.4), channel_id=1, source_target_pairs={{30,0},{31,1},{0,2},{1,3},{2,4},{3,5},{4,6},{5,7},{6,8},{7,9},{8,1... | collective-permute-start | bytes 786440 | tf_op jit(solution)/shard_map/ppermute | solution.py:12
  19.7 16.2 %collective-permute-start = (bf16[2,8,8,8,128]{4,3,2,1,0:T(8,128)(2,1)}, bf16[2,8,8,8,128]{4,3,2,1,0:T(8,128)(2,1)}, u32[]{:S(2)}, u32[]{:S(2)}) collective-permute-start(bf16[2,8,8,8,128]{4,3,2,1,0:T(8,128)(2,1)} %pad_maximum_fusion.3), channel_id=1, source_target_pairs={{31,0},{0,1},{1,2},{2,3},{3,4},{4,5},{5,6},{6,7},{7,8},{8,9},{9,10... | collective-permute-start | bytes 786440 | tf_op jit(solution)/shard_map/ppermute | solution.py:12
  20.8 20.2 %collective-permute-start.5 = (bf16[2,8,8,8,128]{4,3,2,1,0:T(8,128)(2,1)}, bf16[2,8,8,8,128]{4,3,2,1,0:T(8,128)(2,1)}, u32[]{:S(2)}, u32[]{:S(2)}) collective-permute-start(bf16[2,8,8,8,128]{4,3,2,1,0:T(8,128)(2,1)} %pad_maximum_fusion.8), channel_id=1, source_target_pairs={{29,0},{30,1},{31,2},{0,3},{1,4},{2,5},{3,6},{4,7},{5,8},{6,9},{7,... | collective-permute-start | bytes 786440 | tf_op jit(solution)/shard_map/ppermute | solution.py:12
  23.5 29.2 %collective-permute-start.4 = (bf16[2,8,8,8,128]{4,3,2,1,0:T(8,128)(2,1)}, bf16[2,8,8,8,128]{4,3,2,1,0:T(8,128)(2,1)}, u32[]{:S(2)}, u32[]{:S(2)}) collective-permute-start(bf16[2,8,8,8,128]{4,3,2,1,0:T(8,128)(2,1)} %pad_maximum_fusion.7), channel_id=1, source_target_pairs={{30,0},{31,1},{0,2},{1,3},{2,4},{3,5},{4,6},{5,7},{6,8},{7,9},{8,1... | collective-permute-start | bytes 786440 | tf_op jit(solution)/shard_map/ppermute | solution.py:12
  25.9 15.1 %copy-start.10 = (bf16[2,8,8,8,128]{4,3,2,1,0:T(8,128)(2,1)S(1)}, bf16[2,8,8,8,128]{4,3,2,1,0:T(8,128)(2,1)}, u32[]{:S(2)}) copy-start(bf16[2,8,8,8,128]{4,3,2,1,0:T(8,128)(2,1)} %pad_maximum_fusion.9) | copy-start | bytes 786436
  28.1 24.6 %collective-permute-start.3 = (bf16[2,8,8,8,128]{4,3,2,1,0:T(8,128)(2,1)}, bf16[2,8,8,8,128]{4,3,2,1,0:T(8,128)(2,1)}, u32[]{:S(2)}, u32[]{:S(2)}) collective-permute-start(bf16[2,8,8,8,128]{4,3,2,1,0:T(8,128)(2,1)} %pad_maximum_fusion.6), channel_id=1, source_target_pairs={{31,0},{0,1},{1,2},{2,3},{3,4},{4,5},{5,6},{6,7},{7,8},{8,9},{9,10... | collective-permute-start | bytes 786440 | tf_op jit(solution)/shard_map/ppermute | solution.py:12
  34.9 19.0 %collective-permute-start.8 = (bf16[2,8,8,8,128]{4,3,2,1,0:T(8,128)(2,1)}, bf16[2,8,8,8,128]{4,3,2,1,0:T(8,128)(2,1)S(1)}, u32[]{:S(2)}, u32[]{:S(2)}) collective-permute-start(bf16[2,8,8,8,128]{4,3,2,1,0:T(8,128)(2,1)} %pad_maximum_fusion.11), channel_id=1, source_target_pairs={{29,0},{30,1},{31,2},{0,3},{1,4},{2,5},{3,6},{4,7},{5,8},{6,9},{7,... | collective-permute-start | bytes 786440 | tf_op jit(solution)/shard_map/ppermute | solution.py:12
  35.9 28.1 %collective-permute-start.7 = (bf16[2,8,8,8,128]{4,3,2,1,0:T(8,128)(2,1)}, bf16[2,8,8,8,128]{4,3,2,1,0:T(8,128)(2,1)S(1)}, u32[]{:S(2)}, u32[]{:S(2)}) collective-permute-start(bf16[2,8,8,8,128]{4,3,2,1,0:T(8,128)(2,1)} %pad_maximum_fusion.10), channel_id=1, source_target_pairs={{30,0},{31,1},{0,2},{1,3},{2,4},{3,5},{4,6},{5,7},{6,8},{7,9},{8,1... | collective-permute-start | bytes 786440 | tf_op jit(solution)/shard_map/ppermute | solution.py:12
  41.0 23.0 %collective-permute-start.6 = (bf16[2,8,8,8,128]{4,3,2,1,0:T(8,128)(2,1)S(1)}, bf16[2,8,8,8,128]{4,3,2,1,0:T(8,128)(2,1)S(1)}, u32[]{:S(2)}, u32[]{:S(2)}) collective-permute-start(bf16[2,8,8,8,128]{4,3,2,1,0:T(8,128)(2,1)S(1)} %copy-done.10), channel_id=1, source_target_pairs={{31,0},{0,1},{1,2},{2,3},{3,4},{4,5},{5,6},{6,7},{7,8},{8,9},{9,10... | collective-permute-start | bytes 786440 | tf_op jit(solution)/shard_map/ppermute | solution.py:12
  64.2 192.1 %copy-start = (bf16[2,4,8,8,8,128]{5,4,3,2,1,0:T(8,128)(2,1)}, bf16[2,4,8,8,8,128]{5,4,3,2,1,0:T(8,128)(2,1)S(1)}, u32[]{:S(2)}) copy-start(bf16[2,4,8,8,8,128]{5,4,3,2,1,0:T(8,128)(2,1)S(1)} %pad_maximum_fusion.2) | copy-start | bytes 3145732
  68.0 12.1 %collective-permute-start.9 = (bf16[4,8,8,8,128]{4,3,2,1,0:T(8,128)(2,1)}, bf16[4,8,8,8,128]{4,3,2,1,0:T(8,128)(2,1)}, u32[]{:S(2)}, u32[]{:S(2)}) collective-permute-start(bf16[4,8,8,8,128]{4,3,2,1,0:T(8,128)(2,1)} %get-tuple-element.812), channel_id=1, source_target_pairs={{32,0},{64,32},{96,64},{33,1},{65,33},{97,65},{34,2},{66,34},{98,6... | collective-permute-start | bytes 1572872 | tf_op jit(solution)/shard_map/ppermute | solution.py:18
  85.4 11.2 %collective-permute-start.10 = (bf16[4,8,8,8,128]{4,3,2,1,0:T(8,128)(2,1)}, bf16[4,8,8,8,128]{4,3,2,1,0:T(8,128)(2,1)}, u32[]{:S(2)}, u32[]{:S(2)}) collective-permute-start(bf16[4,8,8,8,128]{4,3,2,1,0:T(8,128)(2,1)} %get-tuple-element.814), channel_id=1, source_target_pairs={{32,0},{64,32},{96,64},{33,1},{65,33},{97,65},{34,2},{66,34},{98,6... | collective-permute-start | bytes 1572872 | tf_op jit(solution)/shard_map/ppermute | solution.py:18
  102.1 152.1 %collective-permute-start.11 = (bf16[4,8,8,8,128]{4,3,2,1,0:T(8,128)(2,1)}, bf16[4,8,8,8,128]{4,3,2,1,0:T(8,128)(2,1)}, u32[]{:S(2)}, u32[]{:S(2)}) collective-permute-start(bf16[4,8,8,8,128]{4,3,2,1,0:T(8,128)(2,1)} %get-tuple-element.816), channel_id=1, source_target_pairs={{32,0},{64,32},{96,64},{33,1},{65,33},{97,65},{34,2},{66,34},{98,6... | collective-permute-start | bytes 1572872 | tf_op jit(solution)/shard_map/ppermute | solution.py:18
  267.0 1.4 copy-start.8
  278.8 1.4 copy-start.8
  302.3 1.4 copy-start.8
  306.5 1.5 copy-start.1
  306.6 10.1 %collective-permute-start.12 = (bf16[4,8,8,8,128]{4,3,2,1,0:T(8,128)(2,1)}, bf16[4,8,8,8,128]{4,3,2,1,0:T(8,128)(2,1)S(1)}, u32[]{:S(2)}, u32[]{:S(2)}) collective-permute-start(bf16[4,8,8,8,128]{4,3,2,1,0:T(8,128)(2,1)} %get-tuple-element.818), channel_id=1, source_target_pairs={{32,0},{64,32},{96,64},{33,1},{65,33},{97,65},{34,2},{66,34},{98,6... | collective-permute-start | bytes 1572872 | tf_op jit(solution)/shard_map/ppermute | solution.py:18
  339.2 1.4 copy-start.9
  365.9 4.9 copy-start.2
  372.4 116.6 %copy-start.3 = (bf16[1,2,4,8,8,8,128]{6,5,4,3,2,1,0:T(8,128)(2,1)}, bf16[1,2,4,8,8,8,128]{6,5,4,3,2,1,0:T(8,128)(2,1)S(1)}, u32[]{:S(2)}) copy-start(bf16[1,2,4,8,8,8,128]{6,5,4,3,2,1,0:T(8,128)(2,1)S(1)} %bitcast_dynamic-update-slice_fusion) | copy-start | bytes 3145732
  (5 other events, 6.4 us)
Sparse Core Ops, SparseCore 0:
  370.9 115.5 all-reduce.11
where the time goes:
time: 503 us; the launch traced here: 496 us
  waiting for transfers between devices  315 us (63%)
  local copies, waits for them, and re-layouts  55.9 us (11%)
  other arithmetic  43.3 us (9%)
  matrix products  39.9 us (8%)
  starting transfers between devices  24.4 us (5%)
  between operations  14.5 us (3%)
    ppermute x4, waiting for transfers between devices, passed_along(): return lax.ppermute(shard, axis, pairs)  179 us
    psum x1, waiting for transfers between devices, shards(): lax.psum(accumulated.astype(jnp.bfloat16), 'brick').astype(jnp.float32)  114 us
    dot_general x8, matrix products, weight_term(): lax.dot_general(columns(inputs_one), flat_deltas, (((0,), (0,)), ((), ())...  31.2 us
    while x432, local copies, waits for them, and re-layouts  26.7 us
    ppermute x9, waiting for transfers between devices, shifted_2(): return lax.ppermute(block, axis, route)  21.5 us
    ppermute x9, starting transfers between devices, shifted_2(): return lax.ppermute(block, axis, route)  19 us
  transfers between devices with their start and end apart: 14, of which 9 were waited for; matrix products, arithmetic and copies ran while one was open for 3% of the time, Pallas kernels for 0%

commit v1 on v0

v1 whole, which is shorter than its diff:
```python
import functools
import math

import jax
import jax.numpy as jnp
from jax import lax
from jax.experimental import pallas as pl
from jax.experimental.pallas import tpu as pltpu
from jax.sharding import PartitionSpec as P

C = 128
VOX = 512
ANY = pl.BlockSpec(memory_space=pl.ANY)
F32 = jnp.float32
BF16 = jnp.bfloat16


def shift_rows(block, by):
    if by == 0:
        return block
    pad = jnp.zeros((abs(by),) + block.shape[1:], block.dtype)
    if by > 0:
        return jnp.concatenate([pad, block[:-by]], axis=0)
    return jnp.concatenate([block[-by:], pad], axis=0)


def tick_kernel(tick, info, share, p_ref, sup_ref, above_ref, w_ref, *rest):
    gin_ref, pd_all, pd, sem = rest[-4:]

    @pl.when(info[tick, 1] == 1)
    def _():
        scale = share[info[tick, 0]]
        p = p_ref[0].astype(F32)
        weighted = (sup_ref[0].astype(F32) * scale).astype(BF16).astype(F32)
        grad = weighted + above_ref[...].astype(F32)
        sig = jax.nn.sigmoid(p)
        delta = (grad * (sig * (1.0 + p * (1.0 - sig)))).reshape(64, 8, C)
        place = lax.broadcasted_iota(jnp.int32, (64, 8, C), 1)
        for w in (-1, 0, 1):
            if w == 0:
                moved = delta
            elif w == 1:
                moved = jnp.where(place == 0, 0.0, pltpu.roll(delta, 1, 1))
            else:
                moved = jnp.where(place == 7, 0.0, pltpu.roll(delta, 7, 1))
            moved = moved.reshape(8, 8, 8, C)
            zero = jnp.zeros((8, 1, 8, C), F32)
            for v in (-1, 0, 1):
                if v == 0:
                    out = moved
                elif v == 1:
                    out = jnp.concatenate([zero, moved[:, :-1]], axis=1)
                else:
                    out = jnp.concatenate([moved[:, 1:], zero], axis=1)
                at = ((v + 1) * 3 + (w + 1)) * C
                pd[:, at : at + C] = out.reshape(VOX, C).astype(BF16)
        copy = pltpu.make_async_copy(pd, pd_all.at[tick], sem)
        copy.start()
        y = jnp.dot(pd[...], w_ref[...], preferred_element_type=F32)
        gin = y[:, C : 2 * C] + shift_rows(y[:, :C], -64) + shift_rows(y[:, 2 * C :], 64)
        gin_ref[...] = gin.astype(BF16)
        copy.wait()


def tick_step(tick, ticks, info, share, preacts, sup, above, w_all, pd_all):
    one = lambda i, info, share: (info[tick, 0], 0, 0)
    flat = lambda i, info, share: (0, 0)
    in_specs = [
        pl.BlockSpec((1, VOX, C), one),
        pl.BlockSpec((1, VOX, C), one),
        pl.BlockSpec((VOX, C), flat),
        pl.BlockSpec((9 * C, 3 * C), flat),
    ]
    operands = [preacts, sup, above, w_all]
    aliases = {}
    if pd_all is not None:
        in_specs.append(ANY)
        operands.append(pd_all)
        aliases = {6: 1}
    return pl.pallas_call(
        functools.partial(tick_kernel, tick),
        grid_spec=pltpu.PrefetchScalarGridSpec(
            num_scalar_prefetch=2,
            grid=(1,),
            in_specs=in_specs,
            out_specs=[pl.BlockSpec((VOX, C), flat), ANY],
            scratch_shapes=[pltpu.VMEM((VOX, 9 * C), BF16), pltpu.SemaphoreType.DMA],
        ),
        out_shape=[
            jax.ShapeDtypeStruct((VOX, C), BF16),
            jax.ShapeDtypeStruct((ticks, VOX, 9 * C), BF16),
        ],
        input_output_aliases=aliases,
        compiler_params=pltpu.CompilerParams(vmem_limit_bytes=24 << 20),
        cost_estimate=pl.CostEstimate(
            flops=2 * VOX * 27 * C * C, bytes_accessed=4 << 20, transcendentals=VOX * C
        ),
        name="tick%d" % tick,
    )(info, share, *operands)


def weight_kernel(place, pd_ref, x_ref, keep_ref, send_ref, acc):
    step = pl.program_id(0)
    x = x_ref[0]
    x3 = jnp.concatenate([shift_rows(x, 64), x, shift_rows(x, -64)], axis=1)
    part = lax.dot_general(
        x3, pd_ref[0], (((0,), (0,)), ((), ())), preferred_element_type=F32
    )

    @pl.when(step == 0)
    def _():
        acc[...] = part

    @pl.when(step > 0)
    def _():
        acc[...] += part

    @pl.when(step == 3)
    def _():
        mine = pl.multiple_of(place[1] * 192, 16)
        other = pl.multiple_of(192 - place[1] * 192, 16)
        keep_ref[...] = acc[pl.ds(mine, 192), :].astype(BF16)
        send_ref[...] = acc[pl.ds(other, 192), :].astype(BF16)


def weight_step(place, pd_all, inputs):
    half = jax.ShapeDtypeStruct((192, 9 * C), BF16)
    flat = lambda i, place: (0, 0)
    return pl.pallas_call(
        weight_kernel,
        grid_spec=pltpu.PrefetchScalarGridSpec(
            num_scalar_prefetch=1,
            grid=(4,),
            in_specs=[
                pl.BlockSpec((1, VOX, 9 * C), lambda i, place: (i + place[0], 0, 0)),
                pl.BlockSpec((1, VOX, C), lambda i, place: (i, 0, 0)),
            ],
            out_specs=[pl.BlockSpec((192, 9 * C), flat)] * 2,
            scratch_shapes=[pltpu.VMEM((384, 9 * C), F32)],
        ),
        out_shape=[half, half],
        compiler_params=pltpu.CompilerParams(vmem_limit_bytes=32 << 20),
        cost_estimate=pl.CostEstimate(
            flops=8 * VOX * 27 * C * C, bytes_accessed=7 << 20, transcendentals=0
        ),
        name="weight_terms",
    )(place, pd_all, inputs)


def pack_kernel(ticks, pick, *rest):
    gins = rest[:ticks]
    outs = rest[ticks : ticks + 4]
    zero, sems = rest[ticks + 4 :]
    zero[...] = jnp.zeros_like(zero)
    for d in range(4):
        for m in range(2):
            for t in range(-1, ticks):

                @pl.when(pick[m, d] == t)
                def _(t=t, d=d, m=m):
                    src = zero if t < 0 else gins[t]
                    pltpu.make_async_copy(src, outs[d].at[m], sems.at[d, m]).start()

    for d in range(4):
        for m in range(2):
            pltpu.make_async_copy(zero, outs[d].at[m], sems.at[d, m]).wait()


def pack_step(pick, gins):
    return pl.pallas_call(
        functools.partial(pack_kernel, len(gins)),
        grid_spec=pltpu.PrefetchScalarGridSpec(
            num_scalar_prefetch=1,
            grid=(1,),
            in_specs=[ANY] * len(gins),
            out_specs=[ANY] * 4,
            scratch_shapes=[pltpu.VMEM((VOX, C), BF16), pltpu.SemaphoreType.DMA((4, 2))],
        ),
        out_shape=[jax.ShapeDtypeStruct((2, VOX, C), BF16)] * 4,
        name="pack_slots",
    )(pick, *gins)


def finish_kernel(scale, place, mine_ref, other_ref, out_ref):
    core, z = place[1], place[2]
    for ref, half in ((mine_ref, core), (other_ref, 1 - core)):
        for k in range(4):
            first = half * 12 + lax.bitwise_xor(z, k) * 3
            for i in range(3):
                group = first + i
                u = group // 8
                row = pl.multiple_of(u * (9 * C) + (group - u * 8) * 16, 16)
                rows = ref[k, i * 16 : (i + 1) * 16, :].astype(F32) * scale
                for tap in range(9):
                    out_ref[pl.ds(row + tap * C, 16), :] = rows[:, tap * C : (tap + 1) * C]


def finish_step(scale, place, mine, other):
    whole = lambda i, place: (0, 0, 0)
    return pl.pallas_call(
        functools.partial(finish_kernel, scale),
        grid_spec=pltpu.PrefetchScalarGridSpec(
            num_scalar_prefetch=1,
            grid=(1,),
            in_specs=[pl.BlockSpec((4, 48, 9 * C), whole)] * 2,
            out_specs=pl.BlockSpec((27 * C, C), lambda i, place: (0, 0)),
        ),
        out_shape=jax.ShapeDtypeStruct((27 * C, C), F32),
        compiler_params=pltpu.CompilerParams(vmem_limit_bytes=24 << 20),
        name="finish_weights",
    )(place, mine, other)


def swap(block, bit):
    pairs = [(i, i ^ bit) for i in range(lax.axis_size("brick"))]
    return lax.ppermute(block, "brick", pairs)


def shifted(block, distance):
    n = lax.axis_size("brick")
    return lax.ppermute(block, "brick", [(i, (i + distance) % n) for i in range(n)])


def shards(saved_inputs, saved_preacts, supervision, weights, trainer, counts):
    peers = lax.axis_size("brick")
    me = lax.axis_index("brick")
    layers = lax.axis_size("section")
    section = lax.axis_index("section")
    micros, own = saved_inputs.shape[1:3]
    work = micros * own
    ticks = layers + work - 1
    core = jnp.mod(me, 2)
    z = jnp.mod(me // 2, 4)

    inputs = saved_inputs.reshape(work, VOX, C)
    preacts = saved_preacts.reshape(work, VOX, C)
    sup = supervision.reshape(work, VOX, C)
    w_all = (
        weights[0].reshape(3, 9, C, C).transpose(1, 3, 0, 2).reshape(9 * C, 3 * C)
    )
    share = counts.reshape(work).astype(F32) / VOX
    late = layers - 1 - section
    index = jnp.arange(ticks, dtype=jnp.int32) - late
    info = jnp.stack(
        [jnp.clip(index, 0, work - 1), ((index >= 0) & (index < work)).astype(jnp.int32)], axis=1
    )
    place = jnp.stack([late, core, z]).astype(jnp.int32)
    targets = lax.dynamic_slice_in_dim(trainer, me * own, own, 1)
    offsets = jnp.mod(targets - me, peers)
    match = offsets[:, :, None] == jnp.arange(4, dtype=jnp.int32)[None, None, :]
    brick = jnp.arange(work, dtype=jnp.int32).reshape(micros, own)
    pick = jnp.max(jnp.where(match, (brick + late)[:, :, None], -1), axis=1).astype(jnp.int32)

    above = jnp.zeros((VOX, C), BF16)
    pd_all = None
    gins = []
    for tick in range(ticks):
        gin, pd_all = tick_step(tick, ticks, info, share, preacts, sup, above, w_all, pd_all)
        gins.append(gin)
        if tick + 1 < ticks:
            above = lax.ppermute(gin, "section", [(i, i - 1) for i in range(1, layers)])

    keep, send = weight_step(place, pd_all, inputs)
    local, *sent = pack_step(pick, gins)
    slots = [local] + [shifted(block, d + 1) for d, block in enumerate(sent)]
    skip_grads = jnp.stack(slots, axis=1).reshape((1, micros, 4) + saved_inputs.shape[3:])

    half = keep.astype(F32) + swap(send, 1).astype(F32)
    half = half.astype(BF16).reshape(4, 48, 9 * C)
    part = [lax.dynamic_index_in_dim(half, lax.bitwise_xor(z, k), 0, False) for k in range(4)]
    total = part[0].astype(F32)
    for k in (2, 1, 3):
        total = total + swap(part[k], 2 * k).astype(F32)
    total = total.astype(BF16)
    full = total.astype(F32)
    for k in (2, 1, 3):
        full = full + swap(total, 8 * k).astype(F32)
    full = full.astype(BF16)
    mine = jnp.stack([full] + [swap(full, 2 * k) for k in (1, 2, 3)])
    other = swap(mine, 1)
    scale = 1.0 / math.sqrt(work * peers * VOX)
    weight_grads = finish_step(scale, place, mine, other)
    return skip_grads, weight_grads[None]


def solution(mesh):
    bricks = P("section", None, "brick", None, None, None, None)
    in_specs = (bricks, bricks, bricks, P("section", None, None), P(), P(None, "brick"))
    out_specs = (bricks, P("section", None, None))
    return jax.shard_map(shards, mesh=mesh, in_specs=in_specs, out_specs=out_specs, check_vma=False)
```

time: 503 us -> 154 us (0.31); the launches traced: 496 us -> 154 us
  waiting for transfers between devices: 315 us -> 66.2 us
  matrix products: 39.9 us -> 0 us
  other arithmetic: 43.3 us -> 3.89 us
  local copies, waits for them, and re-layouts: 55.9 us -> 18.1 us
  Pallas kernels: 0 us -> 33.4 us
  between operations: 14.5 us -> 0.99 us
  starting transfers between devices: 24.4 us -> 31 us
    ppermute x13 -> x20, waiting for transfers between devices: 201 us -> 66.2 us  [the longest x6 30.1 us: shards(): above = lax.ppermute(gin, 'section', [(i, i - 1) for i in range(1, layers)])]
    psum x1 -> x0, waiting for transfers between devices: 114 us -> none  [shards(): lax.psum(accumulated.astype(jnp.bfloat16), 'brick').astype(jnp.float32)]
    dot_general x16 -> x0, matrix products: 39.9 us -> none  [the longest x8 31.2 us: weight_term(): lax.dot_general(columns(inputs_one), flat_deltas, (((0,), (0,)), ((), ())...]
    pallas_call x0 -> x10, Pallas kernels: none -> 33.4 us  [the longest x1 17.8 us: pack_step(): pl.pallas_call(functools.partial(pack_kernel, len(gins)), grid_spec=pltpu...]
    while x432 -> x0, local copies, waits for them, and re-layouts: 26.7 us -> none
    convert_element_type x14 -> x4, other arithmetic: 22.1 us -> 0.23 us  [the longest x1 0.11 us: shards(): half = half.astype(BF16).reshape(4, 48, 9 * C)]
    unnamed x15 -> x35, local copies, waits for them, and re-layouts: 0.29 us -> 15.5 us
    squeeze x10 -> x1, local copies, waits for them, and re-layouts: 9.46 us -> 0.04 us  [shards(): lax.dynamic_index_in_dim(half, lax.bitwise_xor(z, k), 0, False)]
  transfers between devices with their start and end apart: 14 -> 20, of which waited for: 9 -> 16; matrix products, arithmetic and copies ran while one was open for 3% -> 2% of each run, Pallas kernels for 0% -> 12%
where the time goes in v1:
time: 154 us
  waiting for transfers between devices  66.2 us (43%)
  Pallas kernels  33.4 us (22%)
  starting transfers between devices  31 us (20%)
  local copies, waits for them, and re-layouts  18.1 us (12%)
  other arithmetic  3.89 us (3%)
    ppermute x6, waiting for transfers between devices, shards(): above = lax.ppermute(gin, 'section', [(i, i - 1) for i in range(1, layers)])  30.1 us
    ppermute x11, starting transfers between devices, swap(): return lax.ppermute(block, 'brick', pairs)  21.3 us
    ppermute x3, waiting for transfers between devices, shifted(): lax.ppermute(block, 'brick', [(i, (i + distance) % n) for i in range(n)])  18.4 us
    pallas_call x1, Pallas kernels, pack_step(): pl.pallas_call(functools.partial(pack_kernel, len(gins)), grid_spec=pltpu...  17.8 us
    ppermute x11, waiting for transfers between devices, swap(): return lax.ppermute(block, 'brick', pairs)  17.7 us
    unnamed x35, local copies, waits for them, and re-layouts  15.5 us
    pallas_call x7, Pallas kernels, tick_step(): pl.pallas_call(functools.partial(tick_kernel, tick), grid_spec=pltpu.Pref...  9.49 us
    ppermute x6, starting transfers between devices, shards(): above = lax.ppermute(gin, 'section', [(i, i - 1) for i in range(1, layers)])  7.74 us
  transfers between devices with their start and end apart: 20, of which 16 were waited for; matrix products, arithmetic and copies ran while one was open for 2% of the time, Pallas kernels for 12%

profile of v1, /device:TPU:1, one launch (start us, length us, event | category | flops | bytes accessed | tf_op | source)
XLA Modules:
  0.0 153.7 jit_solution(851735511156716551)
XLA Ops:
  0.8 2.4 %copy.36 = bf16[3,9,128,128]{2,0,3,1:T(4,128)(2,1)S(1)} copy(bf16[3,9,128,128]{3,2,1,0:T(8,128)(2,1)} %bitcast.66) | data formatting | bytes 1769472 | tf_op jit(solution)/shard_map/reshape;squeeze | solution.py:239
  8.2 5.4 %collective-permute-done.above_ref = bf16[512,128]{1,0:T(8,128)(2,1)S(1)} collective-permute-done((bf16[512,128]{1,0:T(8,128)(2,1)S(1)}, bf16[512,128]{1,0:T(8,128)(2,1)S(1)}, u32[]{:S(2)}, u32[]{:S(2)}) %collective-permute-start) | collective-permute-done | bytes 131104 | tf_op jit(solution)/shard_map/ppermute | solution.py:261
  15.5 4.6 %collective-permute-done.1.above_ref = bf16[512,128]{1,0:T(8,128)(2,1)S(1)} collective-permute-done((bf16[512,128]{1,0:T(8,128)(2,1)S(1)}, bf16[512,128]{1,0:T(8,128)(2,1)S(1)}, u32[]{:S(2)}, u32[]{:S(2)}) %collective-permute-start.1) | collective-permute-done | bytes 131104 | tf_op jit(solution)/shard_map/ppermute | solution.py:261
  22.0 7.0 %collective-permute-done.2.above_ref = bf16[512,128]{1,0:T(8,128)(2,1)S(1)} collective-permute-done((bf16[512,128]{1,0:T(8,128)(2,1)S(1)}, bf16[512,128]{1,0:T(8,128)(2,1)S(1)}, u32[]{:S(2)}, u32[]{:S(2)}) %collective-permute-start.2) | collective-permute-done | bytes 131104 | tf_op jit(solution)/shard_map/ppermute | solution.py:261
  32.3 4.4 %collective-permute-done.3.above_ref = bf16[512,128]{1,0:T(8,128)(2,1)S(1)} collective-permute-done((bf16[512,128]{1,0:T(8,128)(2,1)S(1)}, bf16[512,128]{1,0:T(8,128)(2,1)S(1)}, u32[]{:S(2)}, u32[]{:S(2)}) %collective-permute-start.3) | collective-permute-done | bytes 131104 | tf_op jit(solution)/shard_map/ppermute | solution.py:261
  40.0 4.4 %collective-permute-done.4.above_ref = bf16[512,128]{1,0:T(8,128)(2,1)S(1)} collective-permute-done((bf16[512,128]{1,0:T(8,128)(2,1)S(1)}, bf16[512,128]{1,0:T(8,128)(2,1)S(1)}, u32[]{:S(2)}, u32[]{:S(2)}) %collective-permute-start.4) | collective-permute-done | bytes 131104 | tf_op jit(solution)/shard_map/ppermute | solution.py:261
  46.3 3.2 %copy-done = bf16[7,512,1152]{2,1,0:T(8,128)(2,1)} copy-done((bf16[7,512,1152]{2,1,0:T(8,128)(2,1)}, bf16[7,512,1152]{2,1,0:T(8,128)(2,1)S(1)}, u32[]{:S(2)}) %copy-start) | copy-done | bytes 8257560
  50.9 4.3 %collective-permute-done.5.above_ref = bf16[512,128]{1,0:T(8,128)(2,1)S(1)} collective-permute-done((bf16[512,128]{1,0:T(8,128)(2,1)S(1)}, bf16[512,128]{1,0:T(8,128)(2,1)S(1)}, u32[]{:S(2)}, u32[]{:S(2)}) %collective-permute-start.5) | collective-permute-done | bytes 131104 | tf_op jit(solution)/shard_map/ppermute | solution.py:261
  55.3 3.3 %copy-done.1 = bf16[7,512,1152]{2,1,0:T(8,128)(2,1)S(1)} copy-done((bf16[7,512,1152]{2,1,0:T(8,128)(2,1)S(1)}, bf16[7,512,1152]{2,1,0:T(8,128)(2,1)}, u32[]{:S(2)}) %copy-start.1) | copy-done | bytes 8257560
  60.5 3.2 %copy-done.2 = bf16[7,512,1152]{2,1,0:T(8,128)(2,1)} copy-done((bf16[7,512,1152]{2,1,0:T(8,128)(2,1)}, bf16[7,512,1152]{2,1,0:T(8,128)(2,1)S(1)}, u32[]{:S(2)}) %copy-start.2) | copy-done | bytes 8257560
  63.8 3.4 %copy-done.3 = bf16[7,512,1152]{2,1,0:T(8,128)(2,1)S(1)} copy-done((bf16[7,512,1152]{2,1,0:T(8,128)(2,1)S(1)}, bf16[7,512,1152]{2,1,0:T(8,128)(2,1)}, u32[]{:S(2)}) %copy-start.3) | copy-done | bytes 8257560
  67.2 4.2 %weight_terms.1 = (bf16[192,1152]{1,0:T(8,128)(2,1)S(1)}, bf16[192,1152]{1,0:T(8,128)(2,1)S(1)}) custom-call(s32[3]{0:T(128)S(1)} %pad_add_fusion.1.place, bf16[7,512,1152]{2,1,0:T(8,128)(2,1)S(1)} %copy-done.3, bf16[4,512,128]{2,1,0:T(8,128)(2,1)S(1)} %bitcast.61), custom_call_target="tpu_custom_call" | custom-call | flops 1811939328 | bytes 7340032 | tf_op jit(solution)/shard_map/weight_terms/pallas_call | solution.py:129
  71.3 6.7 %collective-permute-start.9 = (bf16[192,1152]{1,0:T(8,128)(2,1)S(1)}, bf16[192,1152]{1,0:T(8,128)(2,1)S(1)}, u32[]{:S(2)}, u32[]{:S(2)}) collective-permute-start(bf16[192,1152]{1,0:T(8,128)(2,1)S(1)} %get-tuple-element.41), channel_id=1, source_target_pairs={{0,1},{1,0},{2,3},{3,2},{4,5},{5,4},{6,7},{7,6},{8,9},{9,8},{10,11... | collective-permute-start | bytes 1327112 | tf_op jit(solution)/shard_map/ppermute | solution.py:216
  79.6 3.7 %collective-permute-start.10 = (bf16[48,1152]{1,0:T(8,128)(2,1)S(1)}, bf16[48,1152]{1,0:T(8,128)(2,1)S(1)}, u32[]{:S(2)}, u32[]{:S(2)}) collective-permute-start(bf16[48,1152]{1,0:T(8,128)(2,1)S(1)} %get-tuple-element.42), channel_id=1, source_target_pairs={{0,4},{1,5},{2,6},{3,7},{4,0},{5,1},{6,2},{7,3},{8,12},{9,13},{10,... | collective-permute-start | bytes 331784 | tf_op jit(solution)/shard_map/ppermute | solution.py:216
  84.0 2.4 %collective-permute-done.10 = bf16[48,1152]{1,0:T(8,128)(2,1)S(1)} collective-permute-done((bf16[48,1152]{1,0:T(8,128)(2,1)S(1)}, bf16[48,1152]{1,0:T(8,128)(2,1)S(1)}, u32[]{:S(2)}, u32[]{:S(2)}) %collective-permute-start.10) | collective-permute-done | bytes 110624 | tf_op jit(solution)/shard_map/ppermute | solution.py:216
  86.4 2.8 %collective-permute-done.11 = bf16[48,1152]{1,0:T(8,128)(2,1)S(1)} collective-permute-done((bf16[48,1152]{1,0:T(8,128)(2,1)S(1)}, bf16[48,1152]{1,0:T(8,128)(2,1)S(1)}, u32[]{:S(2)}, u32[]{:S(2)}) %collective-permute-start.11) | collective-permute-done | bytes 110624 | tf_op jit(solution)/shard_map/ppermute | solution.py:216
  89.2 3.0 %collective-permute-start.13 = (bf16[48,1152]{1,0:T(8,128)(2,1)S(1)}, bf16[48,1152]{1,0:T(8,128)(2,1)S(1)}, u32[]{:S(2)}, u32[]{:S(2)}) collective-permute-start(bf16[48,1152]{1,0:T(8,128)(2,1)S(1)} %fusion.2), channel_id=1, source_target_pairs={{0,16},{1,17},{2,18},{3,19},{4,20},{5,21},{6,22},{7,23},{8,24},{9,... | collective-permute-start | bytes 331784 | tf_op jit(solution)/shard_map/ppermute | solution.py:216
  98.7 3.4 %collective-permute-start.17 = (bf16[48,1152]{1,0:T(8,128)(2,1)S(1)}, bf16[48,1152]{1,0:T(8,128)(2,1)S(1)}, u32[]{:S(2)}, u32[]{:S(2)}) collective-permute-start(bf16[48,1152]{1,0:T(8,128)(2,1)S(1)} %add_convert_fusion.1), channel_id=1, source_target_pairs={{0,4},{1,5},{2,6},{3,7},{4,0},{5,1},{6,2},{7,3},{8,12},{9,13},{10,... | collective-permute-start | bytes 331784 | tf_op jit(solution)/shard_map/ppermute | solution.py:216
  102.3 3.1 %collective-permute-done.17 = bf16[48,1152]{1,0:T(8,128)(2,1)S(1)} collective-permute-done((bf16[48,1152]{1,0:T(8,128)(2,1)S(1)}, bf16[48,1152]{1,0:T(8,128)(2,1)S(1)}, u32[]{:S(2)}, u32[]{:S(2)}) %collective-permute-start.17) | collective-permute-done | bytes 110624 | tf_op jit(solution)/shard_map/ppermute | solution.py:216
  105.4 2.8 %collective-permute-done.18 = bf16[48,1152]{1,0:T(8,128)(2,1)S(1)} collective-permute-done((bf16[48,1152]{1,0:T(8,128)(2,1)S(1)}, bf16[48,1152]{1,0:T(8,128)(2,1)S(1)}, u32[]{:S(2)}, u32[]{:S(2)}) %collective-permute-start.18) | collective-permute-done | bytes 110624 | tf_op jit(solution)/shard_map/ppermute | solution.py:216
  108.3 2.5 %collective-permute-start.19 = (bf16[4,48,1152]{2,1,0:T(8,128)(2,1)S(1)}, bf16[4,48,1152]{2,1,0:T(8,128)(2,1)S(1)}, u32[]{:S(2)}, u32[]{:S(2)}) collective-permute-start(bf16[4,48,1152]{2,1,0:T(8,128)(2,1)S(1)} %pad_maximum_fusion.1.mine_ref), channel_id=1, source_target_pairs={{0,1},{1,0},{2,3},{3,2},{4,5},{5,4},{6,7},{7,6},{8,9},{9,8},{10,11... | collective-permute-start | bytes 1327112 | tf_op jit(solution)/shard_map/ppermute | solution.py:216
  111.4 17.8 %pack_slots.1 = (bf16[2,512,128]{2,1,0:T(8,128)(2,1)}, bf16[2,512,128]{2,1,0:T(8,128)(2,1)}, bf16[2,512,128]{2,1,0:T(8,128)(2,1)}, bf16[2,512,128]{2,1,0:T(8,128)(2,1)}) custom-call(s32[2,4]{1,0:T(2,128)} %fusion.3.pick, bf16[512,128]{1,0:T(8,128)(2,1)} %copy-done.9, bf16[512,128]{1,0:T(8,128)(2,1)} %copy-done.10, bf16[512,128]{1,0:T(8,128)(2,1)} %copy-done.11, ...), custom_call_target="tpu_custom_call" | custom-call | tf_op jit(solution)/shard_map/pack_slots/pallas_call | solution.py:170
  131.2 11.7 %collective-permute-done.8 = bf16[2,512,128]{2,1,0:T(8,128)(2,1)S(1)} collective-permute-done((bf16[2,512,128]{2,1,0:T(8,128)(2,1)}, bf16[2,512,128]{2,1,0:T(8,128)(2,1)S(1)}, u32[]{:S(2)}, u32[]{:S(2)}) %collective-permute-start.8) | collective-permute-done | bytes 262176 | tf_op jit(solution)/shard_map/ppermute | solution.py:221
  142.9 6.7 %collective-permute-done.7 = bf16[2,512,128]{2,1,0:T(8,128)(2,1)S(1)} collective-permute-done((bf16[2,512,128]{2,1,0:T(8,128)(2,1)}, bf16[2,512,128]{2,1,0:T(8,128)(2,1)S(1)}, u32[]{:S(2)}, u32[]{:S(2)}) %collective-permute-start.7) | collective-permute-done | bytes 262176 | tf_op jit(solution)/shard_map/ppermute | solution.py:221
  (78 shorter events, 36.3 us)
Async XLA Ops:
  6.9 6.7 %collective-permute-start = (bf16[512,128]{1,0:T(8,128)(2,1)S(1)}, bf16[512,128]{1,0:T(8,128)(2,1)S(1)}, u32[]{:S(2)}, u32[]{:S(2)}) collective-permute-start(bf16[512,128]{1,0:T(8,128)(2,1)S(1)} %get-tuple-element.22.rest_0_), channel_id=1, source_target_pairs={{32,0},{64,32},{96,64},{33,1},{65,33},{97,65},{34,2},{66,34},{98,6... | collective-permute-start | bytes 393224 | tf_op jit(solution)/shard_map/ppermute | solution.py:261
  14.2 5.9 %collective-permute-start.1 = (bf16[512,128]{1,0:T(8,128)(2,1)S(1)}, bf16[512,128]{1,0:T(8,128)(2,1)S(1)}, u32[]{:S(2)}, u32[]{:S(2)}) collective-permute-start(bf16[512,128]{1,0:T(8,128)(2,1)S(1)} %get-tuple-element.24.rest_1_), channel_id=1, source_target_pairs={{32,0},{64,32},{96,64},{33,1},{65,33},{97,65},{34,2},{66,34},{98,6... | collective-permute-start | bytes 393224 | tf_op jit(solution)/shard_map/ppermute | solution.py:261
  20.7 8.3 %collective-permute-start.2 = (bf16[512,128]{1,0:T(8,128)(2,1)S(1)}, bf16[512,128]{1,0:T(8,128)(2,1)S(1)}, u32[]{:S(2)}, u32[]{:S(2)}) collective-permute-start(bf16[512,128]{1,0:T(8,128)(2,1)S(1)} %get-tuple-element.26.rest_2_), channel_id=1, source_target_pairs={{32,0},{64,32},{96,64},{33,1},{65,33},{97,65},{34,2},{66,34},{98,6... | collective-permute-start | bytes 393224 | tf_op jit(solution)/shard_map/ppermute | solution.py:261
  31.0 5.7 %collective-permute-start.3 = (bf16[512,128]{1,0:T(8,128)(2,1)S(1)}, bf16[512,128]{1,0:T(8,128)(2,1)S(1)}, u32[]{:S(2)}, u32[]{:S(2)}) collective-permute-start(bf16[512,128]{1,0:T(8,128)(2,1)S(1)} %get-tuple-element.28.rest_3_), channel_id=1, source_target_pairs={{32,0},{64,32},{96,64},{33,1},{65,33},{97,65},{34,2},{66,34},{98,6... | collective-permute-start | bytes 393224 | tf_op jit(solution)/shard_map/ppermute | solution.py:261
  38.6 21.9 %copy-start.13 = (bf16[512,128]{1,0:T(8,128)(2,1)}, bf16[512,128]{1,0:T(8,128)(2,1)S(1)}, u32[]{:S(2)}) copy-start(bf16[512,128]{1,0:T(8,128)(2,1)S(1)} %get-tuple-element.30.rest_4_) | copy-start | bytes 393220
  38.7 5.7 %collective-permute-start.4 = (bf16[512,128]{1,0:T(8,128)(2,1)S(1)}, bf16[512,128]{1,0:T(8,128)(2,1)S(1)}, u32[]{:S(2)}, u32[]{:S(2)}) collective-permute-start(bf16[512,128]{1,0:T(8,128)(2,1)S(1)} %get-tuple-element.30.rest_4_), channel_id=1, source_target_pairs={{32,0},{64,32},{96,64},{33,1},{65,33},{97,65},{34,2},{66,34},{98,6... | collective-permute-start | bytes 393224 | tf_op jit(solution)/shard_map/ppermute | solution.py:261
  49.5 21.8 %copy-start.14 = (bf16[512,128]{1,0:T(8,128)(2,1)}, bf16[512,128]{1,0:T(8,128)(2,1)S(1)}, u32[]{:S(2)}) copy-start(bf16[512,128]{1,0:T(8,128)(2,1)S(1)} %get-tuple-element.32.rest_5_) | copy-start | bytes 393220
  49.5 5.7 %collective-permute-start.5 = (bf16[512,128]{1,0:T(8,128)(2,1)S(1)}, bf16[512,128]{1,0:T(8,128)(2,1)S(1)}, u32[]{:S(2)}, u32[]{:S(2)}) collective-permute-start(bf16[512,128]{1,0:T(8,128)(2,1)S(1)} %get-tuple-element.32.rest_5_), channel_id=1, source_target_pairs={{32,0},{64,32},{96,64},{33,1},{65,33},{97,65},{34,2},{66,34},{98,6... | collective-permute-start | bytes 393224 | tf_op jit(solution)/shard_map/ppermute | solution.py:261
  63.8 47.7 %copy-start.15 = (bf16[512,128]{1,0:T(8,128)(2,1)}, bf16[512,128]{1,0:T(8,128)(2,1)S(1)}, u32[]{:S(2)}) copy-start(bf16[512,128]{1,0:T(8,128)(2,1)S(1)} %get-tuple-element.34.rest_6_) | copy-start | bytes 393220
  63.8 38.4 %copy-start.16 = (s32[2,64]{1,0:T(2,128)S(1)}, s32[2,64]{1,0:T(2,128)}, u32[]{:S(2)}) copy-start(s32[2,64]{1,0:T(2,128)} %param.10) | copy-start | bytes 1540
  71.3 8.1 %collective-permute-start.9 = (bf16[192,1152]{1,0:T(8,128)(2,1)S(1)}, bf16[192,1152]{1,0:T(8,128)(2,1)S(1)}, u32[]{:S(2)}, u32[]{:S(2)}) collective-permute-start(bf16[192,1152]{1,0:T(8,128)(2,1)S(1)} %get-tuple-element.41), channel_id=1, source_target_pairs={{0,1},{1,0},{2,3},{3,2},{4,5},{5,4},{6,7},{7,6},{8,9},{9,8},{10,11... | collective-permute-start | bytes 1327112 | tf_op jit(solution)/shard_map/ppermute | solution.py:216
  79.6 6.8 %collective-permute-start.10 = (bf16[48,1152]{1,0:T(8,128)(2,1)S(1)}, bf16[48,1152]{1,0:T(8,128)(2,1)S(1)}, u32[]{:S(2)}, u32[]{:S(2)}) collective-permute-start(bf16[48,1152]{1,0:T(8,128)(2,1)S(1)} %get-tuple-element.42), channel_id=1, source_target_pairs={{0,4},{1,5},{2,6},{3,7},{4,0},{5,1},{6,2},{7,3},{8,12},{9,13},{10,... | collective-permute-start | bytes 331784 | tf_op jit(solution)/shard_map/ppermute | solution.py:216
  83.3 5.9 %collective-permute-start.11 = (bf16[48,1152]{1,0:T(8,128)(2,1)S(1)}, bf16[48,1152]{1,0:T(8,128)(2,1)S(1)}, u32[]{:S(2)}, u32[]{:S(2)}) collective-permute-start(bf16[48,1152]{1,0:T(8,128)(2,1)S(1)} %get-tuple-element.44), channel_id=1, source_target_pairs={{0,2},{1,3},{2,0},{3,1},{4,6},{5,7},{6,4},{7,5},{8,10},{9,11},{10,... | collective-permute-start | bytes 331784 | tf_op jit(solution)/shard_map/ppermute | solution.py:216
  84.0 5.2 %collective-permute-start.12 = (bf16[48,1152]{1,0:T(8,128)(2,1)S(1)}, bf16[48,1152]{1,0:T(8,128)(2,1)S(1)}, u32[]{:S(2)}, u32[]{:S(2)}) collective-permute-start(bf16[48,1152]{1,0:T(8,128)(2,1)S(1)} %get-tuple-element.43), channel_id=1, source_target_pairs={{0,6},{1,7},{2,4},{3,5},{4,2},{5,3},{6,0},{7,1},{8,14},{9,15},{10,... | collective-permute-start | bytes 331784 | tf_op jit(solution)/shard_map/ppermute | solution.py:216
  89.2 5.2 %collective-permute-start.13 = (bf16[48,1152]{1,0:T(8,128)(2,1)S(1)}, bf16[48,1152]{1,0:T(8,128)(2,1)S(1)}, u32[]{:S(2)}, u32[]{:S(2)}) collective-permute-start(bf16[48,1152]{1,0:T(8,128)(2,1)S(1)} %fusion.2), channel_id=1, source_target_pairs={{0,16},{1,17},{2,18},{3,19},{4,20},{5,21},{6,22},{7,23},{8,24},{9,... | collective-permute-start | bytes 331784 | tf_op jit(solution)/shard_map/ppermute | solution.py:216
  92.2 4.1 %collective-permute-start.14 = (bf16[48,1152]{1,0:T(8,128)(2,1)S(1)}, bf16[48,1152]{1,0:T(8,128)(2,1)S(1)}, u32[]{:S(2)}, u32[]{:S(2)}) collective-permute-start(bf16[48,1152]{1,0:T(8,128)(2,1)S(1)} %fusion.2), channel_id=1, source_target_pairs={{0,8},{1,9},{2,10},{3,11},{4,12},{5,13},{6,14},{7,15},{8,0},{9,1},... | collective-permute-start | bytes 331784 | tf_op jit(solution)/shard_map/ppermute | solution.py:216
  92.6 5.6 %collective-permute-start.15 = (bf16[48,1152]{1,0:T(8,128)(2,1)S(1)}, bf16[48,1152]{1,0:T(8,128)(2,1)S(1)}, u32[]{:S(2)}, u32[]{:S(2)}) collective-permute-start(bf16[48,1152]{1,0:T(8,128)(2,1)S(1)} %fusion.2), channel_id=1, source_target_pairs={{0,24},{1,25},{2,26},{3,27},{4,28},{5,29},{6,30},{7,31},{8,16},{9,... | collective-permute-start | bytes 331784 | tf_op jit(solution)/shard_map/ppermute | solution.py:216
  98.3 4.0 %collective-permute-start.16 = (bf16[48,1152]{1,0:T(8,128)(2,1)S(1)}, bf16[48,1152]{1,0:T(8,128)(2,1)S(1)}, u32[]{:S(2)}, u32[]{:S(2)}) collective-permute-start(bf16[48,1152]{1,0:T(8,128)(2,1)S(1)} %add_convert_fusion.1), channel_id=1, source_target_pairs={{0,2},{1,3},{2,0},{3,1},{4,6},{5,7},{6,4},{7,5},{8,10},{9,11},{10,... | collective-permute-start | bytes 331784 | tf_op jit(solution)/shard_map/ppermute | solution.py:216
  98.7 6.7 %collective-permute-start.17 = (bf16[48,1152]{1,0:T(8,128)(2,1)S(1)}, bf16[48,1152]{1,0:T(8,128)(2,1)S(1)}, u32[]{:S(2)}, u32[]{:S(2)}) collective-permute-start(bf16[48,1152]{1,0:T(8,128)(2,1)S(1)} %add_convert_fusion.1), channel_id=1, source_target_pairs={{0,4},{1,5},{2,6},{3,7},{4,0},{5,1},{6,2},{7,3},{8,12},{9,13},{10,... | collective-permute-start | bytes 331784 | tf_op jit(solution)/shard_map/ppermute | solution.py:216
  102.1 6.1 %collective-permute-start.18 = (bf16[48,1152]{1,0:T(8,128)(2,1)S(1)}, bf16[48,1152]{1,0:T(8,128)(2,1)S(1)}, u32[]{:S(2)}, u32[]{:S(2)}) collective-permute-start(bf16[48,1152]{1,0:T(8,128)(2,1)S(1)} %add_convert_fusion.1), channel_id=1, source_target_pairs={{0,6},{1,7},{2,4},{3,5},{4,2},{5,3},{6,0},{7,1},{8,14},{9,15},{10,... | collective-permute-start | bytes 331784 | tf_op jit(solution)/shard_map/ppermute | solution.py:216
  108.3 43.4 %collective-permute-start.19 = (bf16[4,48,1152]{2,1,0:T(8,128)(2,1)S(1)}, bf16[4,48,1152]{2,1,0:T(8,128)(2,1)S(1)}, u32[]{:S(2)}, u32[]{:S(2)}) collective-permute-start(bf16[4,48,1152]{2,1,0:T(8,128)(2,1)S(1)} %pad_maximum_fusion.1.mine_ref), channel_id=1, source_target_pairs={{0,1},{1,0},{2,3},{3,2},{4,5},{5,4},{6,7},{7,6},{8,9},{9,8},{10,11... | collective-permute-start | bytes 1327112 | tf_op jit(solution)/shard_map/ppermute | solution.py:216
  129.2 13.7 %collective-permute-start.8 = (bf16[2,512,128]{2,1,0:T(8,128)(2,1)}, bf16[2,512,128]{2,1,0:T(8,128)(2,1)S(1)}, u32[]{:S(2)}, u32[]{:S(2)}) collective-permute-start(bf16[2,512,128]{2,1,0:T(8,128)(2,1)} %get-tuple-element.38), channel_id=1, source_target_pairs={{0,3},{1,4},{2,5},{3,6},{4,7},{5,8},{6,9},{7,10},{8,11},{9,12},{10... | collective-permute-start | bytes 786440 | tf_op jit(solution)/shard_map/ppermute | solution.py:221
  129.7 13.2 %collective-permute-start.6 = (bf16[2,512,128]{2,1,0:T(8,128)(2,1)}, bf16[2,512,128]{2,1,0:T(8,128)(2,1)S(1)}, u32[]{:S(2)}, u32[]{:S(2)}) collective-permute-start(bf16[2,512,128]{2,1,0:T(8,128)(2,1)} %get-tuple-element.36), channel_id=1, source_target_pairs={{0,1},{1,2},{2,3},{3,4},{4,5},{5,6},{6,7},{7,8},{8,9},{9,10},{10,1... | collective-permute-start | bytes 786440 | tf_op jit(solution)/shard_map/ppermute | solution.py:221
  129.7 19.9 %collective-permute-start.7 = (bf16[2,512,128]{2,1,0:T(8,128)(2,1)}, bf16[2,512,128]{2,1,0:T(8,128)(2,1)S(1)}, u32[]{:S(2)}, u32[]{:S(2)}) collective-permute-start(bf16[2,512,128]{2,1,0:T(8,128)(2,1)} %get-tuple-element.37), channel_id=1, source_target_pairs={{0,2},{1,3},{2,4},{3,5},{4,6},{5,7},{6,8},{7,9},{8,10},{9,11},{10,... | collective-permute-start | bytes 786440 | tf_op jit(solution)/shard_map/ppermute | solution.py:221
  (13 other events, 135.6 us)

commit v2 on v0

v2 whole, which is shorter than its diff:
```python
import functools
import math

import jax
import jax.numpy as jnp
from jax import lax
from jax.experimental import pallas as pl
from jax.experimental.pallas import tpu as pltpu
from jax.sharding import PartitionSpec as P

C = 128
VOX = 512
TAPS = 27
WORK = 4
LAG = 4
F32 = jnp.float32
BF16 = jnp.bfloat16
ANY = pl.BlockSpec(memory_space=pl.ANY)
VM = pl.BlockSpec(memory_space=pltpu.VMEM)
SM = pl.BlockSpec(memory_space=pltpu.SMEM)
Y_BITS = (8, 16, 24)
Z_BITS = (2, 4, 6)


def shape(dims, dtype=BF16):
    return jax.ShapeDtypeStruct(dims, dtype)


def vmem(x):
    return pltpu.with_memory_space_constraint(x, pltpu.MemorySpace.VMEM)


def params():
    return pltpu.CompilerParams(vmem_limit_bytes=16 << 20)


def shift_rows(block, by):
    if by == 0:
        return block
    pad = jnp.zeros((abs(by),) + block.shape[1:], block.dtype)
    if by > 0:
        return jnp.concatenate([pad, block[:-by]], axis=0)
    return jnp.concatenate([block[-by:], pad], axis=0)


def deltas_of(share, p, sup, above):
    p = p.astype(F32)
    weighted = (sup.astype(F32).reshape(64, 8, C) * share[None]).reshape(VOX, C)
    grad = weighted.astype(BF16).astype(F32) + above.astype(F32)
    sig = jax.nn.sigmoid(p)
    return grad * (sig * (1.0 + p * (1.0 - sig)))


def spread(delta, pd):
    delta = delta.reshape(64, 8, C)
    place = lax.broadcasted_iota(jnp.int32, (64, 8, C), 1)
    for w in (-1, 0, 1):
        if w == 0:
            moved = delta
        elif w == 1:
            moved = jnp.where(place == 0, 0.0, pltpu.roll(delta, 1, 1))
        else:
            moved = jnp.where(place == 7, 0.0, pltpu.roll(delta, 7, 1))
        moved = moved.reshape(8, 8, 8, C)
        zero = jnp.zeros((8, 1, 8, C), F32)
        for v in (-1, 0, 1):
            if v == 0:
                out = moved
            elif v == 1:
                out = jnp.concatenate([zero, moved[:, :-1]], axis=1)
            else:
                out = jnp.concatenate([moved[:, 1:], zero], axis=1)
            at = ((v + 1) * 3 + (w + 1)) * C
            pd[:, at : at + C] = out.reshape(VOX, C).astype(BF16)


def input_grad(pd, wn):
    y = lax.dot_general(pd, wn, (((1,), (1,)), ((), ())), preferred_element_type=F32)
    gin = y[:, C : 2 * C] + shift_rows(y[:, :C], -64) + shift_rows(y[:, 2 * C :], 64)
    return gin.astype(BF16)


def position(slot):
    late = lax.axis_size("section") - 1 - lax.axis_index("section")
    index = slot - LAG * late
    return (index >= 0) & (index < WORK), jnp.clip(index, 0, WORK - 1)


def first_kernel(
    c_hbm, p_hbm, sup_hbm, w_hbm, gin_ref, gins, deltas, wn, p_ref, sup_ref, shares, pd, w_ref, counts, sems
):
    active, _ = position(0)
    rest = pl.ds(1, WORK - 1)
    copies = [
        pltpu.make_async_copy(c_hbm, counts, sems.at[5]),
        pltpu.make_async_copy(p_hbm.at[0], p_ref.at[0], sems.at[0]),
        pltpu.make_async_copy(sup_hbm.at[0], sup_ref.at[0], sems.at[1]),
        pltpu.make_async_copy(w_hbm, w_ref, sems.at[2]),
        pltpu.make_async_copy(p_hbm.at[rest], p_ref.at[rest], sems.at[3]),
        pltpu.make_async_copy(sup_hbm.at[rest], sup_ref.at[rest], sems.at[4]),
    ]
    for copy in copies:
        copy.start()
    copies[0].wait()
    for brick in range(WORK):
        count = counts[brick // 2, brick % 2].astype(F32)
        shares[brick] = jnp.full((8, C), count * (1.0 / VOX), F32)
    copies[1].wait()
    copies[2].wait()

    @pl.when(active)
    def _():
        zero = jnp.zeros((VOX, C), BF16)
        delta = deltas_of(shares[0], p_ref[0], sup_ref[0], zero)
        deltas[0] = delta.astype(BF16)
        spread(delta, pd)

    copies[3].wait()
    for u in range(3):
        for tap in range(9):
            at = (u * 9 + tap) * C
            wn[u * C : (u + 1) * C, tap * C : (tap + 1) * C] = w_ref[at : at + C, :]

    @pl.when(active)
    def _():
        gin = input_grad(pd[...], wn[...])
        gin_ref[...] = gin
        gins[0] = gin

    copies[4].wait()
    copies[5].wait()


def first_step(counts, preacts, sup, weights):
    hbm = lambda x: pltpu.with_memory_space_constraint(x, pltpu.MemorySpace.HBM)
    bricks = pltpu.VMEM((WORK, VOX, C), BF16)
    return pl.pallas_call(
        first_kernel,
        in_specs=[ANY] * 4,
        out_specs=[VM] * 7,
        out_shape=[
            shape((VOX, C)),
            bricks,
            bricks,
            pltpu.VMEM((3 * C, 9 * C), BF16),
            bricks,
            bricks,
            pltpu.VMEM((WORK, 8, C), F32),
        ],
        scratch_shapes=[
            pltpu.VMEM((VOX, 9 * C), BF16),
            pltpu.VMEM((TAPS * C, C), BF16),
            pltpu.SMEM((2, 2), jnp.int32),
            pltpu.SemaphoreType.DMA((6,)),
        ],
        compiler_params=params(),
        name="tick_first",
    )(hbm(counts), hbm(preacts), hbm(sup), hbm(weights))


def tick_kernel(slot, sends, shares, p_ref, sup_ref, above_ref, wn, gins_in, deltas_in, *outs):
    gins, deltas, pd = outs[0], outs[1], outs[-1]
    active, brick = position(slot)

    @pl.when(active)
    def _():
        delta = deltas_of(shares[brick], p_ref[brick], sup_ref[brick], above_ref[...])
        deltas[brick] = delta.astype(BF16)
        spread(delta, pd)
        gin = input_grad(pd[...], wn[...])
        gins[brick] = gin
        if sends:
            outs[2][...] = gin


def tick_step(slot, sends, shares, preacts, sup, above, wn, gins, deltas):
    bricks = pltpu.VMEM((WORK, VOX, C), BF16)
    return pl.pallas_call(
        functools.partial(tick_kernel, slot, sends),
        in_specs=[VM] * 7,
        out_specs=[VM] * (2 + sends),
        out_shape=[bricks, bricks] + [shape((VOX, C))] * sends,
        scratch_shapes=[pltpu.VMEM((VOX, 9 * C), BF16)],
        input_output_aliases={5: 0, 6: 1},
        compiler_params=params(),
        cost_estimate=pl.CostEstimate(
            flops=2 * VOX * TAPS * C * C, bytes_accessed=2 << 20, transcendentals=VOX * C
        ),
        name="tick%d" % slot,
    )(vmem(shares), vmem(preacts), vmem(sup), above, vmem(wn), vmem(gins), vmem(deltas))


def transpose_kernel(x_ref, out):
    for brick in range(WORK):
        x = x_ref[brick].T
        pad = jnp.zeros((C, 64), BF16)
        out[brick, :C, :] = jnp.concatenate([pad, x[:, :-64]], axis=1)
        out[brick, C : 2 * C, :] = x
        out[brick, 2 * C :, :] = jnp.concatenate([x[:, 64:], pad], axis=1)


def transpose_step(inputs):
    return pl.pallas_call(
        transpose_kernel,
        in_specs=[VM],
        out_specs=VM,
        out_shape=shape((WORK, 3 * C, VOX)),
        compiler_params=params(),
        name="inputs_across",
    )(inputs)


def early_kernel(deltas, xt, acc, pd):
    spread(deltas[0].astype(F32), pd.at[0])
    total = jnp.dot(xt[0], pd[0], preferred_element_type=F32)
    spread(deltas[1].astype(F32), pd.at[1])
    acc[...] = total + jnp.dot(xt[1], pd[1], preferred_element_type=F32)


def early_step(deltas, xt):
    return pl.pallas_call(
        early_kernel,
        in_specs=[VM] * 2,
        out_specs=VM,
        out_shape=shape((3 * C, 9 * C), F32),
        scratch_shapes=[pltpu.VMEM((2, VOX, 9 * C), BF16)],
        compiler_params=params(),
        cost_estimate=pl.CostEstimate(
            flops=4 * VOX * TAPS * C * C, bytes_accessed=4 << 20, transcendentals=0
        ),
        name="weight_terms_early",
    )(deltas, xt)


def late_kernel(
    slot, shares, p_ref, sup_ref, above_ref, deltas, xt, acc_in, keep_ref, send_ref, pd, pd_2, acc
):
    active, _ = position(slot)
    last = WORK - 1
    spread(deltas[last - 1].astype(F32), pd_2)
    total = acc_in[...] + jnp.dot(xt[last - 1], pd_2[...], preferred_element_type=F32)

    @pl.when(active)
    def _():
        spread(deltas_of(shares[last], p_ref[last], sup_ref[last], above_ref[...]), pd)

    @pl.when(jnp.logical_not(active))
    def _():
        spread(deltas[last].astype(F32), pd)

    acc[...] = total + jnp.dot(xt[last], pd[...], preferred_element_type=F32)
    core = lax.rem(lax.axis_index("brick"), 2)
    mine = pl.multiple_of(core * 192, 16)
    other = pl.multiple_of(192 - core * 192, 16)
    send_ref[...] = acc[pl.ds(other, 192), :].astype(BF16)
    keep_ref[...] = acc[pl.ds(mine, 192), :].astype(BF16)


def late_step(slot, shares, preacts, sup, above, deltas, xt, acc):
    return pl.pallas_call(
        functools.partial(late_kernel, slot),
        in_specs=[VM] * 7,
        out_specs=[VM] * 3,
        out_shape=[shape((192, 9 * C))] * 2 + [shape((VOX, 9 * C))],
        scratch_shapes=[pltpu.VMEM((VOX, 9 * C), BF16), pltpu.VMEM((3 * C, 9 * C), F32)],
        compiler_params=params(),
        cost_estimate=pl.CostEstimate(
            flops=4 * VOX * TAPS * C * C, bytes_accessed=7 << 20, transcendentals=0
        ),
        name="weight_terms",
    )(vmem(shares), vmem(preacts), vmem(sup), above, vmem(deltas), xt, acc)


def pack_kernel(slot, pick, gins, pd, wn, local, *sent):
    active, _ = position(slot)
    zero = jnp.zeros((VOX, C), BF16)
    outs = (local,) + sent

    def put(micro, first, second):
        for d in range(4):
            which = pick[micro, d]
            outs[d][micro] = jnp.where(which == 0, first, jnp.where(which == 1, second, zero))

    put(0, gins[0], gins[1])

    @pl.when(active)
    def _():
        put(1, gins[2], input_grad(pd[...], wn[...]))

    @pl.when(jnp.logical_not(active))
    def _():
        put(1, gins[2], gins[3])


def pack_step(slot, pick, gins, pd, wn):
    return pl.pallas_call(
        functools.partial(pack_kernel, slot),
        in_specs=[SM] + [VM] * 3,
        out_specs=[VM] * 4,
        out_shape=[shape((2, VOX, C))] * 4,
        compiler_params=params(),
        cost_estimate=pl.CostEstimate(
            flops=2 * VOX * TAPS * C * C, bytes_accessed=4 << 20, transcendentals=0
        ),
        name="pack",
    )(pick, vmem(gins), pd, vmem(wn))


def slots_kernel(*refs):
    blocks, out, sems = refs[:4], refs[4], refs[5]
    copies = [
        pltpu.make_async_copy(block.at[micro], out.at[micro, d], sems.at[d, micro])
        for d, block in enumerate(blocks)
        for micro in range(2)
    ]
    for copy in copies:
        copy.start()
    for copy in copies:
        copy.wait()


def slots_step(blocks):
    return pl.pallas_call(
        slots_kernel,
        in_specs=[VM] * 4,
        out_specs=ANY,
        out_shape=shape((2, 4, VOX, C)),
        scratch_shapes=[pltpu.SemaphoreType.DMA((4, 2))],
        compiler_params=params(),
        name="slots",
    )(*blocks)


def finish_kernel(scale, mine, other, out_hbm, out, sems):
    me = lax.axis_index("brick")
    core = lax.rem(me, 2)
    label = lax.div(me, 8)
    copies = []
    for u in range(3):
        for i in range(8):
            group = u * 8 + i
            half, part, row = group // 12, group % 12 // 3, group % 3 * 16
            at = lax.bitwise_xor(label, part)
            rows = jnp.where(core == half, mine[at, row : row + 16], other[at, row : row + 16])
            rows = rows.astype(F32) * scale
            for tap in range(9):
                to = (u * 9 + tap) * C + i * 16
                out[to : to + 16, :] = rows[:, tap * C : (tap + 1) * C]
        size = 9 * C
        copies.append(
            pltpu.make_async_copy(
                out.at[u * size : (u + 1) * size], out_hbm.at[u * size : (u + 1) * size], sems.at[u]
            )
        )
        copies[-1].start()
    for copy in copies:
        copy.wait()


def finish_step(scale, mine, other):
    return pl.pallas_call(
        functools.partial(finish_kernel, scale),
        in_specs=[VM] * 2,
        out_specs=ANY,
        out_shape=shape((TAPS * C, C), F32),
        scratch_shapes=[pltpu.VMEM((TAPS * C, C), F32), pltpu.SemaphoreType.DMA((3,))],
        compiler_params=params(),
        name="finish_weights",
    )(mine, other)


def swap(block, bits):
    pairs = [(i, i ^ bits) for i in range(lax.axis_size("brick"))]
    return lax.ppermute(block, "brick", pairs)


def shifted(block, distance):
    n = lax.axis_size("brick")
    return lax.ppermute(block, "brick", [(i, (i + distance) % n) for i in range(n)])


def shards(saved_inputs, saved_preacts, supervision, weights, trainer, counts):
    peers = lax.axis_size("brick")
    me = lax.axis_index("brick")
    layers = lax.axis_size("section")
    micros, own = saved_inputs.shape[1:3]
    slots = WORK + LAG * (layers - 1)

    inputs = saved_inputs.reshape(WORK, VOX, C)
    preacts = saved_preacts.reshape(WORK, VOX, C)
    sup = supervision.reshape(WORK, VOX, C)
    targets = lax.dynamic_slice_in_dim(trainer, me * own, own, 1)
    offsets = jnp.mod(targets - me, peers)
    match = offsets[:, :, None] == jnp.arange(4, dtype=jnp.int32)[None, None, :]
    brick = jnp.arange(own, dtype=jnp.int32)
    pick = jnp.max(jnp.where(match, brick[None, :, None], -1), axis=1).astype(jnp.int32)

    above = {}
    gin, gins, deltas, wn, preacts, sup, shares = first_step(counts, preacts, sup, weights[0])
    zero = jnp.zeros((VOX, C), BF16)
    xt = transpose_step(inputs)
    for slot in range(slots - 1):
        senders = [s for s in range(1, layers) if 0 <= slot - LAG * (layers - 1 - s) < WORK]
        if slot > 0:
            gins, deltas, *sent = tick_step(
                slot, len(senders) > 0, shares, preacts, sup, above.get(slot, zero), wn, gins, deltas
            )
            gin = sent[0] if sent else None
        if senders:
            above[slot + LAG] = lax.ppermute(gin, "section", [(s, s - 1) for s in senders])
        if slot == slots - 3:
            acc = early_step(deltas, xt)
    last = slots - 1
    keep, send, pd = late_step(last, shares, preacts, sup, above[last], deltas, xt, acc)
    from_core = swap(send, 1)
    local, send_1, send_2, send_3 = pack_step(last, pick, gins, pd, wn)
    from_3 = shifted(send_3, 3)
    from_core, send_1, send_2 = lax.optimization_barrier((from_core, send_1, send_2))

    half = (keep.astype(F32) + from_core.astype(F32)).astype(BF16).reshape(4, 48, 9 * C)
    y = me // 8
    part = [lax.dynamic_index_in_dim(half, lax.bitwise_xor(y, k), 0, False) for k in range(4)]
    total = part[0].astype(F32)
    for k, bits in enumerate(Y_BITS):
        total = total + swap(part[k + 1], bits).astype(F32)
    total, from_3 = lax.optimization_barrier((total.astype(BF16), from_3))
    full = total.astype(F32)
    for bits in Z_BITS:
        full = full + swap(total, bits).astype(F32)
    full, send_1, send_2 = lax.optimization_barrier((full.astype(BF16), send_1, send_2))
    got = [swap(full, bits) for bits in Y_BITS] + [shifted(send_1, 1), shifted(send_2, 2)]
    *got, from_1, from_2 = lax.optimization_barrier(got)
    blocks = [local, from_1, from_2, from_3]
    skip_grads = slots_step(blocks).reshape((1, micros, 4) + saved_inputs.shape[3:])
    mine = jnp.stack([full] + got)
    other = swap(mine, 1)
    scale = 1.0 / math.sqrt(WORK * peers * VOX)
    weight_grads = finish_step(scale, mine, other)
    return skip_grads, weight_grads[None]


def solution(mesh):
    bricks = P("section", None, "brick", None, None, None, None)
    in_specs = (bricks, bricks, bricks, P("section", None, None), P(), P(None, "brick"))
    out_specs = (bricks, P("section", None, None))
    return jax.shard_map(shards, mesh=mesh, in_specs=in_specs, out_specs=out_specs, check_vma=False)
```

time: 503 us -> 91.5 us (0.18); the launches traced: 496 us -> 91.2 us
  waiting for transfers between devices: 315 us -> 45.1 us
  local copies, waits for them, and re-layouts: 55.9 us -> 0.09 us
  other arithmetic: 43.3 us -> 1.66 us
  matrix products: 39.9 us -> 0 us
  Pallas kernels: 0 us -> 13.3 us
  between operations: 14.5 us -> 1.22 us
  starting transfers between devices: 24.4 us -> 29.9 us
    ppermute x13 -> x26, waiting for transfers between devices: 201 us -> 45.1 us  [the longest x3 16.9 us: shifted(): lax.ppermute(block, 'brick', [(i, (i + distance) % n) for i in range(n)])]
    psum x1 -> x0, waiting for transfers between devices: 114 us -> none  [shards(): lax.psum(accumulated.astype(jnp.bfloat16), 'brick').astype(jnp.float32)]
    dot_general x16 -> x0, matrix products: 39.9 us -> none  [the longest x8 31.2 us: weight_term(): lax.dot_general(columns(inputs_one), flat_deltas, (((0,), (0,)), ((), ())...]
    while x432 -> x0, local copies, waits for them, and re-layouts: 26.7 us -> none
    convert_element_type x14 -> x3, other arithmetic: 22.1 us -> 1.42 us  [the longest x1 1.3 us: shards(): (keep.astype(F32) + from_core.astype(F32)).astype(BF16)]
    pallas_call x0 -> x21, Pallas kernels: none -> 13.3 us  [the longest x14 3.12 us: tick_step(): pl.pallas_call(functools.partial(tick_kernel, slot, sends), in_specs=[VM]...]
    squeeze x10 -> x1, local copies, waits for them, and re-layouts: 9.46 us -> 0.04 us  [shards(): lax.dynamic_index_in_dim(half, lax.bitwise_xor(y, k), 0, False)]
    another operation x17 -> x1, other arithmetic: 8.59 us -> 0.07 us  [shards(): mine = jnp.stack([full] + got)]
  transfers between devices with their start and end apart: 14 -> 26, of which waited for: 9 -> 15; matrix products, arithmetic and copies ran while one was open for 3% -> 0% of each run, Pallas kernels for 0% -> 8%
where the time goes in v2:
time: 91.5 us; the launch traced here: 91.2 us
  waiting for transfers between devices  45.1 us (49%)
  starting transfers between devices  29.9 us (33%)
  Pallas kernels  13.3 us (15%)
  other arithmetic  1.66 us (2%)
  between operations  1.22 us (1%)
    ppermute x3, waiting for transfers between devices, shifted(): lax.ppermute(block, 'brick', [(i, (i + distance) % n) for i in range(n)])  16.9 us
    ppermute x11, waiting for transfers between devices, swap(): return lax.ppermute(block, 'brick', pairs)  14.2 us
    ppermute x12, waiting for transfers between devices, shards(): lax.ppermute(gin, 'section', [(s, s - 1) for s in senders])  14 us
    ppermute x11, starting transfers between devices, swap(): return lax.ppermute(block, 'brick', pairs)  13.3 us
    ppermute x12, starting transfers between devices, shards(): lax.ppermute(gin, 'section', [(s, s - 1) for s in senders])  10.7 us
    ppermute x3, starting transfers between devices, shifted(): lax.ppermute(block, 'brick', [(i, (i + distance) % n) for i in range(n)])  5.93 us
    pallas_call x14, Pallas kernels, tick_step(): pl.pallas_call(functools.partial(tick_kernel, slot, sends), in_specs=[VM]...  3.12 us
    pallas_call x1, Pallas kernels, late_step(): pl.pallas_call(functools.partial(late_kernel, slot), in_specs=[VM] * 7, o...  3.03 us
  transfers between devices with their start and end apart: 26, of which 15 were waited for; matrix products, arithmetic and copies ran while one was open for 0% of the time, Pallas kernels for 8%

profile of v2, /device:TPU:1, one launch (start us, length us, event | category | flops | bytes accessed | tf_op | source)
XLA Modules:
  0.0 91.2 jit_solution(1694278908418692084)
XLA Ops:
  0.6 1.6 %tick_first.1 = (bf16[512,128]{1,0:T(8,128)(2,1)S(1)}, bf16[4,512,128]{2,1,0:T(8,128)(2,1)S(1)}, bf16[4,512,128]{2,1,0:T(8,128)(2,1)S(1)}, bf16[384,1152]{1,0:T(...) custom-call(s32[2,2]{1,0:T(2,128)} %c_hbm.1, ...), custom_call_target="tpu_custom_call" | custom-call | tf_op jit(solution)/shard_map/tick_first/pallas_call | solution.py:137
  7.9 1.4 %collective-permute-start.9 = (bf16[512,128]{1,0:T(8,128)(2,1)S(1)}, bf16[512,128]{1,0:T(8,128)(2,1)S(1)}, u32[]{:S(2)}, u32[]{:S(2)}) collective-permute-start(bf16[512,128]{1,0:T(8,128)(2,1)S(1)} %get-tuple-element.101), channel_id=1, source_target_pairs={{32,0},{33,1},{34,2},{35,3},{36,4},{37,5},{38,6},{39,7},{40,8},{41... | collective-permute-start | bytes 393224 | tf_op jit(solution)/shard_map/ppermute | solution.py:410
  9.4 1.3 %collective-permute-start.8 = (bf16[512,128]{1,0:T(8,128)(2,1)S(1)}, bf16[512,128]{1,0:T(8,128)(2,1)S(1)}, u32[]{:S(2)}, u32[]{:S(2)}) collective-permute-start(bf16[512,128]{1,0:T(8,128)(2,1)S(1)} %get-tuple-element.100), channel_id=1, source_target_pairs={{32,0},{33,1},{34,2},{35,3},{36,4},{37,5},{38,6},{39,7},{40,8},{41... | collective-permute-start | bytes 393224 | tf_op jit(solution)/shard_map/ppermute | solution.py:410
  11.1 1.3 %collective-permute-start.7 = (bf16[512,128]{1,0:T(8,128)(2,1)S(1)}, bf16[512,128]{1,0:T(8,128)(2,1)S(1)}, u32[]{:S(2)}, u32[]{:S(2)}) collective-permute-start(bf16[512,128]{1,0:T(8,128)(2,1)S(1)} %get-tuple-element.99), channel_id=1, source_target_pairs={{32,0},{33,1},{34,2},{35,3},{36,4},{37,5},{38,6},{39,7},{40,8},{41... | collective-permute-start | bytes 393224 | tf_op jit(solution)/shard_map/ppermute | solution.py:410
  12.4 1.3 %collective-permute-start.11 = (bf16[512,128]{1,0:T(8,128)(2,1)S(1)}, bf16[512,128]{1,0:T(8,128)(2,1)S(1)}, u32[]{:S(2)}, u32[]{:S(2)}) collective-permute-start(bf16[512,128]{1,0:T(8,128)(2,1)S(1)} %get-tuple-element.112), channel_id=1, source_target_pairs={{32,0},{33,1},{34,2},{35,3},{36,4},{37,5},{38,6},{39,7},{40,8},{41... | collective-permute-start | bytes 393224 | tf_op jit(solution)/shard_map/ppermute | solution.py:410
  13.7 7.2 %collective-permute-done.9.above_ref = bf16[512,128]{1,0:T(8,128)(2,1)S(1)} collective-permute-done((bf16[512,128]{1,0:T(8,128)(2,1)S(1)}, bf16[512,128]{1,0:T(8,128)(2,1)S(1)}, u32[]{:S(2)}, u32[]{:S(2)}) %collective-permute-start.9) | collective-permute-done | bytes 131104 | tf_op jit(solution)/shard_map/ppermute | solution.py:410
  21.9 4.1 %collective-permute-done.8.above_ref = bf16[512,128]{1,0:T(8,128)(2,1)S(1)} collective-permute-done((bf16[512,128]{1,0:T(8,128)(2,1)S(1)}, bf16[512,128]{1,0:T(8,128)(2,1)S(1)}, u32[]{:S(2)}, u32[]{:S(2)}) %collective-permute-start.8) | collective-permute-done | bytes 131104 | tf_op jit(solution)/shard_map/ppermute | solution.py:410
  27.1 1.3 %weight_terms_early.1.acc_in = f32[384,1152]{1,0:T(8,128)S(1)} custom-call(bf16[4,512,128]{2,1,0:T(8,128)(2,1)S(1)} %get-tuple-element.110.deltas_in.deltas, bf16[4,384,512]{2,1,0:T(8,128)(2,1)S(1)} %inputs_across.1.xt), custom_call_target="tpu_custom_call" | custom-call | flops 905969664 | bytes 4194304 | tf_op jit(solution)/shard_map/weight_terms_early/pallas_call | solution.py:221
  29.6 2.4 %collective-permute-done.11.above_ref = bf16[512,128]{1,0:T(8,128)(2,1)S(1)} collective-permute-done((bf16[512,128]{1,0:T(8,128)(2,1)S(1)}, bf16[512,128]{1,0:T(8,128)(2,1)S(1)}, u32[]{:S(2)}, u32[]{:S(2)}) %collective-permute-start.11) | collective-permute-done | bytes 131104 | tf_op jit(solution)/shard_map/ppermute | solution.py:410
  32.0 3.0 %weight_terms.1 = (bf16[192,1152]{1,0:T(8,128)(2,1)S(1)}, bf16[192,1152]{1,0:T(8,128)(2,1)}, bf16[512,1152]{1,0:T(8,128)(2,1)S(1)}) custom-call(f32[4,8,128]{2,1,0:T(8,128)S(1)} %get-tuple-element.68.shares, bf16[4,512,128]{2,1,0:T(8,128)(2,1)S(1)} %get-tuple-element.69.p_ref, bf16[4,512,128]{2,1,0:T(8,128)(2,1)S(1)} %get-tuple-element.70.sup_ref, ...), custom_call_target="tpu_custom_call" | custom-call | flops 905969664 | bytes 7340032 | tf_op jit(solution)/shard_map/weight_terms/pallas_call | solution.py:260
  35.0 1.5 %collective-permute-start.12 = (bf16[192,1152]{1,0:T(8,128)(2,1)}, bf16[192,1152]{1,0:T(8,128)(2,1)}, u32[]{:S(2)}, u32[]{:S(2)}) collective-permute-start(bf16[192,1152]{1,0:T(8,128)(2,1)} %get-tuple-element.117), channel_id=1, source_target_pairs={{0,1},{1,0},{2,3},{3,2},{4,5},{5,4},{6,7},{7,6},{8,9},{9,8},{10,11... | collective-permute-start | bytes 1327112 | tf_op jit(solution)/shard_map/ppermute | solution.py:374
  36.7 1.6 %pack.1 = (bf16[2,512,128]{2,1,0:T(8,128)(2,1)S(1)}, bf16[2,512,128]{2,1,0:T(8,128)(2,1)S(1)}, bf16[2,512,128]{2,1,0:T(8,128)(2,1)S(1)}, bf16[2,512,128]{2,1,0:T(8,128)(2,1)S(1)}) custom-call(s32[2,4]{1,0:T(2,128)S(1)} %fusion.3.pick, bf16[4,512,128]{2,1,0:T(8,128)(2,1)S(1)} %get-tuple-element.111.gins, bf16[512,1152]{1,0:T(8,128)(2,1)S(1)} %get-tuple-element.114.pd, ...), custom_call_target="tpu_custom_call" | custom-call | flops 452984832 | bytes 4194304 | tf_op jit(solution)/shard_map/pack/pallas_call | solution.py:296
  38.3 1.3 %add_convert_fusion = bf16[192,1152]{1,0:T(8,128)(2,1)S(1)} fusion(bf16[192,1152]{1,0:T(8,128)(2,1)} %collective-permute-done.12, bf16[192,1152]{1,0:T(8,128)(2,1)S(1)} %get-tuple-element.116), kind=kLoop, calls=%fused_computation | loop fusion | flops 884736 | bytes 1327104 | tf_op jit(solution)/shard_map/convert_element_type | solution.py:420
  39.7 1.4 %collective-permute-start.13 = (bf16[48,1152]{1,0:T(8,128)(2,1)S(1)}, bf16[48,1152]{1,0:T(8,128)(2,1)S(1)}, u32[]{:S(2)}, u32[]{:S(2)}) collective-permute-start(bf16[48,1152]{1,0:T(8,128)(2,1)S(1)} %get-tuple-element.134), channel_id=1, source_target_pairs={{0,8},{1,9},{2,10},{3,11},{4,12},{5,13},{6,14},{7,15},{8,0},{9,1},... | collective-permute-start | bytes 331784 | tf_op jit(solution)/shard_map/ppermute | solution.py:374
  41.1 2.7 %collective-permute-start.14 = (bf16[48,1152]{1,0:T(8,128)(2,1)S(1)}, bf16[48,1152]{1,0:T(8,128)(2,1)S(1)}, u32[]{:S(2)}, u32[]{:S(2)}) collective-permute-start(bf16[48,1152]{1,0:T(8,128)(2,1)S(1)} %get-tuple-element.136), channel_id=1, source_target_pairs={{0,16},{1,17},{2,18},{3,19},{4,20},{5,21},{6,22},{7,23},{8,24},{9,... | collective-permute-start | bytes 331784 | tf_op jit(solution)/shard_map/ppermute | solution.py:374
  43.7 4.4 %collective-permute-start.16 = (bf16[2,512,128]{2,1,0:T(8,128)(2,1)}, bf16[2,512,128]{2,1,0:T(8,128)(2,1)S(1)}, u32[]{:S(2)}, u32[]{:S(2)}) collective-permute-start(bf16[2,512,128]{2,1,0:T(8,128)(2,1)} %copy-done.3), channel_id=1, source_target_pairs={{0,3},{1,4},{2,5},{3,6},{4,7},{5,8},{6,9},{7,10},{8,11},{9,12},{10... | collective-permute-start | bytes 786440 | tf_op jit(solution)/shard_map/ppermute | solution.py:379
  49.2 2.5 %collective-permute-done.15 = bf16[48,1152]{1,0:T(8,128)(2,1)S(1)} collective-permute-done((bf16[48,1152]{1,0:T(8,128)(2,1)S(1)}, bf16[48,1152]{1,0:T(8,128)(2,1)S(1)}, u32[]{:S(2)}, u32[]{:S(2)}) %collective-permute-start.15) | collective-permute-done | bytes 110624 | tf_op jit(solution)/shard_map/ppermute | solution.py:374
  51.8 8.9 %collective-permute-done.16.refs_3_ = bf16[2,512,128]{2,1,0:T(8,128)(2,1)S(1)} collective-permute-done((bf16[2,512,128]{2,1,0:T(8,128)(2,1)}, bf16[2,512,128]{2,1,0:T(8,128)(2,1)S(1)}, u32[]{:S(2)}, u32[]{:S(2)}) %collective-permute-start.16) | collective-permute-done | bytes 262176 | tf_op jit(solution)/shard_map/ppermute | solution.py:379
  60.7 3.9 %collective-permute-start.19 = (bf16[48,1152]{1,0:T(8,128)(2,1)S(1)}, bf16[48,1152]{1,0:T(8,128)(2,1)S(1)}, u32[]{:S(2)}, u32[]{:S(2)}) collective-permute-start(bf16[48,1152]{1,0:T(8,128)(2,1)S(1)} %fusion.2), channel_id=1, source_target_pairs={{0,6},{1,7},{2,4},{3,5},{4,2},{5,3},{6,0},{7,1},{8,14},{9,15},{10,... | collective-permute-start | bytes 331784 | tf_op jit(solution)/shard_map/ppermute | solution.py:374
  65.9 3.5 %collective-permute-done.19 = bf16[48,1152]{1,0:T(8,128)(2,1)S(1)} collective-permute-done((bf16[48,1152]{1,0:T(8,128)(2,1)S(1)}, bf16[48,1152]{1,0:T(8,128)(2,1)S(1)}, u32[]{:S(2)}, u32[]{:S(2)}) %collective-permute-start.19) | collective-permute-done | bytes 110624 | tf_op jit(solution)/shard_map/ppermute | solution.py:374
  71.0 3.9 %collective-permute-start.22 = (bf16[48,1152]{1,0:T(8,128)(2,1)S(1)}, bf16[48,1152]{1,0:T(8,128)(2,1)S(1)}, u32[]{:S(2)}, u32[]{:S(2)}) collective-permute-start(bf16[48,1152]{1,0:T(8,128)(2,1)S(1)} %add_convert_fusion.1), channel_id=1, source_target_pairs={{0,24},{1,25},{2,26},{3,27},{4,28},{5,29},{6,30},{7,31},{8,16},{9,... | collective-permute-start | bytes 331784 | tf_op jit(solution)/shard_map/ppermute | solution.py:374
  75.7 1.5 %collective-permute-done.21 = bf16[48,1152]{1,0:T(8,128)(2,1)S(1)} collective-permute-done((bf16[48,1152]{1,0:T(8,128)(2,1)S(1)}, bf16[48,1152]{1,0:T(8,128)(2,1)S(1)}, u32[]{:S(2)}, u32[]{:S(2)}) %collective-permute-start.21) | collective-permute-done | bytes 110624 | tf_op jit(solution)/shard_map/ppermute | solution.py:374
  77.2 2.7 %collective-permute-done.22 = bf16[48,1152]{1,0:T(8,128)(2,1)S(1)} collective-permute-done((bf16[48,1152]{1,0:T(8,128)(2,1)S(1)}, bf16[48,1152]{1,0:T(8,128)(2,1)S(1)}, u32[]{:S(2)}, u32[]{:S(2)}) %collective-permute-start.22) | collective-permute-done | bytes 110624 | tf_op jit(solution)/shard_map/ppermute | solution.py:374
  79.9 8.0 %collective-permute-done.24.refs_2_ = bf16[2,512,128]{2,1,0:T(8,128)(2,1)S(1)} collective-permute-done((bf16[2,512,128]{2,1,0:T(8,128)(2,1)S(1)}, bf16[2,512,128]{2,1,0:T(8,128)(2,1)S(1)}, u32[]{:S(2)}, u32[]{:S(2)}) %collective-permute-start.24) | collective-permute-done | bytes 262176 | tf_op jit(solution)/shard_map/ppermute | solution.py:379
  (67 shorter events, 17.5 us)
Async XLA Ops:
  2.2 2.8 %collective-permute-start.2 = (bf16[512,128]{1,0:T(8,128)(2,1)S(1)}, bf16[512,128]{1,0:T(8,128)(2,1)S(1)}, u32[]{:S(2)}, u32[]{:S(2)}) collective-permute-start(bf16[512,128]{1,0:T(8,128)(2,1)S(1)} %get-tuple-element.78), channel_id=1, source_target_pairs={{96,64},{97,65},{98,66},{99,67},{100,68},{101,69},{102,70},{103,71... | collective-permute-start | bytes 393224 | tf_op jit(solution)/shard_map/ppermute | solution.py:410
  3.6 2.8 %collective-permute-start = (bf16[512,128]{1,0:T(8,128)(2,1)S(1)}, bf16[512,128]{1,0:T(8,128)(2,1)S(1)}, u32[]{:S(2)}, u32[]{:S(2)}) collective-permute-start(bf16[512,128]{1,0:T(8,128)(2,1)S(1)} %get-tuple-element.76), channel_id=1, source_target_pairs={{96,64},{97,65},{98,66},{99,67},{100,68},{101,69},{102,70},{103,71... | collective-permute-start | bytes 393224 | tf_op jit(solution)/shard_map/ppermute | solution.py:410
  4.4 2.8 %collective-permute-start.6 = (bf16[512,128]{1,0:T(8,128)(2,1)S(1)}, bf16[512,128]{1,0:T(8,128)(2,1)S(1)}, u32[]{:S(2)}, u32[]{:S(2)}) collective-permute-start(bf16[512,128]{1,0:T(8,128)(2,1)S(1)} %get-tuple-element.90), channel_id=1, source_target_pairs={{96,64},{97,65},{98,66},{99,67},{100,68},{101,69},{102,70},{103,71... | collective-permute-start | bytes 393224 | tf_op jit(solution)/shard_map/ppermute | solution.py:410
  5.1 2.8 %collective-permute-start.5 = (bf16[512,128]{1,0:T(8,128)(2,1)S(1)}, bf16[512,128]{1,0:T(8,128)(2,1)S(1)}, u32[]{:S(2)}, u32[]{:S(2)}) collective-permute-start(bf16[512,128]{1,0:T(8,128)(2,1)S(1)} %get-tuple-element.89), channel_id=1, source_target_pairs={{64,32},{65,33},{66,34},{67,35},{68,36},{69,37},{70,38},{71,39},{7... | collective-permute-start | bytes 393224 | tf_op jit(solution)/shard_map/ppermute | solution.py:410
  5.8 3.6 %collective-permute-start.4 = (bf16[512,128]{1,0:T(8,128)(2,1)S(1)}, bf16[512,128]{1,0:T(8,128)(2,1)S(1)}, u32[]{:S(2)}, u32[]{:S(2)}) collective-permute-start(bf16[512,128]{1,0:T(8,128)(2,1)S(1)} %get-tuple-element.88), channel_id=1, source_target_pairs={{64,32},{65,33},{66,34},{67,35},{68,36},{69,37},{70,38},{71,39},{7... | collective-permute-start | bytes 393224 | tf_op jit(solution)/shard_map/ppermute | solution.py:410
  6.5 4.6 %collective-permute-start.3 = (bf16[512,128]{1,0:T(8,128)(2,1)S(1)}, bf16[512,128]{1,0:T(8,128)(2,1)S(1)}, u32[]{:S(2)}, u32[]{:S(2)}) collective-permute-start(bf16[512,128]{1,0:T(8,128)(2,1)S(1)} %get-tuple-element.87), channel_id=1, source_target_pairs={{64,32},{65,33},{66,34},{67,35},{68,36},{69,37},{70,38},{71,39},{7... | collective-permute-start | bytes 393224 | tf_op jit(solution)/shard_map/ppermute | solution.py:410
  7.2 5.2 %collective-permute-start.10 = (bf16[512,128]{1,0:T(8,128)(2,1)S(1)}, bf16[512,128]{1,0:T(8,128)(2,1)S(1)}, u32[]{:S(2)}, u32[]{:S(2)}) collective-permute-start(bf16[512,128]{1,0:T(8,128)(2,1)S(1)} %get-tuple-element.102), channel_id=1, source_target_pairs={{64,32},{65,33},{66,34},{67,35},{68,36},{69,37},{70,38},{71,39},{7... | collective-permute-start | bytes 393224 | tf_op jit(solution)/shard_map/ppermute | solution.py:410
  7.9 13.0 %collective-permute-start.9 = (bf16[512,128]{1,0:T(8,128)(2,1)S(1)}, bf16[512,128]{1,0:T(8,128)(2,1)S(1)}, u32[]{:S(2)}, u32[]{:S(2)}) collective-permute-start(bf16[512,128]{1,0:T(8,128)(2,1)S(1)} %get-tuple-element.101), channel_id=1, source_target_pairs={{32,0},{33,1},{34,2},{35,3},{36,4},{37,5},{38,6},{39,7},{40,8},{41... | collective-permute-start | bytes 393224 | tf_op jit(solution)/shard_map/ppermute | solution.py:410
  9.4 16.6 %collective-permute-start.8 = (bf16[512,128]{1,0:T(8,128)(2,1)S(1)}, bf16[512,128]{1,0:T(8,128)(2,1)S(1)}, u32[]{:S(2)}, u32[]{:S(2)}) collective-permute-start(bf16[512,128]{1,0:T(8,128)(2,1)S(1)} %get-tuple-element.100), channel_id=1, source_target_pairs={{32,0},{33,1},{34,2},{35,3},{36,4},{37,5},{38,6},{39,7},{40,8},{41... | collective-permute-start | bytes 393224 | tf_op jit(solution)/shard_map/ppermute | solution.py:410
  11.1 17.6 %collective-permute-start.7 = (bf16[512,128]{1,0:T(8,128)(2,1)S(1)}, bf16[512,128]{1,0:T(8,128)(2,1)S(1)}, u32[]{:S(2)}, u32[]{:S(2)}) collective-permute-start(bf16[512,128]{1,0:T(8,128)(2,1)S(1)} %get-tuple-element.99), channel_id=1, source_target_pairs={{32,0},{33,1},{34,2},{35,3},{36,4},{37,5},{38,6},{39,7},{40,8},{41... | collective-permute-start | bytes 393224 | tf_op jit(solution)/shard_map/ppermute | solution.py:410
  12.4 19.6 %collective-permute-start.11 = (bf16[512,128]{1,0:T(8,128)(2,1)S(1)}, bf16[512,128]{1,0:T(8,128)(2,1)S(1)}, u32[]{:S(2)}, u32[]{:S(2)}) collective-permute-start(bf16[512,128]{1,0:T(8,128)(2,1)S(1)} %get-tuple-element.112), channel_id=1, source_target_pairs={{32,0},{33,1},{34,2},{35,3},{36,4},{37,5},{38,6},{39,7},{40,8},{41... | collective-permute-start | bytes 393224 | tf_op jit(solution)/shard_map/ppermute | solution.py:410
  35.0 3.3 %collective-permute-start.12 = (bf16[192,1152]{1,0:T(8,128)(2,1)}, bf16[192,1152]{1,0:T(8,128)(2,1)}, u32[]{:S(2)}, u32[]{:S(2)}) collective-permute-start(bf16[192,1152]{1,0:T(8,128)(2,1)} %get-tuple-element.117), channel_id=1, source_target_pairs={{0,1},{1,0},{2,3},{3,2},{4,5},{5,4},{6,7},{7,6},{8,9},{9,8},{10,11... | collective-permute-start | bytes 1327112 | tf_op jit(solution)/shard_map/ppermute | solution.py:374
  39.7 8.5 %collective-permute-start.13 = (bf16[48,1152]{1,0:T(8,128)(2,1)S(1)}, bf16[48,1152]{1,0:T(8,128)(2,1)S(1)}, u32[]{:S(2)}, u32[]{:S(2)}) collective-permute-start(bf16[48,1152]{1,0:T(8,128)(2,1)S(1)} %get-tuple-element.134), channel_id=1, source_target_pairs={{0,8},{1,9},{2,10},{3,11},{4,12},{5,13},{6,14},{7,15},{8,0},{9,1},... | collective-permute-start | bytes 331784 | tf_op jit(solution)/shard_map/ppermute | solution.py:374
  41.1 8.1 %collective-permute-start.14 = (bf16[48,1152]{1,0:T(8,128)(2,1)S(1)}, bf16[48,1152]{1,0:T(8,128)(2,1)S(1)}, u32[]{:S(2)}, u32[]{:S(2)}) collective-permute-start(bf16[48,1152]{1,0:T(8,128)(2,1)S(1)} %get-tuple-element.136), channel_id=1, source_target_pairs={{0,16},{1,17},{2,18},{3,19},{4,20},{5,21},{6,22},{7,23},{8,24},{9,... | collective-permute-start | bytes 331784 | tf_op jit(solution)/shard_map/ppermute | solution.py:374
  43.7 8.0 %collective-permute-start.15 = (bf16[48,1152]{1,0:T(8,128)(2,1)S(1)}, bf16[48,1152]{1,0:T(8,128)(2,1)S(1)}, u32[]{:S(2)}, u32[]{:S(2)}) collective-permute-start(bf16[48,1152]{1,0:T(8,128)(2,1)S(1)} %get-tuple-element.135), channel_id=1, source_target_pairs={{0,24},{1,25},{2,26},{3,27},{4,28},{5,29},{6,30},{7,31},{8,16},{9,... | collective-permute-start | bytes 331784 | tf_op jit(solution)/shard_map/ppermute | solution.py:374
  43.7 17.0 %collective-permute-start.16 = (bf16[2,512,128]{2,1,0:T(8,128)(2,1)}, bf16[2,512,128]{2,1,0:T(8,128)(2,1)S(1)}, u32[]{:S(2)}, u32[]{:S(2)}) collective-permute-start(bf16[2,512,128]{2,1,0:T(8,128)(2,1)} %copy-done.3), channel_id=1, source_target_pairs={{0,3},{1,4},{2,5},{3,6},{4,7},{5,8},{6,9},{7,10},{8,11},{9,12},{10... | collective-permute-start | bytes 786440 | tf_op jit(solution)/shard_map/ppermute | solution.py:379
  60.7 4.8 %collective-permute-start.17 = (bf16[48,1152]{1,0:T(8,128)(2,1)S(1)}, bf16[48,1152]{1,0:T(8,128)(2,1)S(1)}, u32[]{:S(2)}, u32[]{:S(2)}) collective-permute-start(bf16[48,1152]{1,0:T(8,128)(2,1)S(1)} %fusion.2), channel_id=1, source_target_pairs={{0,2},{1,3},{2,0},{3,1},{4,6},{5,7},{6,4},{7,5},{8,10},{9,11},{10,... | collective-permute-start | bytes 331784 | tf_op jit(solution)/shard_map/ppermute | solution.py:374
  60.7 5.1 %collective-permute-start.18 = (bf16[48,1152]{1,0:T(8,128)(2,1)S(1)}, bf16[48,1152]{1,0:T(8,128)(2,1)S(1)}, u32[]{:S(2)}, u32[]{:S(2)}) collective-permute-start(bf16[48,1152]{1,0:T(8,128)(2,1)S(1)} %fusion.2), channel_id=1, source_target_pairs={{0,4},{1,5},{2,6},{3,7},{4,0},{5,1},{6,2},{7,3},{8,12},{9,13},{10,... | collective-permute-start | bytes 331784 | tf_op jit(solution)/shard_map/ppermute | solution.py:374
  60.7 8.6 %collective-permute-start.19 = (bf16[48,1152]{1,0:T(8,128)(2,1)S(1)}, bf16[48,1152]{1,0:T(8,128)(2,1)S(1)}, u32[]{:S(2)}, u32[]{:S(2)}) collective-permute-start(bf16[48,1152]{1,0:T(8,128)(2,1)S(1)} %fusion.2), channel_id=1, source_target_pairs={{0,6},{1,7},{2,4},{3,5},{4,2},{5,3},{6,0},{7,1},{8,14},{9,15},{10,... | collective-permute-start | bytes 331784 | tf_op jit(solution)/shard_map/ppermute | solution.py:374
  69.5 10.4 %collective-permute-start.23 = (bf16[2,512,128]{2,1,0:T(8,128)(2,1)S(1)}, bf16[2,512,128]{2,1,0:T(8,128)(2,1)S(1)}, u32[]{:S(2)}, u32[]{:S(2)}) collective-permute-start(bf16[2,512,128]{2,1,0:T(8,128)(2,1)S(1)} %copy-done.2), channel_id=1, source_target_pairs={{0,1},{1,2},{2,3},{3,4},{4,5},{5,6},{6,7},{7,8},{8,9},{9,10},{10,1... | collective-permute-start | bytes 786440 | tf_op jit(solution)/shard_map/ppermute | solution.py:379
  70.4 17.4 %collective-permute-start.24 = (bf16[2,512,128]{2,1,0:T(8,128)(2,1)S(1)}, bf16[2,512,128]{2,1,0:T(8,128)(2,1)S(1)}, u32[]{:S(2)}, u32[]{:S(2)}) collective-permute-start(bf16[2,512,128]{2,1,0:T(8,128)(2,1)S(1)} %get-tuple-element.127), channel_id=1, source_target_pairs={{0,2},{1,3},{2,4},{3,5},{4,6},{5,7},{6,8},{7,9},{8,10},{9,11},{10,... | collective-permute-start | bytes 786440 | tf_op jit(solution)/shard_map/ppermute | solution.py:379
  71.0 4.7 %collective-permute-start.20 = (bf16[48,1152]{1,0:T(8,128)(2,1)S(1)}, bf16[48,1152]{1,0:T(8,128)(2,1)S(1)}, u32[]{:S(2)}, u32[]{:S(2)}) collective-permute-start(bf16[48,1152]{1,0:T(8,128)(2,1)S(1)} %add_convert_fusion.1), channel_id=1, source_target_pairs={{0,8},{1,9},{2,10},{3,11},{4,12},{5,13},{6,14},{7,15},{8,0},{9,1},... | collective-permute-start | bytes 331784 | tf_op jit(solution)/shard_map/ppermute | solution.py:374
  71.0 6.2 %collective-permute-start.21 = (bf16[48,1152]{1,0:T(8,128)(2,1)S(1)}, bf16[48,1152]{1,0:T(8,128)(2,1)S(1)}, u32[]{:S(2)}, u32[]{:S(2)}) collective-permute-start(bf16[48,1152]{1,0:T(8,128)(2,1)S(1)} %add_convert_fusion.1), channel_id=1, source_target_pairs={{0,16},{1,17},{2,18},{3,19},{4,20},{5,21},{6,22},{7,23},{8,24},{9,... | collective-permute-start | bytes 331784 | tf_op jit(solution)/shard_map/ppermute | solution.py:374
  71.0 8.9 %collective-permute-start.22 = (bf16[48,1152]{1,0:T(8,128)(2,1)S(1)}, bf16[48,1152]{1,0:T(8,128)(2,1)S(1)}, u32[]{:S(2)}, u32[]{:S(2)}) collective-permute-start(bf16[48,1152]{1,0:T(8,128)(2,1)S(1)} %add_convert_fusion.1), channel_id=1, source_target_pairs={{0,24},{1,25},{2,26},{3,27},{4,28},{5,29},{6,30},{7,31},{8,16},{9,... | collective-permute-start | bytes 331784 | tf_op jit(solution)/shard_map/ppermute | solution.py:374
  (7 other events, 44.5 us)

commit v3 on v2

--- a/solution.py
+++ b/solution.py
@@ -12,7 +12,6 @@
 VOX = 512
 TAPS = 27
 WORK = 4
-LAG = 4
 F32 = jnp.float32
 BF16 = jnp.bfloat16
 ANY = pl.BlockSpec(memory_space=pl.ANY)
@@ -80,24 +79,21 @@
     return gin.astype(BF16)
 
 
-def position(slot):
-    late = lax.axis_size("section") - 1 - lax.axis_index("section")
-    index = slot - LAG * late
-    return (index >= 0) & (index < WORK), jnp.clip(index, 0, WORK - 1)
-
-
-def first_kernel(
-    c_hbm, p_hbm, sup_hbm, w_hbm, gin_ref, gins, deltas, wn, p_ref, sup_ref, shares, pd, w_ref, counts, sems
-):
-    active, _ = position(0)
-    rest = pl.ds(1, WORK - 1)
+def working(slot):
+    return lax.axis_size("section") - 1 - lax.axis_index("section") == slot // WORK
+
+
+def first_kernel(c_hbm, p_hbm, sup_hbm, w_hbm, gin, deltas, gins, wn, p_ref, sup_ref, shares, *rest):
+    pd, w_ref, counts, sems = rest
+    active = working(0)
+    later = pl.ds(1, WORK - 1)
     copies = [
-        pltpu.make_async_copy(c_hbm, counts, sems.at[5]),
-        pltpu.make_async_copy(p_hbm.at[0], p_ref.at[0], sems.at[0]),
-        pltpu.make_async_copy(sup_hbm.at[0], sup_ref.at[0], sems.at[1]),
-        pltpu.make_async_copy(w_hbm, w_ref, sems.at[2]),
-        pltpu.make_async_copy(p_hbm.at[rest], p_ref.at[rest], sems.at[3]),
-        pltpu.make_async_copy(sup_hbm.at[rest], sup_ref.at[rest], sems.at[4]),
+        pltpu.make_async_copy(c_hbm, counts, sems.at[0]),
+        pltpu.make_async_copy(p_hbm.at[0], p_ref.at[0], sems.at[1]),
+        pltpu.make_async_copy(sup_hbm.at[0], sup_ref.at[0], sems.at[2]),
+        pltpu.make_async_copy(w_hbm, w_ref, sems.at[3]),
+        pltpu.make_async_copy(p_hbm.at[later], p_ref.at[later], sems.at[4]),
+        pltpu.make_async_copy(sup_hbm.at[later], sup_ref.at[later], sems.at[5]),
     ]
     for copy in copies:
         copy.start()
@@ -123,9 +119,8 @@
 
     @pl.when(active)
     def _():
-        gin = input_grad(pd[...], wn[...])
-        gin_ref[...] = gin
-        gins[0] = gin
+        gin[...] = input_grad(pd[...], wn[...])
+        gins[0] = gin[...]
 
     copies[4].wait()
     copies[5].wait()
@@ -133,13 +128,13 @@
 
 def first_step(counts, preacts, sup, weights):
     hbm = lambda x: pltpu.with_memory_space_constraint(x, pltpu.MemorySpace.HBM)
-    bricks = pltpu.VMEM((WORK, VOX, C), BF16)
+    block, bricks = pltpu.VMEM((VOX, C), BF16), pltpu.VMEM((WORK, VOX, C), BF16)
     return pl.pallas_call(
         first_kernel,
         in_specs=[ANY] * 4,
         out_specs=[VM] * 7,
         out_shape=[
-            shape((VOX, C)),
+            block,
             bricks,
             bricks,
             pltpu.VMEM((3 * C, 9 * C), BF16),
@@ -158,36 +153,39 @@
     )(hbm(counts), hbm(preacts), hbm(sup), hbm(weights))
 
 
-def tick_kernel(slot, sends, shares, p_ref, sup_ref, above_ref, wn, gins_in, deltas_in, *outs):
-    gins, deltas, pd = outs[0], outs[1], outs[-1]
-    active, brick = position(slot)
-
-    @pl.when(active)
-    def _():
-        delta = deltas_of(shares[brick], p_ref[brick], sup_ref[brick], above_ref[...])
+def tick_kernel(slot, shares, p_ref, sup_ref, wn, *rest):
+    deltas, gins, gin, pd = rest[-4:]
+    zero = jnp.zeros((VOX, C), BF16)
+    brick = slot % WORK
+
+    @pl.when(working(slot))
+    def _():
+        above = zero if slot < WORK else rest[2][...]
+        delta = deltas_of(shares[brick], p_ref[brick], sup_ref[brick], above)
         deltas[brick] = delta.astype(BF16)
         spread(delta, pd)
-        gin = input_grad(pd[...], wn[...])
-        gins[brick] = gin
-        if sends:
-            outs[2][...] = gin
-
-
-def tick_step(slot, sends, shares, preacts, sup, above, wn, gins, deltas):
-    bricks = pltpu.VMEM((WORK, VOX, C), BF16)
-    return pl.pallas_call(
-        functools.partial(tick_kernel, slot, sends),
-        in_specs=[VM] * 7,
-        out_specs=[VM] * (2 + sends),
-        out_shape=[bricks, bricks] + [shape((VOX, C))] * sends,
+        gin[...] = input_grad(pd[...], wn[...])
+        gins[brick] = gin[...]
+
+    if slot // WORK == lax.axis_size("section") - 1:
+        @pl.when(jnp.logical_not(working(slot)))
+        def _():
+            gin[...] = gins[brick]
+
+
+def tick_step(slot, shares, preacts, sup, wn, deltas, gins, above):
+    block, bricks = pltpu.VMEM((VOX, C), BF16), pltpu.VMEM((WORK, VOX, C), BF16)
+    return pl.pallas_call(
+        functools.partial(tick_kernel, slot),
+        in_specs=[VM] * (6 + len(above)),
+        out_specs=[VM] * 3,
+        out_shape=[bricks, bricks, block],
         scratch_shapes=[pltpu.VMEM((VOX, 9 * C), BF16)],
-        input_output_aliases={5: 0, 6: 1},
-        compiler_params=params(),
-        cost_estimate=pl.CostEstimate(
-            flops=2 * VOX * TAPS * C * C, bytes_accessed=2 << 20, transcendentals=VOX * C
-        ),
+        input_output_aliases={4: 0, 5: 1},
+        compiler_params=params(),
+        cost_estimate=pl.CostEstimate(flops=1, bytes_accessed=1 << 18, transcendentals=0),
         name="tick%d" % slot,
-    )(vmem(shares), vmem(preacts), vmem(sup), above, vmem(wn), vmem(gins), vmem(deltas))
+    )(vmem(shares), vmem(preacts), vmem(sup), vmem(wn), vmem(deltas), vmem(gins), *above)
 
 
 def transpose_kernel(x_ref, out):
@@ -225,17 +223,14 @@
         out_shape=shape((3 * C, 9 * C), F32),
         scratch_shapes=[pltpu.VMEM((2, VOX, 9 * C), BF16)],
         compiler_params=params(),
-        cost_estimate=pl.CostEstimate(
-            flops=4 * VOX * TAPS * C * C, bytes_accessed=4 << 20, transcendentals=0
-        ),
+        cost_estimate=pl.CostEstimate(flops=1, bytes_accessed=1 << 18, transcendentals=0),
         name="weight_terms_early",
-    )(deltas, xt)
-
-
-def late_kernel(
-    slot, shares, p_ref, sup_ref, above_ref, deltas, xt, acc_in, keep_ref, send_ref, pd, pd_2, acc
-):
-    active, _ = position(slot)
+    )(vmem(deltas), xt)
+
+
+def late_kernel(slot, shares, p_ref, sup_ref, above_ref, deltas, xt, acc_in, *rest):
+    keep, send, (pd, pd_2, acc) = rest[:4], rest[4:8], rest[8:]
+    active = working(slot)
     last = WORK - 1
     spread(deltas[last - 1].astype(F32), pd_2)
     total = acc_in[...] + jnp.dot(xt[last - 1], pd_2[...], preferred_element_type=F32)
@@ -249,19 +244,22 @@
         spread(deltas[last].astype(F32), pd)
 
     acc[...] = total + jnp.dot(xt[last], pd[...], preferred_element_type=F32)
-    core = lax.rem(lax.axis_index("brick"), 2)
-    mine = pl.multiple_of(core * 192, 16)
-    other = pl.multiple_of(192 - core * 192, 16)
-    send_ref[...] = acc[pl.ds(other, 192), :].astype(BF16)
-    keep_ref[...] = acc[pl.ds(mine, 192), :].astype(BF16)
+    me = lax.axis_index("brick")
+    core, y = lax.rem(me, 2), lax.div(me, 8)
+    for k in range(4):
+        row = lax.bitwise_xor(y, k) * 48
+        mine = pl.multiple_of(core * 192 + row, 16)
+        other = pl.multiple_of((1 - core) * 192 + row, 16)
+        send[k][...] = acc[pl.ds(other, 48), :].astype(BF16)
+        keep[k][...] = acc[pl.ds(mine, 48), :].astype(BF16)
 
 
 def late_step(slot, shares, preacts, sup, above, deltas, xt, acc):
     return pl.pallas_call(
         functools.partial(late_kernel, slot),
         in_specs=[VM] * 7,
-        out_specs=[VM] * 3,
-        out_shape=[shape((192, 9 * C))] * 2 + [shape((VOX, 9 * C))],
+        out_specs=[VM] * 9,
+        out_shape=[shape((48, 9 * C))] * 8 + [shape((VOX, 9 * C))],
         scratch_shapes=[pltpu.VMEM((VOX, 9 * C), BF16), pltpu.VMEM((3 * C, 9 * C), F32)],
         compiler_params=params(),
         cost_estimate=pl.CostEstimate(
@@ -271,46 +269,76 @@
     )(vmem(shares), vmem(preacts), vmem(sup), above, vmem(deltas), xt, acc)
 
 
-def pack_kernel(slot, pick, gins, pd, wn, local, *sent):
-    active, _ = position(slot)
-    zero = jnp.zeros((VOX, C), BF16)
-    outs = (local,) + sent
-
-    def put(micro, first, second):
-        for d in range(4):
-            which = pick[micro, d]
-            outs[d][micro] = jnp.where(which == 0, first, jnp.where(which == 1, second, zero))
-
-    put(0, gins[0], gins[1])
+def choose(trainer, micro, owner, offset, first, second):
+    peers = trainer.shape[1] // 2
+    to = lax.rem(owner + offset, peers)
+    first = jnp.where(trainer[micro, 2 * owner] == to, first, jnp.zeros_like(first))
+    return jnp.where(trainer[micro, 2 * owner + 1] == to, second, first)
+
+
+def last_kernel(slot, trainer, gins, pd, wn, gin, stays, leaves):
+    active = working(slot)
 
     @pl.when(active)
     def _():
-        put(1, gins[2], input_grad(pd[...], wn[...]))
+        gin[...] = input_grad(pd[...], wn[...])
 
     @pl.when(jnp.logical_not(active))
     def _():
-        put(1, gins[2], gins[3])
-
-
-def pack_step(slot, pick, gins, pd, wn):
-    return pl.pallas_call(
-        functools.partial(pack_kernel, slot),
+        gin[...] = gins[WORK - 1]
+
+    me = lax.axis_index("brick")
+    core = lax.rem(me, 2)
+    for micro in range(2):
+        first, second = gins.at[2 * micro], gins.at[1] if micro == 0 else gin
+        stays[micro] = choose(trainer, micro, me, 0, first[...], second[...])
+        leaves[micro] = choose(trainer, micro, me, 1 + 2 * core, first[...], second[...])
+
+
+def last_step(slot, trainer, gins, pd, wn):
+    return pl.pallas_call(
+        functools.partial(last_kernel, slot),
         in_specs=[SM] + [VM] * 3,
-        out_specs=[VM] * 4,
-        out_shape=[shape((2, VOX, C))] * 4,
+        out_specs=[VM] * 3,
+        out_shape=[shape((VOX, C)), shape((2, VOX, C)), shape((2, VOX, C))],
         compiler_params=params(),
         cost_estimate=pl.CostEstimate(
             flops=2 * VOX * TAPS * C * C, bytes_accessed=4 << 20, transcendentals=0
         ),
-        name="pack",
-    )(pick, vmem(gins), pd, vmem(wn))
-
-
-def slots_kernel(*refs):
-    blocks, out, sems = refs[:4], refs[4], refs[5]
+        name="last_grad",
+    )(trainer, vmem(gins), pd, vmem(wn))
+
+
+def sort_kernel(trainer, *refs):
+    came, keeps, passes = refs[:4], refs[4], refs[5]
+    me = lax.axis_index("brick")
+    core = lax.rem(me, 2)
+    peers = trainer.shape[1] // 2
+    owner = lax.rem(me + peers - 2, peers)
+    for micro in range(2):
+        first, second = came[2 * micro][...], came[2 * micro + 1][...]
+        keeps[micro] = choose(trainer, micro, owner, 2, first, second)
+        passes[micro] = choose(trainer, micro, owner, 3 - 2 * core, first, second)
+
+
+def sort_step(trainer, came):
+    return pl.pallas_call(
+        sort_kernel,
+        in_specs=[SM] + [VM] * 4,
+        out_specs=[VM] * 2,
+        out_shape=[shape((2, VOX, C))] * 2,
+        compiler_params=params(),
+        name="sort_slots",
+    )(trainer, *came)
+
+
+def slots_kernel(stays, keeps, passed, arrived, out, sems):
+    core = lax.rem(lax.axis_index("brick"), 2)
     copies = [
-        pltpu.make_async_copy(block.at[micro], out.at[micro, d], sems.at[d, micro])
-        for d, block in enumerate(blocks)
+        pltpu.make_async_copy(block.at[micro], out.at[micro, d], sems.at[i, micro])
+        for i, (block, d) in enumerate(
+            ((stays, 0), (keeps, 2), (passed, 1 + 2 * core), (arrived, 3 - 2 * core))
+        )
         for micro in range(2)
     ]
     for copy in copies:
@@ -319,7 +347,7 @@
         copy.wait()
 
 
-def slots_step(blocks):
+def slots_step(*blocks):
     return pl.pallas_call(
         slots_kernel,
         in_specs=[VM] * 4,
@@ -384,54 +412,54 @@
     me = lax.axis_index("brick")
     layers = lax.axis_size("section")
     micros, own = saved_inputs.shape[1:3]
-    slots = WORK + LAG * (layers - 1)
+    slots = WORK * layers
 
     inputs = saved_inputs.reshape(WORK, VOX, C)
     preacts = saved_preacts.reshape(WORK, VOX, C)
     sup = supervision.reshape(WORK, VOX, C)
-    targets = lax.dynamic_slice_in_dim(trainer, me * own, own, 1)
-    offsets = jnp.mod(targets - me, peers)
-    match = offsets[:, :, None] == jnp.arange(4, dtype=jnp.int32)[None, None, :]
-    brick = jnp.arange(own, dtype=jnp.int32)
-    pick = jnp.max(jnp.where(match, brick[None, :, None], -1), axis=1).astype(jnp.int32)
-
-    above = {}
-    gin, gins, deltas, wn, preacts, sup, shares = first_step(counts, preacts, sup, weights[0])
-    zero = jnp.zeros((VOX, C), BF16)
+    above, came = {}, []
+    gin, deltas, gins, wn, preacts, sup, shares = first_step(counts, preacts, sup, weights[0])
     xt = transpose_step(inputs)
     for slot in range(slots - 1):
-        senders = [s for s in range(1, layers) if 0 <= slot - LAG * (layers - 1 - s) < WORK]
         if slot > 0:
-            gins, deltas, *sent = tick_step(
-                slot, len(senders) > 0, shares, preacts, sup, above.get(slot, zero), wn, gins, deltas
+            arrived = [above[slot]] if slot >= WORK else []
+            deltas, gins, gin = tick_step(
+                slot, shares, preacts, sup, wn, deltas, gins, arrived
             )
-            gin = sent[0] if sent else None
-        if senders:
-            above[slot + LAG] = lax.ppermute(gin, "section", [(s, s - 1) for s in senders])
+        sender = layers - 1 - slot // WORK
+        if sender > 0:
+            above[slot + WORK] = lax.ppermute(gin, "section", [(sender, sender - 1)])
+        else:
+            came.append(shifted(gin, 2))
         if slot == slots - 3:
             acc = early_step(deltas, xt)
     last = slots - 1
-    keep, send, pd = late_step(last, shares, preacts, sup, above[last], deltas, xt, acc)
-    from_core = swap(send, 1)
-    local, send_1, send_2, send_3 = pack_step(last, pick, gins, pd, wn)
-    from_3 = shifted(send_3, 3)
-    from_core, send_1, send_2 = lax.optimization_barrier((from_core, send_1, send_2))
-
-    half = (keep.astype(F32) + from_core.astype(F32)).astype(BF16).reshape(4, 48, 9 * C)
-    y = me // 8
-    part = [lax.dynamic_index_in_dim(half, lax.bitwise_xor(y, k), 0, False) for k in range(4)]
-    total = part[0].astype(F32)
-    for k, bits in enumerate(Y_BITS):
-        total = total + swap(part[k + 1], bits).astype(F32)
-    total, from_3 = lax.optimization_barrier((total.astype(BF16), from_3))
+    *halves, pd = late_step(last, shares, preacts, sup, above[last], deltas, xt, acc)
+    keep, send = halves[:4], halves[4:]
+    send, came[0] = lax.optimization_barrier([send, came[0]])
+    from_core = [swap(block, 1) for block in send]
+    gin, stays, leaves = last_step(last, trainer, gins, pd, wn)
+    from_core, gin, leaves, came[1] = lax.optimization_barrier([from_core, gin, leaves, came[1]])
+    came.append(shifted(gin, 2))
+    across = [(i, (i + 1 + 2 * (i % 2)) % peers) for i in range(peers)]
+    arrived = lax.ppermute(leaves, "brick", across)
+
+    part = [mine.astype(F32) + theirs.astype(F32) for mine, theirs in zip(keep, from_core)]
+    total = part[0]
+    for block, bits in zip(part[1:], Y_BITS):
+        total = total + swap(block.astype(BF16), bits).astype(F32)
+    total = total.astype(BF16)
+    keeps, passes = sort_step(trainer, came)
+    passed = swap(passes, 1)
+    total, passed = lax.optimization_barrier([total, passed])
     full = total.astype(F32)
     for bits in Z_BITS:
         full = full + swap(total, bits).astype(F32)
-    full, send_1, send_2 = lax.optimization_barrier((full.astype(BF16), send_1, send_2))
-    got = [swap(full, bits) for bits in Y_BITS] + [shifted(send_1, 1), shifted(send_2, 2)]
-    *got, from_1, from_2 = lax.optimization_barrier(got)
-    blocks = [local, from_1, from_2, from_3]
-    skip_grads = slots_step(blocks).reshape((1, micros, 4) + saved_inputs.shape[3:])
+    full = full.astype(BF16)
+    got = [swap(full, bits) for bits in Y_BITS]
+    got, arrived = lax.optimization_barrier([got, arrived])
+    skip_grads = slots_step(stays, keeps, passed, arrived)
+    skip_grads = skip_grads.reshape((1, micros, 4) + saved_inputs.shape[3:])
     mine = jnp.stack([full] + got)
     other = swap(mine, 1)
     scale = 1.0 / math.sqrt(WORK * peers * VOX)

time: 91.5 us -> 81.3 us (0.89)
  waiting for transfers between devices: 45.1 us -> 28 us
  starting transfers between devices: 29.9 us -> 38.8 us
  other arithmetic: 1.66 us -> 0.3 us
    ppermute x3 -> x4, waiting for transfers between devices: 16.9 us -> 8.99 us  [shifted(): lax.ppermute(block, 'brick', [(i, (i + distance) % n) for i in range(n)])]
    ppermute x11 -> x15, starting transfers between devices: 13.3 us -> 21.2 us  [swap(): return lax.ppermute(block, 'brick', pairs)]
    ppermute x11 -> x15, waiting for transfers between devices: 14.2 us -> 8.69 us  [swap(): return lax.ppermute(block, 'brick', pairs)]
    ppermute x12 -> x13, waiting for transfers between devices: 14 us -> 10.3 us  [the longest x12 10.3 us: shards(): above[slot + WORK] = lax.ppermute(gin, 'section', [(sender, sender - 1)])]
    ppermute x12 -> x13, starting transfers between devices: 10.7 us -> 12.1 us  [the longest x12 10.7 us: shards(): above[slot + WORK] = lax.ppermute(gin, 'section', [(sender, sender - 1)])]
    convert_element_type x3 -> x5, other arithmetic: 1.42 us -> 0.23 us  [the longest x3 0.09 us: shards(): total = total + swap(block.astype(BF16), bits).astype(F32)]
    pallas_call x1, Pallas kernels: 3.03 us -> 1.99 us  [late_step(): pl.pallas_call(functools.partial(late_kernel, slot), in_specs=[VM] * 7, o...]
    pallas_call x15 -> x16, Pallas kernels: 4.7 us -> 5.21 us  [the longest x14 2.98 us: tick_step(): pl.pallas_call(functools.partial(tick_kernel, slot), in_specs=[VM] * (6 +...]
  transfers between devices with their start and end apart: 26 -> 32, of which waited for: 15 -> 10; matrix products, arithmetic and copies ran while one was open for 0% -> 0% of each run, Pallas kernels for 8% -> 12%
where the time goes in v3:
time: 81.3 us; the launch traced here: 81 us
  starting transfers between devices  38.8 us (48%)
  waiting for transfers between devices  28 us (34%)
  Pallas kernels  12.7 us (16%)
  between operations  1.21 us (1%)
    ppermute x15, starting transfers between devices, swap(): return lax.ppermute(block, 'brick', pairs)  21.2 us
    ppermute x12, starting transfers between devices, shards(): above[slot + WORK] = lax.ppermute(gin, 'section', [(sender, sender - 1)])  10.7 us
    ppermute x12, waiting for transfers between devices, shards(): above[slot + WORK] = lax.ppermute(gin, 'section', [(sender, sender - 1)])  10.3 us
    ppermute x4, waiting for transfers between devices, shifted(): lax.ppermute(block, 'brick', [(i, (i + distance) % n) for i in range(n)])  8.99 us
    ppermute x15, waiting for transfers between devices, swap(): return lax.ppermute(block, 'brick', pairs)  8.69 us
    ppermute x4, starting transfers between devices, shifted(): lax.ppermute(block, 'brick', [(i, (i + distance) % n) for i in range(n)])  5.53 us
    pallas_call x14, Pallas kernels, tick_step(): pl.pallas_call(functools.partial(tick_kernel, slot), in_specs=[VM] * (6 +...  2.98 us
    pallas_call x1, Pallas kernels, late_step(): pl.pallas_call(functools.partial(late_kernel, slot), in_specs=[VM] * 7, o...  1.99 us
  transfers between devices with their start and end apart: 32, of which 10 were waited for; matrix products, arithmetic and copies ran while one was open for 0% of the time, Pallas kernels for 12%

profile of v3, /device:TPU:1, one launch (start us, length us, event | category | flops | bytes accessed | tf_op | source)
XLA Modules:
  0.0 81.0 jit_solution(16261783931484403102)
XLA Ops:
  0.6 1.6 %tick_first.1 = (bf16[512,128]{1,0:T(8,128)(2,1)S(1)}, bf16[4,512,128]{2,1,0:T(8,128)(2,1)S(1)}, bf16[4,512,128]{2,1,0:T(8,128)(2,1)S(1)}, bf16[384,1152]{1,0:T(...) custom-call(s32[2,2]{1,0:T(2,128)} %c_hbm.1, ...), custom_call_target="tpu_custom_call" | custom-call | tf_op jit(solution)/shard_map/tick_first/pallas_call | solution.py:132
  7.9 1.3 %collective-permute-start.8 = (bf16[512,128]{1,0:T(8,128)(2,1)S(1)}, bf16[512,128]{1,0:T(8,128)(2,1)S(1)}, u32[]{:S(2)}, u32[]{:S(2)}) collective-permute-start(bf16[512,128]{1,0:T(8,128)(2,1)S(1)} %get-tuple-element.119), channel_id=1, source_target_pairs={{32,0},{33,1},{34,2},{35,3},{36,4},{37,5},{38,6},{39,7},{40,8},{41... | collective-permute-start | bytes 393224 | tf_op jit(solution)/shard_map/ppermute | solution.py:431
  9.2 1.3 %collective-permute-start.9 = (bf16[512,128]{1,0:T(8,128)(2,1)S(1)}, bf16[512,128]{1,0:T(8,128)(2,1)S(1)}, u32[]{:S(2)}, u32[]{:S(2)}) collective-permute-start(bf16[512,128]{1,0:T(8,128)(2,1)S(1)} %get-tuple-element.122), channel_id=1, source_target_pairs={{32,0},{33,1},{34,2},{35,3},{36,4},{37,5},{38,6},{39,7},{40,8},{41... | collective-permute-start | bytes 393224 | tf_op jit(solution)/shard_map/ppermute | solution.py:431
  10.6 1.3 %collective-permute-start.10 = (bf16[512,128]{1,0:T(8,128)(2,1)S(1)}, bf16[512,128]{1,0:T(8,128)(2,1)S(1)}, u32[]{:S(2)}, u32[]{:S(2)}) collective-permute-start(bf16[512,128]{1,0:T(8,128)(2,1)S(1)} %get-tuple-element.125), channel_id=1, source_target_pairs={{32,0},{33,1},{34,2},{35,3},{36,4},{37,5},{38,6},{39,7},{40,8},{41... | collective-permute-start | bytes 393224 | tf_op jit(solution)/shard_map/ppermute | solution.py:431
  11.9 1.4 %collective-permute-start.11 = (bf16[512,128]{1,0:T(8,128)(2,1)S(1)}, bf16[512,128]{1,0:T(8,128)(2,1)S(1)}, u32[]{:S(2)}, u32[]{:S(2)}) collective-permute-start(bf16[512,128]{1,0:T(8,128)(2,1)S(1)} %get-tuple-element.127), channel_id=1, source_target_pairs={{32,0},{33,1},{34,2},{35,3},{36,4},{37,5},{38,6},{39,7},{40,8},{41... | collective-permute-start | bytes 393224 | tf_op jit(solution)/shard_map/ppermute | solution.py:431
  13.3 7.5 %collective-permute-done.8.rest_2_ = bf16[512,128]{1,0:T(8,128)(2,1)S(1)} collective-permute-done((bf16[512,128]{1,0:T(8,128)(2,1)S(1)}, bf16[512,128]{1,0:T(8,128)(2,1)S(1)}, u32[]{:S(2)}, u32[]{:S(2)}) %collective-permute-start.8) | collective-permute-done | bytes 131104 | tf_op jit(solution)/shard_map/ppermute | solution.py:431
  21.8 1.7 %collective-permute-start.12 = (bf16[512,128]{1,0:T(8,128)(2,1)S(1)}, bf16[512,128]{1,0:T(8,128)(2,1)S(1)}, u32[]{:S(2)}, u32[]{:S(2)}) collective-permute-start(bf16[512,128]{1,0:T(8,128)(2,1)S(1)} %get-tuple-element.135), channel_id=1, source_target_pairs={{0,2},{1,3},{2,4},{3,5},{4,6},{5,7},{6,8},{7,9},{8,10},{9,11},{10,... | collective-permute-start | bytes 393224 | tf_op jit(solution)/shard_map/ppermute | solution.py:407
  23.8 1.9 %collective-permute-done.9.rest_2_ = bf16[512,128]{1,0:T(8,128)(2,1)S(1)} collective-permute-done((bf16[512,128]{1,0:T(8,128)(2,1)S(1)}, bf16[512,128]{1,0:T(8,128)(2,1)S(1)}, u32[]{:S(2)}, u32[]{:S(2)}) %collective-permute-start.9) | collective-permute-done | bytes 131104 | tf_op jit(solution)/shard_map/ppermute | solution.py:431
  26.7 1.9 %collective-permute-start.17 = (bf16[512,128]{1,0:T(8,128)(2,1)S(1)}, bf16[512,128]{1,0:T(8,128)(2,1)S(1)}, u32[]{:S(2)}, u32[]{:S(2)}) collective-permute-start(bf16[512,128]{1,0:T(8,128)(2,1)S(1)} %get-tuple-element.143), channel_id=1, source_target_pairs={{0,2},{1,3},{2,4},{3,5},{4,6},{5,7},{6,8},{7,9},{8,10},{9,11},{10,... | collective-permute-start | bytes 393224 | tf_op jit(solution)/shard_map/ppermute | solution.py:407
  28.5 1.3 %weight_terms_early.1.acc_in = f32[384,1152]{1,0:T(8,128)S(1)} custom-call(bf16[4,512,128]{2,1,0:T(8,128)(2,1)S(1)} %get-tuple-element.123.rest_0_.deltas, bf16[4,384,512]{2,1,0:T(8,128)(2,1)S(1)} %inputs_across.1.xt), custom_call_target="tpu_custom_call" | custom-call | flops 1 | bytes 262144 | tf_op jit(solution)/shard_map/weight_terms_early/pallas_call | solution.py:219
  31.7 2.0 %weight_terms.1 = (bf16[48,1152]{1,0:T(8,128)(2,1)S(1)}, bf16[48,1152]{1,0:T(8,128)(2,1)S(1)}, bf16[48,1152]{1,0:T(8,128)(2,1)S(1)}, bf16[48,1152]{1,0:T(8,128)(...) custom-call(f32[4,8,128]{2,1,0:T(8,128)S(1)} %get-tuple-element.83.s, ...), custom_call_target="tpu_custom_call" | custom-call | flops 905969664 | bytes 7340032 | tf_op jit(solution)/shard_map/weight_terms/pallas_call | solution.py:258
  33.7 3.9 %collective-permute-start.13 = (bf16[48,1152]{1,0:T(8,128)(2,1)S(1)}, bf16[48,1152]{1,0:T(8,128)(2,1)S(1)}, u32[]{:S(2)}, u32[]{:S(2)}) collective-permute-start(bf16[48,1152]{1,0:T(8,128)(2,1)S(1)} %get-tuple-element.137), channel_id=1, source_target_pairs={{0,1},{1,0},{2,3},{3,2},{4,5},{5,4},{6,7},{7,6},{8,9},{9,8},{10,11... | collective-permute-start | bytes 331784 | tf_op jit(solution)/shard_map/ppermute | solution.py:402
  38.1 1.5 %last_grad.1 = (bf16[512,128]{1,0:T(8,128)(2,1)S(1)}, bf16[2,512,128]{2,1,0:T(8,128)(2,1)S(1)}, bf16[2,512,128]{2,1,0:T(8,128)(2,1)S(1)}) custom-call(s32[2,64]{1,0:T(2,128)S(1)} %copy-done.1, bf16[4,512,128]{2,1,0:T(8,128)(2,1)S(1)} %get-tuple-element.126.gins, bf16[512,1152]{1,0:T(8,128)(2,1)S(1)} %get-tuple-element.129.pd, ...), custom_call_target="tpu_custom_call" | custom-call | flops 452984832 | bytes 4194304 | tf_op jit(solution)/shard_map/last_grad/pallas_call | solution.py:299
  40.5 1.4 %collective-permute-start.20 = (bf16[48,1152]{1,0:T(8,128)(2,1)S(1)}, bf16[48,1152]{1,0:T(8,128)(2,1)S(1)}, u32[]{:S(2)}, u32[]{:S(2)}) collective-permute-start(bf16[48,1152]{1,0:T(8,128)(2,1)S(1)} %add_convert_fusion.4), channel_id=1, source_target_pairs={{0,8},{1,9},{2,10},{3,11},{4,12},{5,13},{6,14},{7,15},{8,0},{9,1},... | collective-permute-start | bytes 331784 | tf_op jit(solution)/shard_map/ppermute | solution.py:402
  41.9 2.7 %collective-permute-start.21 = (bf16[48,1152]{1,0:T(8,128)(2,1)S(1)}, bf16[48,1152]{1,0:T(8,128)(2,1)S(1)}, u32[]{:S(2)}, u32[]{:S(2)}) collective-permute-start(bf16[48,1152]{1,0:T(8,128)(2,1)S(1)} %add_convert_fusion.3), channel_id=1, source_target_pairs={{0,16},{1,17},{2,18},{3,19},{4,20},{5,21},{6,22},{7,23},{8,24},{9,... | collective-permute-start | bytes 331784 | tf_op jit(solution)/shard_map/ppermute | solution.py:402
  45.9 1.7 %collective-permute-done.18.refs_2_ = bf16[512,128]{1,0:T(8,128)(2,1)S(1)} collective-permute-done((bf16[512,128]{1,0:T(8,128)(2,1)S(1)}, bf16[512,128]{1,0:T(8,128)(2,1)S(1)}, u32[]{:S(2)}, u32[]{:S(2)}) %collective-permute-start.18) | collective-permute-done | bytes 131104 | tf_op jit(solution)/shard_map/ppermute | solution.py:407
  47.6 7.3 %collective-permute-done.19.refs_3_ = bf16[512,128]{1,0:T(8,128)(2,1)S(1)} collective-permute-done((bf16[512,128]{1,0:T(8,128)(2,1)S(1)}, bf16[512,128]{1,0:T(8,128)(2,1)S(1)}, u32[]{:S(2)}, u32[]{:S(2)}) %collective-permute-start.19) | collective-permute-done | bytes 131104 | tf_op jit(solution)/shard_map/ppermute | solution.py:407
  55.6 2.3 %collective-permute-start.23 = (bf16[2,512,128]{2,1,0:T(8,128)(2,1)S(1)}, bf16[2,512,128]{2,1,0:T(8,128)(2,1)S(1)}, u32[]{:S(2)}, u32[]{:S(2)}) collective-permute-start(bf16[2,512,128]{2,1,0:T(8,128)(2,1)S(1)} %get-tuple-element.156), channel_id=1, source_target_pairs={{0,1},{1,0},{2,3},{3,2},{4,5},{5,4},{6,7},{7,6},{8,9},{9,8},{10,11... | collective-permute-start | bytes 786440 | tf_op jit(solution)/shard_map/ppermute | solution.py:402
  59.1 3.2 %collective-permute-start.24 = (bf16[48,1152]{1,0:T(8,128)(2,1)S(1)}, bf16[48,1152]{1,0:T(8,128)(2,1)S(1)}, u32[]{:S(2)}, u32[]{:S(2)}) collective-permute-start(bf16[48,1152]{1,0:T(8,128)(2,1)S(1)} %add_convert_fusion.1), channel_id=1, source_target_pairs={{0,2},{1,3},{2,0},{3,1},{4,6},{5,7},{6,4},{7,5},{8,10},{9,11},{10,... | collective-permute-start | bytes 331784 | tf_op jit(solution)/shard_map/ppermute | solution.py:402
  62.4 1.4 %collective-permute-start.30 = (bf16[2,512,128]{2,1,0:T(8,128)(2,1)S(1)}, bf16[2,512,128]{2,1,0:T(8,128)(2,1)S(1)}, u32[]{:S(2)}, u32[]{:S(2)}) collective-permute-start(bf16[2,512,128]{2,1,0:T(8,128)(2,1)S(1)} %get-tuple-element.159), channel_id=1, source_target_pairs={{0,1},{1,4},{2,3},{3,6},{4,5},{5,8},{6,7},{7,10},{8,9},{9,12},{10,... | collective-permute-start | bytes 786440 | tf_op jit(solution)/shard_map/ppermute | solution.py:445
  63.8 3.6 %collective-permute-done.26 = bf16[48,1152]{1,0:T(8,128)(2,1)S(1)} collective-permute-done((bf16[48,1152]{1,0:T(8,128)(2,1)S(1)}, bf16[48,1152]{1,0:T(8,128)(2,1)S(1)}, u32[]{:S(2)}, u32[]{:S(2)}) %collective-permute-start.26) | collective-permute-done | bytes 110624 | tf_op jit(solution)/shard_map/ppermute | solution.py:402
  68.2 2.6 %collective-permute-start.27 = (bf16[48,1152]{1,0:T(8,128)(2,1)S(1)}, bf16[48,1152]{1,0:T(8,128)(2,1)S(1)}, u32[]{:S(2)}, u32[]{:S(2)}) collective-permute-start(bf16[48,1152]{1,0:T(8,128)(2,1)S(1)} %add_convert_fusion), channel_id=1, source_target_pairs={{0,8},{1,9},{2,10},{3,11},{4,12},{5,13},{6,14},{7,15},{8,0},{9,1},... | collective-permute-start | bytes 331784 | tf_op jit(solution)/shard_map/ppermute | solution.py:402
  70.8 2.7 %collective-permute-done.29 = bf16[48,1152]{1,0:T(8,128)(2,1)S(1)} collective-permute-done((bf16[48,1152]{1,0:T(8,128)(2,1)S(1)}, bf16[48,1152]{1,0:T(8,128)(2,1)S(1)}, u32[]{:S(2)}, u32[]{:S(2)}) %collective-permute-start.29) | collective-permute-done | bytes 110624 | tf_op jit(solution)/shard_map/ppermute | solution.py:402
  74.5 3.7 %collective-permute-start.31 = (bf16[4,48,1152]{2,1,0:T(8,128)(2,1)S(1)}, bf16[4,48,1152]{2,1,0:T(8,128)(2,1)S(1)}, u32[]{:S(2)}, u32[]{:S(2)}) collective-permute-start(bf16[4,48,1152]{2,1,0:T(8,128)(2,1)S(1)} %pad_maximum_fusion.mine), channel_id=1, source_target_pairs={{0,1},{1,0},{2,3},{3,2},{4,5},{5,4},{6,7},{7,6},{8,9},{9,8},{10,11... | collective-permute-start | bytes 1327112 | tf_op jit(solution)/shard_map/ppermute | solution.py:402
  (72 shorter events, 18.5 us)
Async XLA Ops:
  5.7 3.4 %collective-permute-start.5 = (bf16[512,128]{1,0:T(8,128)(2,1)S(1)}, bf16[512,128]{1,0:T(8,128)(2,1)S(1)}, u32[]{:S(2)}, u32[]{:S(2)}) collective-permute-start(bf16[512,128]{1,0:T(8,128)(2,1)S(1)} %get-tuple-element.110), channel_id=1, source_target_pairs={{64,32},{65,33},{66,34},{67,35},{68,36},{69,37},{70,38},{71,39},{7... | collective-permute-start | bytes 393224 | tf_op jit(solution)/shard_map/ppermute | solution.py:431
  6.5 4.1 %collective-permute-start.6 = (bf16[512,128]{1,0:T(8,128)(2,1)S(1)}, bf16[512,128]{1,0:T(8,128)(2,1)S(1)}, u32[]{:S(2)}, u32[]{:S(2)}) collective-permute-start(bf16[512,128]{1,0:T(8,128)(2,1)S(1)} %get-tuple-element.113), channel_id=1, source_target_pairs={{64,32},{65,33},{66,34},{67,35},{68,36},{69,37},{70,38},{71,39},{7... | collective-permute-start | bytes 393224 | tf_op jit(solution)/shard_map/ppermute | solution.py:431
  7.2 4.7 %collective-permute-start.7 = (bf16[512,128]{1,0:T(8,128)(2,1)S(1)}, bf16[512,128]{1,0:T(8,128)(2,1)S(1)}, u32[]{:S(2)}, u32[]{:S(2)}) collective-permute-start(bf16[512,128]{1,0:T(8,128)(2,1)S(1)} %get-tuple-element.116), channel_id=1, source_target_pairs={{64,32},{65,33},{66,34},{67,35},{68,36},{69,37},{70,38},{71,39},{7... | collective-permute-start | bytes 393224 | tf_op jit(solution)/shard_map/ppermute | solution.py:431
  7.9 12.9 %collective-permute-start.8 = (bf16[512,128]{1,0:T(8,128)(2,1)S(1)}, bf16[512,128]{1,0:T(8,128)(2,1)S(1)}, u32[]{:S(2)}, u32[]{:S(2)}) collective-permute-start(bf16[512,128]{1,0:T(8,128)(2,1)S(1)} %get-tuple-element.119), channel_id=1, source_target_pairs={{32,0},{33,1},{34,2},{35,3},{36,4},{37,5},{38,6},{39,7},{40,8},{41... | collective-permute-start | bytes 393224 | tf_op jit(solution)/shard_map/ppermute | solution.py:431
  9.2 16.5 %collective-permute-start.9 = (bf16[512,128]{1,0:T(8,128)(2,1)S(1)}, bf16[512,128]{1,0:T(8,128)(2,1)S(1)}, u32[]{:S(2)}, u32[]{:S(2)}) collective-permute-start(bf16[512,128]{1,0:T(8,128)(2,1)S(1)} %get-tuple-element.122), channel_id=1, source_target_pairs={{32,0},{33,1},{34,2},{35,3},{36,4},{37,5},{38,6},{39,7},{40,8},{41... | collective-permute-start | bytes 393224 | tf_op jit(solution)/shard_map/ppermute | solution.py:431
  10.6 19.3 %collective-permute-start.10 = (bf16[512,128]{1,0:T(8,128)(2,1)S(1)}, bf16[512,128]{1,0:T(8,128)(2,1)S(1)}, u32[]{:S(2)}, u32[]{:S(2)}) collective-permute-start(bf16[512,128]{1,0:T(8,128)(2,1)S(1)} %get-tuple-element.125), channel_id=1, source_target_pairs={{32,0},{33,1},{34,2},{35,3},{36,4},{37,5},{38,6},{39,7},{40,8},{41... | collective-permute-start | bytes 393224 | tf_op jit(solution)/shard_map/ppermute | solution.py:431
  11.9 19.8 %collective-permute-start.11 = (bf16[512,128]{1,0:T(8,128)(2,1)S(1)}, bf16[512,128]{1,0:T(8,128)(2,1)S(1)}, u32[]{:S(2)}, u32[]{:S(2)}) collective-permute-start(bf16[512,128]{1,0:T(8,128)(2,1)S(1)} %get-tuple-element.127), channel_id=1, source_target_pairs={{32,0},{33,1},{34,2},{35,3},{36,4},{37,5},{38,6},{39,7},{40,8},{41... | collective-permute-start | bytes 393224 | tf_op jit(solution)/shard_map/ppermute | solution.py:431
  21.8 11.9 %collective-permute-start.12 = (bf16[512,128]{1,0:T(8,128)(2,1)S(1)}, bf16[512,128]{1,0:T(8,128)(2,1)S(1)}, u32[]{:S(2)}, u32[]{:S(2)}) collective-permute-start(bf16[512,128]{1,0:T(8,128)(2,1)S(1)} %get-tuple-element.135), channel_id=1, source_target_pairs={{0,2},{1,3},{2,4},{3,5},{4,6},{5,7},{6,8},{7,9},{8,10},{9,11},{10,... | collective-permute-start | bytes 393224 | tf_op jit(solution)/shard_map/ppermute | solution.py:407
  26.7 13.0 %collective-permute-start.17 = (bf16[512,128]{1,0:T(8,128)(2,1)S(1)}, bf16[512,128]{1,0:T(8,128)(2,1)S(1)}, u32[]{:S(2)}, u32[]{:S(2)}) collective-permute-start(bf16[512,128]{1,0:T(8,128)(2,1)S(1)} %get-tuple-element.143), channel_id=1, source_target_pairs={{0,2},{1,3},{2,4},{3,5},{4,6},{5,7},{6,8},{7,9},{8,10},{9,11},{10,... | collective-permute-start | bytes 393224 | tf_op jit(solution)/shard_map/ppermute | solution.py:407
  33.7 6.7 %collective-permute-start.13 = (bf16[48,1152]{1,0:T(8,128)(2,1)S(1)}, bf16[48,1152]{1,0:T(8,128)(2,1)S(1)}, u32[]{:S(2)}, u32[]{:S(2)}) collective-permute-start(bf16[48,1152]{1,0:T(8,128)(2,1)S(1)} %get-tuple-element.137), channel_id=1, source_target_pairs={{0,1},{1,0},{2,3},{3,2},{4,5},{5,4},{6,7},{7,6},{8,9},{9,8},{10,11... | collective-permute-start | bytes 331784 | tf_op jit(solution)/shard_map/ppermute | solution.py:402
  39.6 7.9 %collective-permute-start.18 = (bf16[512,128]{1,0:T(8,128)(2,1)S(1)}, bf16[512,128]{1,0:T(8,128)(2,1)S(1)}, u32[]{:S(2)}, u32[]{:S(2)}) collective-permute-start(bf16[512,128]{1,0:T(8,128)(2,1)S(1)} %get-tuple-element.145), channel_id=1, source_target_pairs={{0,2},{1,3},{2,4},{3,5},{4,6},{5,7},{6,8},{7,9},{8,10},{9,11},{10,... | collective-permute-start | bytes 393224 | tf_op jit(solution)/shard_map/ppermute | solution.py:407
  40.5 17.5 %collective-permute-start.20 = (bf16[48,1152]{1,0:T(8,128)(2,1)S(1)}, bf16[48,1152]{1,0:T(8,128)(2,1)S(1)}, u32[]{:S(2)}, u32[]{:S(2)}) collective-permute-start(bf16[48,1152]{1,0:T(8,128)(2,1)S(1)} %add_convert_fusion.4), channel_id=1, source_target_pairs={{0,8},{1,9},{2,10},{3,11},{4,12},{5,13},{6,14},{7,15},{8,0},{9,1},... | collective-permute-start | bytes 331784 | tf_op jit(solution)/shard_map/ppermute | solution.py:402
  41.9 16.0 %collective-permute-start.21 = (bf16[48,1152]{1,0:T(8,128)(2,1)S(1)}, bf16[48,1152]{1,0:T(8,128)(2,1)S(1)}, u32[]{:S(2)}, u32[]{:S(2)}) collective-permute-start(bf16[48,1152]{1,0:T(8,128)(2,1)S(1)} %add_convert_fusion.3), channel_id=1, source_target_pairs={{0,16},{1,17},{2,18},{3,19},{4,20},{5,21},{6,22},{7,23},{8,24},{9,... | collective-permute-start | bytes 331784 | tf_op jit(solution)/shard_map/ppermute | solution.py:402
  44.6 10.3 %collective-permute-start.19 = (bf16[512,128]{1,0:T(8,128)(2,1)S(1)}, bf16[512,128]{1,0:T(8,128)(2,1)S(1)}, u32[]{:S(2)}, u32[]{:S(2)}) collective-permute-start(bf16[512,128]{1,0:T(8,128)(2,1)S(1)} %get-tuple-element.146), channel_id=1, source_target_pairs={{0,2},{1,3},{2,4},{3,5},{4,6},{5,7},{6,8},{7,9},{8,10},{9,11},{10,... | collective-permute-start | bytes 393224 | tf_op jit(solution)/shard_map/ppermute | solution.py:407
  45.8 12.1 %collective-permute-start.22 = (bf16[48,1152]{1,0:T(8,128)(2,1)S(1)}, bf16[48,1152]{1,0:T(8,128)(2,1)S(1)}, u32[]{:S(2)}, u32[]{:S(2)}) collective-permute-start(bf16[48,1152]{1,0:T(8,128)(2,1)S(1)} %add_convert_fusion.2), channel_id=1, source_target_pairs={{0,24},{1,25},{2,26},{3,27},{4,28},{5,29},{6,30},{7,31},{8,16},{9,... | collective-permute-start | bytes 331784 | tf_op jit(solution)/shard_map/ppermute | solution.py:402
  55.6 3.5 %collective-permute-start.23 = (bf16[2,512,128]{2,1,0:T(8,128)(2,1)S(1)}, bf16[2,512,128]{2,1,0:T(8,128)(2,1)S(1)}, u32[]{:S(2)}, u32[]{:S(2)}) collective-permute-start(bf16[2,512,128]{2,1,0:T(8,128)(2,1)S(1)} %get-tuple-element.156), channel_id=1, source_target_pairs={{0,1},{1,0},{2,3},{3,2},{4,5},{5,4},{6,7},{7,6},{8,9},{9,8},{10,11... | collective-permute-start | bytes 786440 | tf_op jit(solution)/shard_map/ppermute | solution.py:402
  59.1 8.3 %collective-permute-start.26 = (bf16[48,1152]{1,0:T(8,128)(2,1)S(1)}, bf16[48,1152]{1,0:T(8,128)(2,1)S(1)}, u32[]{:S(2)}, u32[]{:S(2)}) collective-permute-start(bf16[48,1152]{1,0:T(8,128)(2,1)S(1)} %add_convert_fusion.1), channel_id=1, source_target_pairs={{0,6},{1,7},{2,4},{3,5},{4,2},{5,3},{6,0},{7,1},{8,14},{9,15},{10,... | collective-permute-start | bytes 331784 | tf_op jit(solution)/shard_map/ppermute | solution.py:402
  59.1 8.3 %collective-permute-start.25 = (bf16[48,1152]{1,0:T(8,128)(2,1)S(1)}, bf16[48,1152]{1,0:T(8,128)(2,1)S(1)}, u32[]{:S(2)}, u32[]{:S(2)}) collective-permute-start(bf16[48,1152]{1,0:T(8,128)(2,1)S(1)} %add_convert_fusion.1), channel_id=1, source_target_pairs={{0,4},{1,5},{2,6},{3,7},{4,0},{5,1},{6,2},{7,3},{8,12},{9,13},{10,... | collective-permute-start | bytes 331784 | tf_op jit(solution)/shard_map/ppermute | solution.py:402
  59.1 8.3 %collective-permute-start.24 = (bf16[48,1152]{1,0:T(8,128)(2,1)S(1)}, bf16[48,1152]{1,0:T(8,128)(2,1)S(1)}, u32[]{:S(2)}, u32[]{:S(2)}) collective-permute-start(bf16[48,1152]{1,0:T(8,128)(2,1)S(1)} %add_convert_fusion.1), channel_id=1, source_target_pairs={{0,2},{1,3},{2,0},{3,1},{4,6},{5,7},{6,4},{7,5},{8,10},{9,11},{10,... | collective-permute-start | bytes 331784 | tf_op jit(solution)/shard_map/ppermute | solution.py:402
  62.4 8.4 %collective-permute-start.30 = (bf16[2,512,128]{2,1,0:T(8,128)(2,1)S(1)}, bf16[2,512,128]{2,1,0:T(8,128)(2,1)S(1)}, u32[]{:S(2)}, u32[]{:S(2)}) collective-permute-start(bf16[2,512,128]{2,1,0:T(8,128)(2,1)S(1)} %get-tuple-element.159), channel_id=1, source_target_pairs={{0,1},{1,4},{2,3},{3,6},{4,5},{5,8},{6,7},{7,10},{8,9},{9,12},{10,... | collective-permute-start | bytes 786440 | tf_op jit(solution)/shard_map/ppermute | solution.py:445
  67.5 6.1 %collective-permute-start.29 = (bf16[48,1152]{1,0:T(8,128)(2,1)S(1)}, bf16[48,1152]{1,0:T(8,128)(2,1)S(1)}, u32[]{:S(2)}, u32[]{:S(2)}) collective-permute-start(bf16[48,1152]{1,0:T(8,128)(2,1)S(1)} %add_convert_fusion), channel_id=1, source_target_pairs={{0,24},{1,25},{2,26},{3,27},{4,28},{5,29},{6,30},{7,31},{8,16},{9,... | collective-permute-start | bytes 331784 | tf_op jit(solution)/shard_map/ppermute | solution.py:402
  67.8 5.8 %collective-permute-start.28 = (bf16[48,1152]{1,0:T(8,128)(2,1)S(1)}, bf16[48,1152]{1,0:T(8,128)(2,1)S(1)}, u32[]{:S(2)}, u32[]{:S(2)}) collective-permute-start(bf16[48,1152]{1,0:T(8,128)(2,1)S(1)} %add_convert_fusion), channel_id=1, source_target_pairs={{0,16},{1,17},{2,18},{3,19},{4,20},{5,21},{6,22},{7,23},{8,24},{9,... | collective-permute-start | bytes 331784 | tf_op jit(solution)/shard_map/ppermute | solution.py:402
  68.2 6.3 %collective-permute-start.27 = (bf16[48,1152]{1,0:T(8,128)(2,1)S(1)}, bf16[48,1152]{1,0:T(8,128)(2,1)S(1)}, u32[]{:S(2)}, u32[]{:S(2)}) collective-permute-start(bf16[48,1152]{1,0:T(8,128)(2,1)S(1)} %add_convert_fusion), channel_id=1, source_target_pairs={{0,8},{1,9},{2,10},{3,11},{4,12},{5,13},{6,14},{7,15},{8,0},{9,1},... | collective-permute-start | bytes 331784 | tf_op jit(solution)/shard_map/ppermute | solution.py:402
  74.5 5.1 %collective-permute-start.31 = (bf16[4,48,1152]{2,1,0:T(8,128)(2,1)S(1)}, bf16[4,48,1152]{2,1,0:T(8,128)(2,1)S(1)}, u32[]{:S(2)}, u32[]{:S(2)}) collective-permute-start(bf16[4,48,1152]{2,1,0:T(8,128)(2,1)S(1)} %pad_maximum_fusion.mine), channel_id=1, source_target_pairs={{0,1},{1,0},{2,3},{3,2},{4,5},{5,4},{6,7},{7,6},{8,9},{9,8},{10,11... | collective-permute-start | bytes 1327112 | tf_op jit(solution)/shard_map/ppermute | solution.py:402
  (10 other events, 40.1 us)

commit v4 on v3

--- a/solution.py
+++ b/solution.py
@@ -309,54 +309,48 @@
     )(trainer, vmem(gins), pd, vmem(wn))
 
 
-def sort_kernel(trainer, *refs):
-    came, keeps, passes = refs[:4], refs[4], refs[5]
+def slots_kernel(trainer, stays, arrived, *refs):
+    came, passed, out, keeps, passes, sems = refs[:4], refs[4:8], *refs[8:]
     me = lax.axis_index("brick")
     core = lax.rem(me, 2)
     peers = trainer.shape[1] // 2
-    owner = lax.rem(me + peers - 2, peers)
-    for micro in range(2):
-        first, second = came[2 * micro][...], came[2 * micro + 1][...]
-        keeps[micro] = choose(trainer, micro, owner, 2, first, second)
-        passes[micro] = choose(trainer, micro, owner, 3 - 2 * core, first, second)
-
-
-def sort_step(trainer, came):
-    return pl.pallas_call(
-        sort_kernel,
-        in_specs=[SM] + [VM] * 4,
-        out_specs=[VM] * 2,
-        out_shape=[shape((2, VOX, C))] * 2,
-        compiler_params=params(),
-        name="sort_slots",
-    )(trainer, *came)
-
-
-def slots_kernel(stays, keeps, passed, arrived, out, sems):
-    core = lax.rem(lax.axis_index("brick"), 2)
+    near = lax.rem(me + peers - 2, peers)
+    far = lax.rem(me + peers - 1 - 2 * core, peers)
     copies = [
         pltpu.make_async_copy(block.at[micro], out.at[micro, d], sems.at[i, micro])
         for i, (block, d) in enumerate(
-            ((stays, 0), (keeps, 2), (passed, 1 + 2 * core), (arrived, 3 - 2 * core))
+            ((stays, 0), (arrived, 3 - 2 * core), (keeps, 2), (passes, 1 + 2 * core))
         )
         for micro in range(2)
     ]
-    for copy in copies:
+    for copy in copies[:4]:
         copy.start()
+    for micro in range(2):
+        bricks = slice(2 * micro, 2 * micro + 2)
+        first, second = [ref[...] for ref in came[bricks]]
+        keeps[micro] = choose(trainer, micro, near, 2, first, second)
+        first, second = [ref[...] for ref in passed[bricks]]
+        passes[micro] = choose(trainer, micro, far, 1 + 2 * core, first, second)
+        copies[4 + micro].start()
+        copies[6 + micro].start()
     for copy in copies:
         copy.wait()
 
 
-def slots_step(*blocks):
+def slots_step(trainer, stays, arrived, came, passed):
     return pl.pallas_call(
         slots_kernel,
-        in_specs=[VM] * 4,
+        in_specs=[SM] + [VM] * 10,
         out_specs=ANY,
         out_shape=shape((2, 4, VOX, C)),
-        scratch_shapes=[pltpu.SemaphoreType.DMA((4, 2))],
+        scratch_shapes=[
+            pltpu.VMEM((2, VOX, C), BF16),
+            pltpu.VMEM((2, VOX, C), BF16),
+            pltpu.SemaphoreType.DMA((4, 2)),
+        ],
         compiler_params=params(),
         name="slots",
-    )(*blocks)
+    )(trainer, stays, arrived, *came, *passed)
 
 
 def finish_kernel(scale, mine, other, out_hbm, out, sems):
@@ -439,8 +433,7 @@
     send, came[0] = lax.optimization_barrier([send, came[0]])
     from_core = [swap(block, 1) for block in send]
     gin, stays, leaves = last_step(last, trainer, gins, pd, wn)
-    from_core, gin, leaves, came[1] = lax.optimization_barrier([from_core, gin, leaves, came[1]])
-    came.append(shifted(gin, 2))
+    from_core, came[1] = lax.optimization_barrier([from_core, came[1]])
     across = [(i, (i + 1 + 2 * (i % 2)) % peers) for i in range(peers)]
     arrived = lax.ppermute(leaves, "brick", across)
 
@@ -449,16 +442,17 @@
     for block, bits in zip(part[1:], Y_BITS):
         total = total + swap(block.astype(BF16), bits).astype(F32)
     total = total.astype(BF16)
-    keeps, passes = sort_step(trainer, came)
-    passed = swap(passes, 1)
+    passed = [swap(block, 1) for block in came]
     total, passed = lax.optimization_barrier([total, passed])
     full = total.astype(F32)
     for bits in Z_BITS:
         full = full + swap(total, bits).astype(F32)
     full = full.astype(BF16)
     got = [swap(full, bits) for bits in Y_BITS]
-    got, arrived = lax.optimization_barrier([got, arrived])
-    skip_grads = slots_step(stays, keeps, passed, arrived)
+    came.append(shifted(gin, 2))
+    passed.append(swap(came[3], 1))
+    got, arrived, passed = lax.optimization_barrier([got, arrived, passed])
+    skip_grads = slots_step(trainer, stays, arrived, came, passed)
     skip_grads = skip_grads.reshape((1, micros, 4) + saved_inputs.shape[3:])
     mine = jnp.stack([full] + got)
     other = swap(mine, 1)

time: 81.3 us -> 75.2 us (0.925)
  waiting for transfers between devices: 28 us -> 15.7 us
  starting transfers between devices: 38.8 us -> 44.7 us
    ppermute x4, waiting for transfers between devices: 8.99 us -> 0.01 us  [shifted(): lax.ppermute(block, 'brick', [(i, (i + distance) % n) for i in range(n)])]
    ppermute x15 -> x18, starting transfers between devices: 21.2 us -> 24.8 us  [swap(): return lax.ppermute(block, 'brick', pairs)]
    ppermute x15 -> x18, waiting for transfers between devices: 8.69 us -> 5.39 us  [swap(): return lax.ppermute(block, 'brick', pairs)]
    ppermute x1, starting transfers between devices: 1.43 us -> 4.2 us  [shards(): arrived = lax.ppermute(leaves, 'brick', across)]
    pallas_call x2 -> x1, Pallas kernels: 1.73 us -> 1.57 us  [slots_step(): pl.pallas_call(slots_kernel, in_specs=[SM] + [VM] * 10, out_specs=ANY, ou...]
  transfers between devices with their start and end apart: 32 -> 35, of which waited for: 10 -> 10; matrix products, arithmetic and copies ran while one was open for 0% -> 0% of each run, Pallas kernels for 12% -> 13%
where the time goes in v4:
time: 75.2 us; the launch traced here: 74.6 us
  starting transfers between devices  44.7 us (59%)
  waiting for transfers between devices  15.7 us (21%)
  Pallas kernels  12.6 us (17%)
  between operations  1.21 us (2%)
    ppermute x18, starting transfers between devices, swap(): return lax.ppermute(block, 'brick', pairs)  24.8 us
    ppermute x12, starting transfers between devices, shards(): above[slot + WORK] = lax.ppermute(gin, 'section', [(sender, sender - 1)])  10.7 us
    ppermute x12, waiting for transfers between devices, shards(): above[slot + WORK] = lax.ppermute(gin, 'section', [(sender, sender - 1)])  10.3 us
    ppermute x18, waiting for transfers between devices, swap(): return lax.ppermute(block, 'brick', pairs)  5.39 us
    ppermute x4, starting transfers between devices, shifted(): lax.ppermute(block, 'brick', [(i, (i + distance) % n) for i in range(n)])  5.11 us
    ppermute x1, starting transfers between devices, shards(): arrived = lax.ppermute(leaves, 'brick', across)  4.2 us
    pallas_call x14, Pallas kernels, tick_step(): pl.pallas_call(functools.partial(tick_kernel, slot), in_specs=[VM] * (6 +...  2.98 us
    pallas_call x1, Pallas kernels, late_step(): pl.pallas_call(functools.partial(late_kernel, slot), in_specs=[VM] * 7, o...  1.99 us
  transfers between devices with their start and end apart: 35, of which 10 were waited for; matrix products, arithmetic and copies ran while one was open for 0% of the time, Pallas kernels for 13%

profile of v4, /device:TPU:1, one launch (start us, length us, event | category | flops | bytes accessed | tf_op | source)
XLA Modules:
  0.0 74.6 jit_solution(17493413426085481701)
XLA Ops:
  0.6 1.6 %tick_first.1 = (bf16[512,128]{1,0:T(8,128)(2,1)S(1)}, bf16[4,512,128]{2,1,0:T(8,128)(2,1)S(1)}, bf16[4,512,128]{2,1,0:T(8,128)(2,1)S(1)}, bf16[384,1152]{1,0:T(...) custom-call(s32[2,2]{1,0:T(2,128)} %c_hbm.1, ...), custom_call_target="tpu_custom_call" | custom-call | tf_op jit(solution)/shard_map/tick_first/pallas_call | solution.py:132
  7.9 1.3 %collective-permute-start.8 = (bf16[512,128]{1,0:T(8,128)(2,1)S(1)}, bf16[512,128]{1,0:T(8,128)(2,1)S(1)}, u32[]{:S(2)}, u32[]{:S(2)}) collective-permute-start(bf16[512,128]{1,0:T(8,128)(2,1)S(1)} %get-tuple-element.121), channel_id=1, source_target_pairs={{32,0},{33,1},{34,2},{35,3},{36,4},{37,5},{38,6},{39,7},{40,8},{41... | collective-permute-start | bytes 393224 | tf_op jit(solution)/shard_map/ppermute | solution.py:425
  9.2 1.3 %collective-permute-start.9 = (bf16[512,128]{1,0:T(8,128)(2,1)S(1)}, bf16[512,128]{1,0:T(8,128)(2,1)S(1)}, u32[]{:S(2)}, u32[]{:S(2)}) collective-permute-start(bf16[512,128]{1,0:T(8,128)(2,1)S(1)} %get-tuple-element.124), channel_id=1, source_target_pairs={{32,0},{33,1},{34,2},{35,3},{36,4},{37,5},{38,6},{39,7},{40,8},{41... | collective-permute-start | bytes 393224 | tf_op jit(solution)/shard_map/ppermute | solution.py:425
  10.6 1.3 %collective-permute-start.10 = (bf16[512,128]{1,0:T(8,128)(2,1)S(1)}, bf16[512,128]{1,0:T(8,128)(2,1)S(1)}, u32[]{:S(2)}, u32[]{:S(2)}) collective-permute-start(bf16[512,128]{1,0:T(8,128)(2,1)S(1)} %get-tuple-element.127), channel_id=1, source_target_pairs={{32,0},{33,1},{34,2},{35,3},{36,4},{37,5},{38,6},{39,7},{40,8},{41... | collective-permute-start | bytes 393224 | tf_op jit(solution)/shard_map/ppermute | solution.py:425
  11.9 1.4 %collective-permute-start.11 = (bf16[512,128]{1,0:T(8,128)(2,1)S(1)}, bf16[512,128]{1,0:T(8,128)(2,1)S(1)}, u32[]{:S(2)}, u32[]{:S(2)}) collective-permute-start(bf16[512,128]{1,0:T(8,128)(2,1)S(1)} %get-tuple-element.129), channel_id=1, source_target_pairs={{32,0},{33,1},{34,2},{35,3},{36,4},{37,5},{38,6},{39,7},{40,8},{41... | collective-permute-start | bytes 393224 | tf_op jit(solution)/shard_map/ppermute | solution.py:425
  13.3 7.5 %collective-permute-done.8.rest_2_ = bf16[512,128]{1,0:T(8,128)(2,1)S(1)} collective-permute-done((bf16[512,128]{1,0:T(8,128)(2,1)S(1)}, bf16[512,128]{1,0:T(8,128)(2,1)S(1)}, u32[]{:S(2)}, u32[]{:S(2)}) %collective-permute-start.8) | collective-permute-done | bytes 131104 | tf_op jit(solution)/shard_map/ppermute | solution.py:425
  21.8 1.7 %collective-permute-start.12 = (bf16[512,128]{1,0:T(8,128)(2,1)S(1)}, bf16[512,128]{1,0:T(8,128)(2,1)S(1)}, u32[]{:S(2)}, u32[]{:S(2)}) collective-permute-start(bf16[512,128]{1,0:T(8,128)(2,1)S(1)} %get-tuple-element.138), channel_id=1, source_target_pairs={{0,2},{1,3},{2,4},{3,5},{4,6},{5,7},{6,8},{7,9},{8,10},{9,11},{10,... | collective-permute-start | bytes 393224 | tf_op jit(solution)/shard_map/ppermute | solution.py:401
  23.8 1.9 %collective-permute-done.9.rest_2_ = bf16[512,128]{1,0:T(8,128)(2,1)S(1)} collective-permute-done((bf16[512,128]{1,0:T(8,128)(2,1)S(1)}, bf16[512,128]{1,0:T(8,128)(2,1)S(1)}, u32[]{:S(2)}, u32[]{:S(2)}) %collective-permute-start.9) | collective-permute-done | bytes 131104 | tf_op jit(solution)/shard_map/ppermute | solution.py:425
  26.7 1.9 %collective-permute-start.17 = (bf16[512,128]{1,0:T(8,128)(2,1)S(1)}, bf16[512,128]{1,0:T(8,128)(2,1)S(1)}, u32[]{:S(2)}, u32[]{:S(2)}) collective-permute-start(bf16[512,128]{1,0:T(8,128)(2,1)S(1)} %get-tuple-element.143), channel_id=1, source_target_pairs={{0,2},{1,3},{2,4},{3,5},{4,6},{5,7},{6,8},{7,9},{8,10},{9,11},{10,... | collective-permute-start | bytes 393224 | tf_op jit(solution)/shard_map/ppermute | solution.py:401
  28.5 1.3 %weight_terms_early.1.acc_in = f32[384,1152]{1,0:T(8,128)S(1)} custom-call(bf16[4,512,128]{2,1,0:T(8,128)(2,1)S(1)} %get-tuple-element.125.rest_0_.deltas, bf16[4,384,512]{2,1,0:T(8,128)(2,1)S(1)} %inputs_across.1.xt), custom_call_target="tpu_custom_call" | custom-call | flops 1 | bytes 262144 | tf_op jit(solution)/shard_map/weight_terms_early/pallas_call | solution.py:219
  31.7 2.0 %weight_terms.1 = (bf16[48,1152]{1,0:T(8,128)(2,1)S(1)}, bf16[48,1152]{1,0:T(8,128)(2,1)S(1)}, bf16[48,1152]{1,0:T(8,128)(2,1)S(1)}, bf16[48,1152]{1,0:T(8,128)(...) custom-call(f32[4,8,128]{2,1,0:T(8,128)S(1)} %get-tuple-element.85.s, ...), custom_call_target="tpu_custom_call" | custom-call | flops 905969664 | bytes 7340032 | tf_op jit(solution)/shard_map/weight_terms/pallas_call | solution.py:258
  33.7 3.9 %collective-permute-start.13 = (bf16[48,1152]{1,0:T(8,128)(2,1)S(1)}, bf16[48,1152]{1,0:T(8,128)(2,1)S(1)}, u32[]{:S(2)}, u32[]{:S(2)}) collective-permute-start(bf16[48,1152]{1,0:T(8,128)(2,1)S(1)} %get-tuple-element.139), channel_id=1, source_target_pairs={{0,1},{1,0},{2,3},{3,2},{4,5},{5,4},{6,7},{7,6},{8,9},{9,8},{10,11... | collective-permute-start | bytes 331784 | tf_op jit(solution)/shard_map/ppermute | solution.py:396
  40.3 2.7 %collective-permute-start.19 = (bf16[48,1152]{1,0:T(8,128)(2,1)S(1)}, bf16[48,1152]{1,0:T(8,128)(2,1)S(1)}, u32[]{:S(2)}, u32[]{:S(2)}) collective-permute-start(bf16[48,1152]{1,0:T(8,128)(2,1)S(1)} %add_convert_fusion.3), channel_id=1, source_target_pairs={{0,16},{1,17},{2,18},{3,19},{4,20},{5,21},{6,22},{7,23},{8,24},{9,... | collective-permute-start | bytes 331784 | tf_op jit(solution)/shard_map/ppermute | solution.py:396
  43.6 1.5 %last_grad.1 = (bf16[512,128]{1,0:T(8,128)(2,1)S(1)}, bf16[2,512,128]{2,1,0:T(8,128)(2,1)S(1)}, bf16[2,512,128]{2,1,0:T(8,128)(2,1)S(1)}) custom-call(s32[2,64]{1,0:T(2,128)S(1)} %copy-done.1, bf16[4,512,128]{2,1,0:T(8,128)(2,1)S(1)} %get-tuple-element.128.gins, bf16[512,1152]{1,0:T(8,128)(2,1)S(1)} %get-tuple-element.131.pd, ...), custom_call_target="tpu_custom_call" | custom-call | flops 452984832 | bytes 4194304 | tf_op jit(solution)/shard_map/last_grad/pallas_call | solution.py:299
  46.0 1.9 %collective-permute-start.21 = (bf16[512,128]{1,0:T(8,128)(2,1)S(1)}, bf16[512,128]{1,0:T(8,128)(2,1)S(1)}, u32[]{:S(2)}, u32[]{:S(2)}) collective-permute-start(bf16[512,128]{1,0:T(8,128)(2,1)S(1)} %collective-permute-done.12.refs_0_), channel_id=1, source_target_pairs={{0,1},{1,0},{2,3},{3,2},{4,5},{5,4},{6,7},{7,6},{8,9},{9,8},{10,11... | collective-permute-start | bytes 393224 | tf_op jit(solution)/shard_map/ppermute | solution.py:396
  47.9 1.5 %collective-permute-start.22 = (bf16[512,128]{1,0:T(8,128)(2,1)S(1)}, bf16[512,128]{1,0:T(8,128)(2,1)S(1)}, u32[]{:S(2)}, u32[]{:S(2)}) collective-permute-start(bf16[512,128]{1,0:T(8,128)(2,1)S(1)} %collective-permute-done.17.refs_1_), channel_id=1, source_target_pairs={{0,1},{1,0},{2,3},{3,2},{4,5},{5,4},{6,7},{7,6},{8,9},{9,8},{10,11... | collective-permute-start | bytes 393224 | tf_op jit(solution)/shard_map/ppermute | solution.py:396
  49.4 1.1 %collective-permute-done.20 = bf16[48,1152]{1,0:T(8,128)(2,1)S(1)} collective-permute-done((bf16[48,1152]{1,0:T(8,128)(2,1)S(1)}, bf16[48,1152]{1,0:T(8,128)(2,1)S(1)}, u32[]{:S(2)}, u32[]{:S(2)}) %collective-permute-start.20) | collective-permute-done | bytes 110624 | tf_op jit(solution)/shard_map/ppermute | solution.py:396
  50.6 3.8 %collective-permute-start.27 = (bf16[48,1152]{1,0:T(8,128)(2,1)S(1)}, bf16[48,1152]{1,0:T(8,128)(2,1)S(1)}, u32[]{:S(2)}, u32[]{:S(2)}) collective-permute-start(bf16[48,1152]{1,0:T(8,128)(2,1)S(1)} %add_convert_fusion.1), channel_id=1, source_target_pairs={{0,6},{1,7},{2,4},{3,5},{4,2},{5,3},{6,0},{7,1},{8,14},{9,15},{10,... | collective-permute-start | bytes 331784 | tf_op jit(solution)/shard_map/ppermute | solution.py:396
  54.9 4.2 %collective-permute-start.31 = (bf16[2,512,128]{2,1,0:T(8,128)(2,1)S(1)}, bf16[2,512,128]{2,1,0:T(8,128)(2,1)S(1)}, u32[]{:S(2)}, u32[]{:S(2)}) collective-permute-start(bf16[2,512,128]{2,1,0:T(8,128)(2,1)S(1)} %get-tuple-element.155), channel_id=1, source_target_pairs={{0,1},{1,4},{2,3},{3,6},{4,5},{5,8},{6,7},{7,10},{8,9},{9,12},{10,... | collective-permute-start | bytes 786440 | tf_op jit(solution)/shard_map/ppermute | solution.py:438
  61.2 1.7 %collective-permute-start.28 = (bf16[48,1152]{1,0:T(8,128)(2,1)S(1)}, bf16[48,1152]{1,0:T(8,128)(2,1)S(1)}, u32[]{:S(2)}, u32[]{:S(2)}) collective-permute-start(bf16[48,1152]{1,0:T(8,128)(2,1)S(1)} %add_convert_fusion), channel_id=1, source_target_pairs={{0,8},{1,9},{2,10},{3,11},{4,12},{5,13},{6,14},{7,15},{8,0},{9,1},... | collective-permute-start | bytes 331784 | tf_op jit(solution)/shard_map/ppermute | solution.py:396
  63.0 3.0 %collective-permute-done.30 = bf16[48,1152]{1,0:T(8,128)(2,1)S(1)} collective-permute-done((bf16[48,1152]{1,0:T(8,128)(2,1)S(1)}, bf16[48,1152]{1,0:T(8,128)(2,1)S(1)}, u32[]{:S(2)}, u32[]{:S(2)}) %collective-permute-start.30) | collective-permute-done | bytes 110624 | tf_op jit(solution)/shard_map/ppermute | solution.py:396
  66.3 5.2 %collective-permute-start.34 = (bf16[4,48,1152]{2,1,0:T(8,128)(2,1)S(1)}, bf16[4,48,1152]{2,1,0:T(8,128)(2,1)S(1)}, u32[]{:S(2)}, u32[]{:S(2)}) collective-permute-start(bf16[4,48,1152]{2,1,0:T(8,128)(2,1)S(1)} %pad_maximum_fusion.mine), channel_id=1, source_target_pairs={{0,1},{1,0},{2,3},{3,2},{4,5},{5,4},{6,7},{7,6},{8,9},{9,8},{10,11... | collective-permute-start | bytes 1327112 | tf_op jit(solution)/shard_map/ppermute | solution.py:396
  71.5 1.6 %slots.1 = bf16[2,4,512,128]{3,2,1,0:T(8,128)(2,1)} custom-call(s32[2,64]{1,0:T(2,128)S(1)} %copy-done.1, bf16[2,512,128]{2,1,0:T(8,128)(2,1)S(1)} %get-tuple-element.132.stays, bf16[2,512,128]{2,1,0:T(8,128)(2,1)S(1)} %collective-permute-done.31.arrived, bf16[512,128]{1,0:T(8,128)(2,1)S(1)} %collective-permute-done.12.refs_0_, ...), custom_call_target="tpu_custom_call" | custom-call | tf_op jit(solution)/shard_map/slots/pallas_call | solution.py:341
  73.1 1.3 %finish_weights.1 = f32[3456,128]{1,0:T(8,128)} custom-call(bf16[4,48,1152]{2,1,0:T(8,128)(2,1)S(1)} %pad_maximum_fusion.mine, bf16[4,48,1152]{2,1,0:T(8,128)(2,1)S(1)} %collective-permute-done.34.other), custom_call_target="tpu_custom_call" | custom-call | tf_op jit(solution)/shard_map/finish_weights/pallas_call | solution.py:383
  (77 shorter events, 16.9 us)
Async XLA Ops:
  6.5 4.1 %collective-permute-start.6 = (bf16[512,128]{1,0:T(8,128)(2,1)S(1)}, bf16[512,128]{1,0:T(8,128)(2,1)S(1)}, u32[]{:S(2)}, u32[]{:S(2)}) collective-permute-start(bf16[512,128]{1,0:T(8,128)(2,1)S(1)} %get-tuple-element.115), channel_id=1, source_target_pairs={{64,32},{65,33},{66,34},{67,35},{68,36},{69,37},{70,38},{71,39},{7... | collective-permute-start | bytes 393224 | tf_op jit(solution)/shard_map/ppermute | solution.py:425
  7.2 4.7 %collective-permute-start.7 = (bf16[512,128]{1,0:T(8,128)(2,1)S(1)}, bf16[512,128]{1,0:T(8,128)(2,1)S(1)}, u32[]{:S(2)}, u32[]{:S(2)}) collective-permute-start(bf16[512,128]{1,0:T(8,128)(2,1)S(1)} %get-tuple-element.118), channel_id=1, source_target_pairs={{64,32},{65,33},{66,34},{67,35},{68,36},{69,37},{70,38},{71,39},{7... | collective-permute-start | bytes 393224 | tf_op jit(solution)/shard_map/ppermute | solution.py:425
  7.9 12.9 %collective-permute-start.8 = (bf16[512,128]{1,0:T(8,128)(2,1)S(1)}, bf16[512,128]{1,0:T(8,128)(2,1)S(1)}, u32[]{:S(2)}, u32[]{:S(2)}) collective-permute-start(bf16[512,128]{1,0:T(8,128)(2,1)S(1)} %get-tuple-element.121), channel_id=1, source_target_pairs={{32,0},{33,1},{34,2},{35,3},{36,4},{37,5},{38,6},{39,7},{40,8},{41... | collective-permute-start | bytes 393224 | tf_op jit(solution)/shard_map/ppermute | solution.py:425
  9.2 16.5 %collective-permute-start.9 = (bf16[512,128]{1,0:T(8,128)(2,1)S(1)}, bf16[512,128]{1,0:T(8,128)(2,1)S(1)}, u32[]{:S(2)}, u32[]{:S(2)}) collective-permute-start(bf16[512,128]{1,0:T(8,128)(2,1)S(1)} %get-tuple-element.124), channel_id=1, source_target_pairs={{32,0},{33,1},{34,2},{35,3},{36,4},{37,5},{38,6},{39,7},{40,8},{41... | collective-permute-start | bytes 393224 | tf_op jit(solution)/shard_map/ppermute | solution.py:425
  10.6 19.3 %collective-permute-start.10 = (bf16[512,128]{1,0:T(8,128)(2,1)S(1)}, bf16[512,128]{1,0:T(8,128)(2,1)S(1)}, u32[]{:S(2)}, u32[]{:S(2)}) collective-permute-start(bf16[512,128]{1,0:T(8,128)(2,1)S(1)} %get-tuple-element.127), channel_id=1, source_target_pairs={{32,0},{33,1},{34,2},{35,3},{36,4},{37,5},{38,6},{39,7},{40,8},{41... | collective-permute-start | bytes 393224 | tf_op jit(solution)/shard_map/ppermute | solution.py:425
  11.9 19.8 %collective-permute-start.11 = (bf16[512,128]{1,0:T(8,128)(2,1)S(1)}, bf16[512,128]{1,0:T(8,128)(2,1)S(1)}, u32[]{:S(2)}, u32[]{:S(2)}) collective-permute-start(bf16[512,128]{1,0:T(8,128)(2,1)S(1)} %get-tuple-element.129), channel_id=1, source_target_pairs={{32,0},{33,1},{34,2},{35,3},{36,4},{37,5},{38,6},{39,7},{40,8},{41... | collective-permute-start | bytes 393224 | tf_op jit(solution)/shard_map/ppermute | solution.py:425
  21.8 11.9 %collective-permute-start.12 = (bf16[512,128]{1,0:T(8,128)(2,1)S(1)}, bf16[512,128]{1,0:T(8,128)(2,1)S(1)}, u32[]{:S(2)}, u32[]{:S(2)}) collective-permute-start(bf16[512,128]{1,0:T(8,128)(2,1)S(1)} %get-tuple-element.138), channel_id=1, source_target_pairs={{0,2},{1,3},{2,4},{3,5},{4,6},{5,7},{6,8},{7,9},{8,10},{9,11},{10,... | collective-permute-start | bytes 393224 | tf_op jit(solution)/shard_map/ppermute | solution.py:401
  26.7 11.4 %collective-permute-start.17 = (bf16[512,128]{1,0:T(8,128)(2,1)S(1)}, bf16[512,128]{1,0:T(8,128)(2,1)S(1)}, u32[]{:S(2)}, u32[]{:S(2)}) collective-permute-start(bf16[512,128]{1,0:T(8,128)(2,1)S(1)} %get-tuple-element.143), channel_id=1, source_target_pairs={{0,2},{1,3},{2,4},{3,5},{4,6},{5,7},{6,8},{7,9},{8,10},{9,11},{10,... | collective-permute-start | bytes 393224 | tf_op jit(solution)/shard_map/ppermute | solution.py:401
  33.7 5.1 %collective-permute-start.13 = (bf16[48,1152]{1,0:T(8,128)(2,1)S(1)}, bf16[48,1152]{1,0:T(8,128)(2,1)S(1)}, u32[]{:S(2)}, u32[]{:S(2)}) collective-permute-start(bf16[48,1152]{1,0:T(8,128)(2,1)S(1)} %get-tuple-element.139), channel_id=1, source_target_pairs={{0,1},{1,0},{2,3},{3,2},{4,5},{5,4},{6,7},{7,6},{8,9},{9,8},{10,11... | collective-permute-start | bytes 331784 | tf_op jit(solution)/shard_map/ppermute | solution.py:396
  38.1 7.9 %collective-permute-start.23 = (bf16[512,128]{1,0:T(8,128)(2,1)S(1)}, bf16[512,128]{1,0:T(8,128)(2,1)S(1)}, u32[]{:S(2)}, u32[]{:S(2)}) collective-permute-start(bf16[512,128]{1,0:T(8,128)(2,1)S(1)} %get-tuple-element.153), channel_id=1, source_target_pairs={{0,2},{1,3},{2,4},{3,5},{4,6},{5,7},{6,8},{7,9},{8,10},{9,11},{10,... | collective-permute-start | bytes 393224 | tf_op jit(solution)/shard_map/ppermute | solution.py:401
  39.4 8.4 %collective-permute-start.18 = (bf16[48,1152]{1,0:T(8,128)(2,1)S(1)}, bf16[48,1152]{1,0:T(8,128)(2,1)S(1)}, u32[]{:S(2)}, u32[]{:S(2)}) collective-permute-start(bf16[48,1152]{1,0:T(8,128)(2,1)S(1)} %add_convert_fusion.4), channel_id=1, source_target_pairs={{0,8},{1,9},{2,10},{3,11},{4,12},{5,13},{6,14},{7,15},{8,0},{9,1},... | collective-permute-start | bytes 331784 | tf_op jit(solution)/shard_map/ppermute | solution.py:396
  40.3 7.5 %collective-permute-start.19 = (bf16[48,1152]{1,0:T(8,128)(2,1)S(1)}, bf16[48,1152]{1,0:T(8,128)(2,1)S(1)}, u32[]{:S(2)}, u32[]{:S(2)}) collective-permute-start(bf16[48,1152]{1,0:T(8,128)(2,1)S(1)} %add_convert_fusion.3), channel_id=1, source_target_pairs={{0,16},{1,17},{2,18},{3,19},{4,20},{5,21},{6,22},{7,23},{8,24},{9,... | collective-permute-start | bytes 331784 | tf_op jit(solution)/shard_map/ppermute | solution.py:396
  43.1 7.4 %collective-permute-start.20 = (bf16[48,1152]{1,0:T(8,128)(2,1)S(1)}, bf16[48,1152]{1,0:T(8,128)(2,1)S(1)}, u32[]{:S(2)}, u32[]{:S(2)}) collective-permute-start(bf16[48,1152]{1,0:T(8,128)(2,1)S(1)} %add_convert_fusion.2), channel_id=1, source_target_pairs={{0,24},{1,25},{2,26},{3,27},{4,28},{5,29},{6,30},{7,31},{8,16},{9,... | collective-permute-start | bytes 331784 | tf_op jit(solution)/shard_map/ppermute | solution.py:396
  45.1 14.0 %collective-permute-start.32 = (bf16[512,128]{1,0:T(8,128)(2,1)S(1)}, bf16[512,128]{1,0:T(8,128)(2,1)S(1)}, u32[]{:S(2)}, u32[]{:S(2)}) collective-permute-start(bf16[512,128]{1,0:T(8,128)(2,1)S(1)} %get-tuple-element.159), channel_id=1, source_target_pairs={{0,2},{1,3},{2,4},{3,5},{4,6},{5,7},{6,8},{7,9},{8,10},{9,11},{10,... | collective-permute-start | bytes 393224 | tf_op jit(solution)/shard_map/ppermute | solution.py:401
  46.0 4.6 %collective-permute-start.21 = (bf16[512,128]{1,0:T(8,128)(2,1)S(1)}, bf16[512,128]{1,0:T(8,128)(2,1)S(1)}, u32[]{:S(2)}, u32[]{:S(2)}) collective-permute-start(bf16[512,128]{1,0:T(8,128)(2,1)S(1)} %collective-permute-done.12.refs_0_), channel_id=1, source_target_pairs={{0,1},{1,0},{2,3},{3,2},{4,5},{5,4},{6,7},{7,6},{8,9},{9,8},{10,11... | collective-permute-start | bytes 393224 | tf_op jit(solution)/shard_map/ppermute | solution.py:396
  50.6 8.6 %collective-permute-start.27 = (bf16[48,1152]{1,0:T(8,128)(2,1)S(1)}, bf16[48,1152]{1,0:T(8,128)(2,1)S(1)}, u32[]{:S(2)}, u32[]{:S(2)}) collective-permute-start(bf16[48,1152]{1,0:T(8,128)(2,1)S(1)} %add_convert_fusion.1), channel_id=1, source_target_pairs={{0,6},{1,7},{2,4},{3,5},{4,2},{5,3},{6,0},{7,1},{8,14},{9,15},{10,... | collective-permute-start | bytes 331784 | tf_op jit(solution)/shard_map/ppermute | solution.py:396
  54.3 5.2 %collective-permute-start.26 = (bf16[48,1152]{1,0:T(8,128)(2,1)S(1)}, bf16[48,1152]{1,0:T(8,128)(2,1)S(1)}, u32[]{:S(2)}, u32[]{:S(2)}) collective-permute-start(bf16[48,1152]{1,0:T(8,128)(2,1)S(1)} %add_convert_fusion.1), channel_id=1, source_target_pairs={{0,4},{1,5},{2,6},{3,7},{4,0},{5,1},{6,2},{7,3},{8,12},{9,13},{10,... | collective-permute-start | bytes 331784 | tf_op jit(solution)/shard_map/ppermute | solution.py:396
  54.3 5.2 %collective-permute-start.25 = (bf16[48,1152]{1,0:T(8,128)(2,1)S(1)}, bf16[48,1152]{1,0:T(8,128)(2,1)S(1)}, u32[]{:S(2)}, u32[]{:S(2)}) collective-permute-start(bf16[48,1152]{1,0:T(8,128)(2,1)S(1)} %add_convert_fusion.1), channel_id=1, source_target_pairs={{0,2},{1,3},{2,0},{3,1},{4,6},{5,7},{6,4},{7,5},{8,10},{9,11},{10,... | collective-permute-start | bytes 331784 | tf_op jit(solution)/shard_map/ppermute | solution.py:396
  54.9 8.0 %collective-permute-start.31 = (bf16[2,512,128]{2,1,0:T(8,128)(2,1)S(1)}, bf16[2,512,128]{2,1,0:T(8,128)(2,1)S(1)}, u32[]{:S(2)}, u32[]{:S(2)}) collective-permute-start(bf16[2,512,128]{2,1,0:T(8,128)(2,1)S(1)} %get-tuple-element.155), channel_id=1, source_target_pairs={{0,1},{1,4},{2,3},{3,6},{4,5},{5,8},{6,7},{7,10},{8,9},{9,12},{10,... | collective-permute-start | bytes 786440 | tf_op jit(solution)/shard_map/ppermute | solution.py:438
  59.1 3.8 %collective-permute-start.33 = (bf16[512,128]{1,0:T(8,128)(2,1)S(1)}, bf16[512,128]{1,0:T(8,128)(2,1)S(1)}, u32[]{:S(2)}, u32[]{:S(2)}) collective-permute-start(bf16[512,128]{1,0:T(8,128)(2,1)S(1)} %collective-permute-done.32.refs_3_), channel_id=1, source_target_pairs={{0,1},{1,0},{2,3},{3,2},{4,5},{5,4},{6,7},{7,6},{8,9},{9,8},{10,11... | collective-permute-start | bytes 393224 | tf_op jit(solution)/shard_map/ppermute | solution.py:396
  59.6 6.4 %collective-permute-start.30 = (bf16[48,1152]{1,0:T(8,128)(2,1)S(1)}, bf16[48,1152]{1,0:T(8,128)(2,1)S(1)}, u32[]{:S(2)}, u32[]{:S(2)}) collective-permute-start(bf16[48,1152]{1,0:T(8,128)(2,1)S(1)} %add_convert_fusion), channel_id=1, source_target_pairs={{0,24},{1,25},{2,26},{3,27},{4,28},{5,29},{6,30},{7,31},{8,16},{9,... | collective-permute-start | bytes 331784 | tf_op jit(solution)/shard_map/ppermute | solution.py:396
  60.2 5.8 %collective-permute-start.29 = (bf16[48,1152]{1,0:T(8,128)(2,1)S(1)}, bf16[48,1152]{1,0:T(8,128)(2,1)S(1)}, u32[]{:S(2)}, u32[]{:S(2)}) collective-permute-start(bf16[48,1152]{1,0:T(8,128)(2,1)S(1)} %add_convert_fusion), channel_id=1, source_target_pairs={{0,16},{1,17},{2,18},{3,19},{4,20},{5,21},{6,22},{7,23},{8,24},{9,... | collective-permute-start | bytes 331784 | tf_op jit(solution)/shard_map/ppermute | solution.py:396
  61.2 5.0 %collective-permute-start.28 = (bf16[48,1152]{1,0:T(8,128)(2,1)S(1)}, bf16[48,1152]{1,0:T(8,128)(2,1)S(1)}, u32[]{:S(2)}, u32[]{:S(2)}) collective-permute-start(bf16[48,1152]{1,0:T(8,128)(2,1)S(1)} %add_convert_fusion), channel_id=1, source_target_pairs={{0,8},{1,9},{2,10},{3,11},{4,12},{5,13},{6,14},{7,15},{8,0},{9,1},... | collective-permute-start | bytes 331784 | tf_op jit(solution)/shard_map/ppermute | solution.py:396
  66.3 6.8 %collective-permute-start.34 = (bf16[4,48,1152]{2,1,0:T(8,128)(2,1)S(1)}, bf16[4,48,1152]{2,1,0:T(8,128)(2,1)S(1)}, u32[]{:S(2)}, u32[]{:S(2)}) collective-permute-start(bf16[4,48,1152]{2,1,0:T(8,128)(2,1)S(1)} %pad_maximum_fusion.mine), channel_id=1, source_target_pairs={{0,1},{1,0},{2,3},{3,2},{4,5},{5,4},{6,7},{7,6},{8,9},{9,8},{10,11... | collective-permute-start | bytes 1327112 | tf_op jit(solution)/shard_map/ppermute | solution.py:396
  (13 other events, 50.4 us)

commit v5 on v4

--- a/solution.py
+++ b/solution.py
@@ -154,6 +154,7 @@
 
 
 def tick_kernel(slot, shares, p_ref, sup_ref, wn, *rest):
+    last = slot // WORK == lax.axis_size("section") - 1
     deltas, gins, gin, pd = rest[-4:]
     zero = jnp.zeros((VOX, C), BF16)
     brick = slot % WORK
@@ -167,20 +168,23 @@
         gin[...] = input_grad(pd[...], wn[...])
         gins[brick] = gin[...]
 
-    if slot // WORK == lax.axis_size("section") - 1:
+    if last:
         @pl.when(jnp.logical_not(working(slot)))
         def _():
             gin[...] = gins[brick]
+            spread(deltas[brick].astype(F32), pd)
 
 
 def tick_step(slot, shares, preacts, sup, wn, deltas, gins, above):
     block, bricks = pltpu.VMEM((VOX, C), BF16), pltpu.VMEM((WORK, VOX, C), BF16)
+    last = slot // WORK == lax.axis_size("section") - 1
+    spread_deltas = pltpu.VMEM((VOX, 9 * C), BF16)
     return pl.pallas_call(
         functools.partial(tick_kernel, slot),
         in_specs=[VM] * (6 + len(above)),
-        out_specs=[VM] * 3,
-        out_shape=[bricks, bricks, block],
-        scratch_shapes=[pltpu.VMEM((VOX, 9 * C), BF16)],
+        out_specs=[VM] * (3 + last),
+        out_shape=[bricks, bricks, block] + [spread_deltas] * last,
+        scratch_shapes=[] if last else [spread_deltas],
         input_output_aliases={4: 0, 5: 1},
         compiler_params=params(),
         cost_estimate=pl.CostEstimate(flops=1, bytes_accessed=1 << 18, transcendentals=0),
@@ -208,32 +212,13 @@
     )(inputs)
 
 
-def early_kernel(deltas, xt, acc, pd):
-    spread(deltas[0].astype(F32), pd.at[0])
-    total = jnp.dot(xt[0], pd[0], preferred_element_type=F32)
-    spread(deltas[1].astype(F32), pd.at[1])
-    acc[...] = total + jnp.dot(xt[1], pd[1], preferred_element_type=F32)
-
-
-def early_step(deltas, xt):
-    return pl.pallas_call(
-        early_kernel,
-        in_specs=[VM] * 2,
-        out_specs=VM,
-        out_shape=shape((3 * C, 9 * C), F32),
-        scratch_shapes=[pltpu.VMEM((2, VOX, 9 * C), BF16)],
-        compiler_params=params(),
-        cost_estimate=pl.CostEstimate(flops=1, bytes_accessed=1 << 18, transcendentals=0),
-        name="weight_terms_early",
-    )(vmem(deltas), xt)
-
-
-def late_kernel(slot, shares, p_ref, sup_ref, above_ref, deltas, xt, acc_in, *rest):
-    keep, send, (pd, pd_2, acc) = rest[:4], rest[4:8], rest[8:]
+def late_kernel(slot, shares, p_ref, sup_ref, above_ref, deltas, xt, *rest):
+    pds, keep, send, (pd, acc) = rest[:3], rest[3:7], rest[7:11], rest[11:]
     active = working(slot)
     last = WORK - 1
-    spread(deltas[last - 1].astype(F32), pd_2)
-    total = acc_in[...] + jnp.dot(xt[last - 1], pd_2[...], preferred_element_type=F32)
+    total = jnp.dot(xt[0], pds[0][...], preferred_element_type=F32)
+    for brick in range(1, last):
+        total = total + jnp.dot(xt[brick], pds[brick][...], preferred_element_type=F32)
 
     @pl.when(active)
     def _():
@@ -254,19 +239,19 @@
         keep[k][...] = acc[pl.ds(mine, 48), :].astype(BF16)
 
 
-def late_step(slot, shares, preacts, sup, above, deltas, xt, acc):
+def late_step(slot, shares, preacts, sup, above, deltas, xt, pds):
     return pl.pallas_call(
         functools.partial(late_kernel, slot),
-        in_specs=[VM] * 7,
+        in_specs=[VM] * 9,
         out_specs=[VM] * 9,
         out_shape=[shape((48, 9 * C))] * 8 + [shape((VOX, 9 * C))],
-        scratch_shapes=[pltpu.VMEM((VOX, 9 * C), BF16), pltpu.VMEM((3 * C, 9 * C), F32)],
+        scratch_shapes=[pltpu.VMEM((3 * C, 9 * C), F32)],
         compiler_params=params(),
         cost_estimate=pl.CostEstimate(
             flops=4 * VOX * TAPS * C * C, bytes_accessed=7 << 20, transcendentals=0
         ),
         name="weight_terms",
-    )(vmem(shares), vmem(preacts), vmem(sup), above, vmem(deltas), xt, acc)
+    )(vmem(shares), vmem(preacts), vmem(sup), above, vmem(deltas), xt, *pds)
 
 
 def choose(trainer, micro, owner, offset, first, second):
@@ -353,27 +338,26 @@
     )(trainer, stays, arrived, *came, *passed)
 
 
-def finish_kernel(scale, mine, other, out_hbm, out, sems):
+def finish_kernel(scale, *refs):
+    mine, other, (out_hbm, halves, out, sems) = refs[:4], refs[4:8], refs[8:]
     me = lax.axis_index("brick")
-    core = lax.rem(me, 2)
-    label = lax.div(me, 8)
+    core, y = lax.rem(me, 2), lax.div(me, 8)
+    for k in range(4):
+        at = lax.bitwise_xor(y, k)
+        halves[core, at] = mine[k][...]
+        halves[1 - core, at] = other[k][...]
+    size = 9 * C
     copies = []
     for u in range(3):
         for i in range(8):
             group = u * 8 + i
             half, part, row = group // 12, group % 12 // 3, group % 3 * 16
-            at = lax.bitwise_xor(label, part)
-            rows = jnp.where(core == half, mine[at, row : row + 16], other[at, row : row + 16])
-            rows = rows.astype(F32) * scale
+            rows = halves[half, part, row : row + 16].astype(F32) * scale
             for tap in range(9):
                 to = (u * 9 + tap) * C + i * 16
                 out[to : to + 16, :] = rows[:, tap * C : (tap + 1) * C]
-        size = 9 * C
-        copies.append(
-            pltpu.make_async_copy(
-                out.at[u * size : (u + 1) * size], out_hbm.at[u * size : (u + 1) * size], sems.at[u]
-            )
-        )
+        at = slice(u * size, (u + 1) * size)
+        copies.append(pltpu.make_async_copy(out.at[at], out_hbm.at[at], sems.at[u]))
         copies[-1].start()
     for copy in copies:
         copy.wait()
@@ -382,13 +366,17 @@
 def finish_step(scale, mine, other):
     return pl.pallas_call(
         functools.partial(finish_kernel, scale),
-        in_specs=[VM] * 2,
+        in_specs=[VM] * 8,
         out_specs=ANY,
         out_shape=shape((TAPS * C, C), F32),
-        scratch_shapes=[pltpu.VMEM((TAPS * C, C), F32), pltpu.SemaphoreType.DMA((3,))],
+        scratch_shapes=[
+            pltpu.VMEM((2, 4, 48, 9 * C), BF16),
+            pltpu.VMEM((TAPS * C, C), F32),
+            pltpu.SemaphoreType.DMA((3,)),
+        ],
         compiler_params=params(),
         name="finish_weights",
-    )(mine, other)
+    )(*mine, *other)
 
 
 def swap(block, bits):
@@ -411,24 +399,24 @@
     inputs = saved_inputs.reshape(WORK, VOX, C)
     preacts = saved_preacts.reshape(WORK, VOX, C)
     sup = supervision.reshape(WORK, VOX, C)
-    above, came = {}, []
+    above, came, pds = {}, [], []
     gin, deltas, gins, wn, preacts, sup, shares = first_step(counts, preacts, sup, weights[0])
-    xt = transpose_step(inputs)
     for slot in range(slots - 1):
         if slot > 0:
             arrived = [above[slot]] if slot >= WORK else []
-            deltas, gins, gin = tick_step(
+            if slot == WORK + 2:
+                shares, xt = lax.optimization_barrier([shares, transpose_step(inputs)])
+            deltas, gins, gin, *pd = tick_step(
                 slot, shares, preacts, sup, wn, deltas, gins, arrived
             )
+            pds += pd
         sender = layers - 1 - slot // WORK
         if sender > 0:
             above[slot + WORK] = lax.ppermute(gin, "section", [(sender, sender - 1)])
         else:
             came.append(shifted(gin, 2))
-        if slot == slots - 3:
-            acc = early_step(deltas, xt)
     last = slots - 1
-    *halves, pd = late_step(last, shares, preacts, sup, above[last], deltas, xt, acc)
+    *halves, pd = late_step(last, shares, preacts, sup, above[last], deltas, xt, pds)
     keep, send = halves[:4], halves[4:]
     send, came[0] = lax.optimization_barrier([send, came[0]])
     from_core = [swap(block, 1) for block in send]
@@ -445,17 +433,17 @@
     passed = [swap(block, 1) for block in came]
     total, passed = lax.optimization_barrier([total, passed])
     full = total.astype(F32)
-    for bits in Z_BITS:
+    for bits in (6, 2, 4):
         full = full + swap(total, bits).astype(F32)
     full = full.astype(BF16)
     got = [swap(full, bits) for bits in Y_BITS]
     came.append(shifted(gin, 2))
     passed.append(swap(came[3], 1))
-    got, arrived, passed = lax.optimization_barrier([got, arrived, passed])
     skip_grads = slots_step(trainer, stays, arrived, came, passed)
+    got, skip_grads = lax.optimization_barrier([got, skip_grads])
     skip_grads = skip_grads.reshape((1, micros, 4) + saved_inputs.shape[3:])
-    mine = jnp.stack([full] + got)
-    other = swap(mine, 1)
+    mine = [full] + got
+    other = [swap(block, 1) for block in mine]
     scale = 1.0 / math.sqrt(WORK * peers * VOX)
     weight_grads = finish_step(scale, mine, other)
     return skip_grads, weight_grads[None]

time: 75.2 us -> 74.5 us (level)
    ppermute x12, waiting for transfers between devices: 10.3 us -> 11.6 us  [shards(): above[slot + WORK] = lax.ppermute(gin, 'section', [(sender, sender - 1)])]
    ppermute x18 -> x21, waiting for transfers between devices: 5.39 us -> 4.19 us  [swap(): return lax.ppermute(block, 'brick', pairs)]
    ppermute x18 -> x21, starting transfers between devices: 24.8 us -> 25.6 us  [swap(): return lax.ppermute(block, 'brick', pairs)]
    ppermute x1, starting transfers between devices: 4.2 us -> 3.43 us  [shards(): arrived = lax.ppermute(leaves, 'brick', across)]
    pallas_call x3 -> x2, Pallas kernels: 4.59 us -> 4.15 us  [the longest x1 2.79 us: late_step(): pl.pallas_call(functools.partial(late_kernel, slot), in_specs=[VM] * 9, o...]
  transfers between devices with their start and end apart: 35 -> 38, of which waited for: 10 -> 12; matrix products, arithmetic and copies ran while one was open for 0% -> 0% of each run, Pallas kernels for 13% -> 12%
where the time goes in v5:
time: 74.5 us; the launch traced here: 74.2 us
  starting transfers between devices  44.6 us (60%)
  waiting for transfers between devices  15.8 us (21%)
  Pallas kernels  12.1 us (16%)
  between operations  1.2 us (2%)
    ppermute x21, starting transfers between devices, swap(): return lax.ppermute(block, 'brick', pairs)  25.6 us
    ppermute x12, waiting for transfers between devices, shards(): above[slot + WORK] = lax.ppermute(gin, 'section', [(sender, sender - 1)])  11.6 us
    ppermute x12, starting transfers between devices, shards(): above[slot + WORK] = lax.ppermute(gin, 'section', [(sender, sender - 1)])  10.7 us
    ppermute x4, starting transfers between devices, shifted(): lax.ppermute(block, 'brick', [(i, (i + distance) % n) for i in range(n)])  4.93 us
    ppermute x21, waiting for transfers between devices, swap(): return lax.ppermute(block, 'brick', pairs)  4.19 us
    ppermute x1, starting transfers between devices, shards(): arrived = lax.ppermute(leaves, 'brick', across)  3.43 us
    pallas_call x14, Pallas kernels, tick_step(): pl.pallas_call(functools.partial(tick_kernel, slot), in_specs=[VM] * (6 +...  2.98 us
    pallas_call x1, Pallas kernels, late_step(): pl.pallas_call(functools.partial(late_kernel, slot), in_specs=[VM] * 9, o...  2.79 us
  transfers between devices with their start and end apart: 38, of which 12 were waited for; matrix products, arithmetic and copies ran while one was open for 0% of the time, Pallas kernels for 12%

profile of v5, /device:TPU:1, one launch (start us, length us, event | category | flops | bytes accessed | tf_op | source)
XLA Modules:
  0.0 74.2 jit_solution(4666399728348734078)
XLA Ops:
  0.6 1.6 %tick_first.1 = (bf16[512,128]{1,0:T(8,128)(2,1)S(1)}, bf16[4,512,128]{2,1,0:T(8,128)(2,1)S(1)}, bf16[4,512,128]{2,1,0:T(8,128)(2,1)S(1)}, bf16[384,1152]{1,0:T(...) custom-call(s32[2,2]{1,0:T(2,128)} %c_hbm.1, ...), custom_call_target="tpu_custom_call" | custom-call | tf_op jit(solution)/shard_map/tick_first/pallas_call | solution.py:132
  8.6 1.3 %collective-permute-start.9 = (bf16[512,128]{1,0:T(8,128)(2,1)S(1)}, bf16[512,128]{1,0:T(8,128)(2,1)S(1)}, u32[]{:S(2)}, u32[]{:S(2)}) collective-permute-start(bf16[512,128]{1,0:T(8,128)(2,1)S(1)} %get-tuple-element.124), channel_id=1, source_target_pairs={{32,0},{33,1},{34,2},{35,3},{36,4},{37,5},{38,6},{39,7},{40,8},{41... | collective-permute-start | bytes 393224 | tf_op jit(solution)/shard_map/ppermute | solution.py:415
  9.9 1.3 %collective-permute-start.10 = (bf16[512,128]{1,0:T(8,128)(2,1)S(1)}, bf16[512,128]{1,0:T(8,128)(2,1)S(1)}, u32[]{:S(2)}, u32[]{:S(2)}) collective-permute-start(bf16[512,128]{1,0:T(8,128)(2,1)S(1)} %get-tuple-element.127), channel_id=1, source_target_pairs={{32,0},{33,1},{34,2},{35,3},{36,4},{37,5},{38,6},{39,7},{40,8},{41... | collective-permute-start | bytes 393224 | tf_op jit(solution)/shard_map/ppermute | solution.py:415
  11.2 1.3 %collective-permute-start.11 = (bf16[512,128]{1,0:T(8,128)(2,1)S(1)}, bf16[512,128]{1,0:T(8,128)(2,1)S(1)}, u32[]{:S(2)}, u32[]{:S(2)}) collective-permute-start(bf16[512,128]{1,0:T(8,128)(2,1)S(1)} %get-tuple-element.130), channel_id=1, source_target_pairs={{32,0},{33,1},{34,2},{35,3},{36,4},{37,5},{38,6},{39,7},{40,8},{41... | collective-permute-start | bytes 393224 | tf_op jit(solution)/shard_map/ppermute | solution.py:415
  12.6 1.3 %collective-permute-start.8 = (bf16[512,128]{1,0:T(8,128)(2,1)S(1)}, bf16[512,128]{1,0:T(8,128)(2,1)S(1)}, u32[]{:S(2)}, u32[]{:S(2)}) collective-permute-start(bf16[512,128]{1,0:T(8,128)(2,1)S(1)} %get-tuple-element.121), channel_id=1, source_target_pairs={{32,0},{33,1},{34,2},{35,3},{36,4},{37,5},{38,6},{39,7},{40,8},{41... | collective-permute-start | bytes 393224 | tf_op jit(solution)/shard_map/ppermute | solution.py:415
  13.9 6.9 %collective-permute-done.9.rest_2_ = bf16[512,128]{1,0:T(8,128)(2,1)S(1)} collective-permute-done((bf16[512,128]{1,0:T(8,128)(2,1)S(1)}, bf16[512,128]{1,0:T(8,128)(2,1)S(1)}, u32[]{:S(2)}, u32[]{:S(2)}) %collective-permute-start.9) | collective-permute-done | bytes 131104 | tf_op jit(solution)/shard_map/ppermute | solution.py:415
  21.8 1.7 %collective-permute-start.12 = (bf16[512,128]{1,0:T(8,128)(2,1)S(1)}, bf16[512,128]{1,0:T(8,128)(2,1)S(1)}, u32[]{:S(2)}, u32[]{:S(2)}) collective-permute-start(bf16[512,128]{1,0:T(8,128)(2,1)S(1)} %get-tuple-element.141), channel_id=1, source_target_pairs={{0,2},{1,3},{2,4},{3,5},{4,6},{5,7},{6,8},{7,9},{8,10},{9,11},{10,... | collective-permute-start | bytes 393224 | tf_op jit(solution)/shard_map/ppermute | solution.py:389
  23.5 2.3 %collective-permute-done.10.rest_2_ = bf16[512,128]{1,0:T(8,128)(2,1)S(1)} collective-permute-done((bf16[512,128]{1,0:T(8,128)(2,1)S(1)}, bf16[512,128]{1,0:T(8,128)(2,1)S(1)}, u32[]{:S(2)}, u32[]{:S(2)}) %collective-permute-start.10) | collective-permute-done | bytes 131104 | tf_op jit(solution)/shard_map/ppermute | solution.py:415
  26.7 1.9 %collective-permute-start.17 = (bf16[512,128]{1,0:T(8,128)(2,1)S(1)}, bf16[512,128]{1,0:T(8,128)(2,1)S(1)}, u32[]{:S(2)}, u32[]{:S(2)}) collective-permute-start(bf16[512,128]{1,0:T(8,128)(2,1)S(1)} %get-tuple-element.146), channel_id=1, source_target_pairs={{0,2},{1,3},{2,4},{3,5},{4,6},{5,7},{6,8},{7,9},{8,10},{9,11},{10,... | collective-permute-start | bytes 393224 | tf_op jit(solution)/shard_map/ppermute | solution.py:389
  29.5 2.4 %collective-permute-done.8.above_ref = bf16[512,128]{1,0:T(8,128)(2,1)S(1)} collective-permute-done((bf16[512,128]{1,0:T(8,128)(2,1)S(1)}, bf16[512,128]{1,0:T(8,128)(2,1)S(1)}, u32[]{:S(2)}, u32[]{:S(2)}) %collective-permute-start.8) | collective-permute-done | bytes 131104 | tf_op jit(solution)/shard_map/ppermute | solution.py:415
  31.8 2.8 %weight_terms.1 = (bf16[48,1152]{1,0:T(8,128)(2,1)S(1)}, bf16[48,1152]{1,0:T(8,128)(2,1)S(1)}, bf16[48,1152]{1,0:T(8,128)(2,1)S(1)}, bf16[48,1152]{1,0:T(8,128)(...) custom-call(f32[4,8,128]{2,1,0:T(8,128)S(1)} %get-tuple-element.87.s, ...), custom_call_target="tpu_custom_call" | custom-call | flops 905969664 | bytes 7340032 | tf_op jit(solution)/shard_map/weight_terms/pallas_call | solution.py:243
  34.6 2.9 %collective-permute-start.13 = (bf16[48,1152]{1,0:T(8,128)(2,1)S(1)}, bf16[48,1152]{1,0:T(8,128)(2,1)S(1)}, u32[]{:S(2)}, u32[]{:S(2)}) collective-permute-start(bf16[48,1152]{1,0:T(8,128)(2,1)S(1)} %get-tuple-element.142), channel_id=1, source_target_pairs={{0,1},{1,0},{2,3},{3,2},{4,5},{5,4},{6,7},{7,6},{8,9},{9,8},{10,11... | collective-permute-start | bytes 331784 | tf_op jit(solution)/shard_map/ppermute | solution.py:384
  40.0 2.7 %collective-permute-start.19 = (bf16[48,1152]{1,0:T(8,128)(2,1)S(1)}, bf16[48,1152]{1,0:T(8,128)(2,1)S(1)}, u32[]{:S(2)}, u32[]{:S(2)}) collective-permute-start(bf16[48,1152]{1,0:T(8,128)(2,1)S(1)} %add_convert_fusion.3), channel_id=1, source_target_pairs={{0,16},{1,17},{2,18},{3,19},{4,20},{5,21},{6,22},{7,23},{8,24},{9,... | collective-permute-start | bytes 331784 | tf_op jit(solution)/shard_map/ppermute | solution.py:384
  43.6 1.5 %last_grad.1 = (bf16[512,128]{1,0:T(8,128)(2,1)S(1)}, bf16[2,512,128]{2,1,0:T(8,128)(2,1)S(1)}, bf16[2,512,128]{2,1,0:T(8,128)(2,1)S(1)}) custom-call(s32[2,64]{1,0:T(2,128)S(1)} %copy-done.1, bf16[4,512,128]{2,1,0:T(8,128)(2,1)S(1)} %get-tuple-element.158.gins, bf16[512,1152]{1,0:T(8,128)(2,1)S(1)} %get-tuple-element.159.pd, ...), custom_call_target="tpu_custom_call" | custom-call | flops 452984832 | bytes 4194304 | tf_op jit(solution)/shard_map/last_grad/pallas_call | solution.py:284
  46.1 1.8 %collective-permute-start.21 = (bf16[512,128]{1,0:T(8,128)(2,1)S(1)}, bf16[512,128]{1,0:T(8,128)(2,1)S(1)}, u32[]{:S(2)}, u32[]{:S(2)}) collective-permute-start(bf16[512,128]{1,0:T(8,128)(2,1)S(1)} %collective-permute-done.12.refs_0_), channel_id=1, source_target_pairs={{0,1},{1,0},{2,3},{3,2},{4,5},{5,4},{6,7},{7,6},{8,9},{9,8},{10,11... | collective-permute-start | bytes 393224 | tf_op jit(solution)/shard_map/ppermute | solution.py:384
  47.9 1.2 %collective-permute-start.22 = (bf16[512,128]{1,0:T(8,128)(2,1)S(1)}, bf16[512,128]{1,0:T(8,128)(2,1)S(1)}, u32[]{:S(2)}, u32[]{:S(2)}) collective-permute-start(bf16[512,128]{1,0:T(8,128)(2,1)S(1)} %collective-permute-done.17.refs_1_), channel_id=1, source_target_pairs={{0,1},{1,0},{2,3},{3,2},{4,5},{5,4},{6,7},{7,6},{8,9},{9,8},{10,11... | collective-permute-start | bytes 393224 | tf_op jit(solution)/shard_map/ppermute | solution.py:384
  50.3 3.4 %collective-permute-start.27 = (bf16[48,1152]{1,0:T(8,128)(2,1)S(1)}, bf16[48,1152]{1,0:T(8,128)(2,1)S(1)}, u32[]{:S(2)}, u32[]{:S(2)}) collective-permute-start(bf16[48,1152]{1,0:T(8,128)(2,1)S(1)} %add_convert_fusion.1), channel_id=1, source_target_pairs={{0,4},{1,5},{2,6},{3,7},{4,0},{5,1},{6,2},{7,3},{8,12},{9,13},{10,... | collective-permute-start | bytes 331784 | tf_op jit(solution)/shard_map/ppermute | solution.py:384
  53.6 1.4 %collective-permute-start.26 = (bf16[48,1152]{1,0:T(8,128)(2,1)S(1)}, bf16[48,1152]{1,0:T(8,128)(2,1)S(1)}, u32[]{:S(2)}, u32[]{:S(2)}) collective-permute-start(bf16[48,1152]{1,0:T(8,128)(2,1)S(1)} %add_convert_fusion.1), channel_id=1, source_target_pairs={{0,2},{1,3},{2,0},{3,1},{4,6},{5,7},{6,4},{7,5},{8,10},{9,11},{10,... | collective-permute-start | bytes 331784 | tf_op jit(solution)/shard_map/ppermute | solution.py:384
  55.1 3.4 %collective-permute-start.31 = (bf16[2,512,128]{2,1,0:T(8,128)(2,1)S(1)}, bf16[2,512,128]{2,1,0:T(8,128)(2,1)S(1)}, u32[]{:S(2)}, u32[]{:S(2)}) collective-permute-start(bf16[2,512,128]{2,1,0:T(8,128)(2,1)S(1)} %get-tuple-element.161), channel_id=1, source_target_pairs={{0,1},{1,4},{2,3},{3,6},{4,5},{5,8},{6,7},{7,10},{8,9},{9,12},{10,... | collective-permute-start | bytes 786440 | tf_op jit(solution)/shard_map/ppermute | solution.py:426
  60.6 3.1 %collective-permute-start.28 = (bf16[48,1152]{1,0:T(8,128)(2,1)S(1)}, bf16[48,1152]{1,0:T(8,128)(2,1)S(1)}, u32[]{:S(2)}, u32[]{:S(2)}) collective-permute-start(bf16[48,1152]{1,0:T(8,128)(2,1)S(1)} %add_convert_fusion.refs_0_), channel_id=1, source_target_pairs={{0,8},{1,9},{2,10},{3,11},{4,12},{5,13},{6,14},{7,15},{8,0},{9,1},... | collective-permute-start | bytes 331784 | tf_op jit(solution)/shard_map/ppermute | solution.py:384
  63.8 1.6 %slots.1 = bf16[2,4,512,128]{3,2,1,0:T(8,128)(2,1)} custom-call(s32[2,64]{1,0:T(2,128)S(1)} %copy-done.1, bf16[2,512,128]{2,1,0:T(8,128)(2,1)S(1)} %get-tuple-element.160.stays, bf16[2,512,128]{2,1,0:T(8,128)(2,1)S(1)} %collective-permute-done.31.arrived, bf16[512,128]{1,0:T(8,128)(2,1)S(1)} %collective-permute-done.12.refs_0_, ...), custom_call_target="tpu_custom_call" | custom-call | tf_op jit(solution)/shard_map/slots/pallas_call | solution.py:326
  65.3 3.1 %collective-permute-start.34 = (bf16[48,1152]{1,0:T(8,128)(2,1)S(1)}, bf16[48,1152]{1,0:T(8,128)(2,1)S(1)}, u32[]{:S(2)}, u32[]{:S(2)}) collective-permute-start(bf16[48,1152]{1,0:T(8,128)(2,1)S(1)} %add_convert_fusion.refs_0_), channel_id=1, source_target_pairs={{0,1},{1,0},{2,3},{3,2},{4,5},{5,4},{6,7},{7,6},{8,9},{9,8},{10,11... | collective-permute-start | bytes 331784 | tf_op jit(solution)/shard_map/ppermute | solution.py:384
  68.4 2.7 %collective-permute-start.35 = (bf16[48,1152]{1,0:T(8,128)(2,1)S(1)}, bf16[48,1152]{1,0:T(8,128)(2,1)S(1)}, u32[]{:S(2)}, u32[]{:S(2)}) collective-permute-start(bf16[48,1152]{1,0:T(8,128)(2,1)S(1)} %collective-permute-done.28.refs_1_), channel_id=1, source_target_pairs={{0,1},{1,0},{2,3},{3,2},{4,5},{5,4},{6,7},{7,6},{8,9},{9,8},{10,11... | collective-permute-start | bytes 331784 | tf_op jit(solution)/shard_map/ppermute | solution.py:384
  72.7 1.4 %finish_weights.1 = f32[3456,128]{1,0:T(8,128)} custom-call(bf16[48,1152]{1,0:T(8,128)(2,1)S(1)} %add_convert_fusion.refs_0_, bf16[48,1152]{1,0:T(8,128)(2,1)S(1)} %collective-permute-done.28.refs_1_, bf16[48,1152]{1,0:T(8,128)(2,1)S(1)} %collective-permute-done.29.refs_2_, bf16[48,1152]{1,0:T(8,128)(2,1)S(1)} %collective-permute-done.30.refs_3_, ...), custom_call_target="tpu_custom_call" | custom-call | tf_op jit(solution)/shard_map/finish_weights/pallas_call | solution.py:367
  (81 shorter events, 18.1 us)
Async XLA Ops:
  7.1 4.1 %collective-permute-start.6 = (bf16[512,128]{1,0:T(8,128)(2,1)S(1)}, bf16[512,128]{1,0:T(8,128)(2,1)S(1)}, u32[]{:S(2)}, u32[]{:S(2)}) collective-permute-start(bf16[512,128]{1,0:T(8,128)(2,1)S(1)} %get-tuple-element.117), channel_id=1, source_target_pairs={{64,32},{65,33},{66,34},{67,35},{68,36},{69,37},{70,38},{71,39},{7... | collective-permute-start | bytes 393224 | tf_op jit(solution)/shard_map/ppermute | solution.py:415
  7.9 4.7 %collective-permute-start.7 = (bf16[512,128]{1,0:T(8,128)(2,1)S(1)}, bf16[512,128]{1,0:T(8,128)(2,1)S(1)}, u32[]{:S(2)}, u32[]{:S(2)}) collective-permute-start(bf16[512,128]{1,0:T(8,128)(2,1)S(1)} %get-tuple-element.120), channel_id=1, source_target_pairs={{64,32},{65,33},{66,34},{67,35},{68,36},{69,37},{70,38},{71,39},{7... | collective-permute-start | bytes 393224 | tf_op jit(solution)/shard_map/ppermute | solution.py:415
  8.6 12.3 %collective-permute-start.9 = (bf16[512,128]{1,0:T(8,128)(2,1)S(1)}, bf16[512,128]{1,0:T(8,128)(2,1)S(1)}, u32[]{:S(2)}, u32[]{:S(2)}) collective-permute-start(bf16[512,128]{1,0:T(8,128)(2,1)S(1)} %get-tuple-element.124), channel_id=1, source_target_pairs={{32,0},{33,1},{34,2},{35,3},{36,4},{37,5},{38,6},{39,7},{40,8},{41... | collective-permute-start | bytes 393224 | tf_op jit(solution)/shard_map/ppermute | solution.py:415
  9.9 15.8 %collective-permute-start.10 = (bf16[512,128]{1,0:T(8,128)(2,1)S(1)}, bf16[512,128]{1,0:T(8,128)(2,1)S(1)}, u32[]{:S(2)}, u32[]{:S(2)}) collective-permute-start(bf16[512,128]{1,0:T(8,128)(2,1)S(1)} %get-tuple-element.127), channel_id=1, source_target_pairs={{32,0},{33,1},{34,2},{35,3},{36,4},{37,5},{38,6},{39,7},{40,8},{41... | collective-permute-start | bytes 393224 | tf_op jit(solution)/shard_map/ppermute | solution.py:415
  11.2 17.3 %collective-permute-start.11 = (bf16[512,128]{1,0:T(8,128)(2,1)S(1)}, bf16[512,128]{1,0:T(8,128)(2,1)S(1)}, u32[]{:S(2)}, u32[]{:S(2)}) collective-permute-start(bf16[512,128]{1,0:T(8,128)(2,1)S(1)} %get-tuple-element.130), channel_id=1, source_target_pairs={{32,0},{33,1},{34,2},{35,3},{36,4},{37,5},{38,6},{39,7},{40,8},{41... | collective-permute-start | bytes 393224 | tf_op jit(solution)/shard_map/ppermute | solution.py:415
  12.6 19.2 %collective-permute-start.8 = (bf16[512,128]{1,0:T(8,128)(2,1)S(1)}, bf16[512,128]{1,0:T(8,128)(2,1)S(1)}, u32[]{:S(2)}, u32[]{:S(2)}) collective-permute-start(bf16[512,128]{1,0:T(8,128)(2,1)S(1)} %get-tuple-element.121), channel_id=1, source_target_pairs={{32,0},{33,1},{34,2},{35,3},{36,4},{37,5},{38,6},{39,7},{40,8},{41... | collective-permute-start | bytes 393224 | tf_op jit(solution)/shard_map/ppermute | solution.py:415
  21.8 12.9 %collective-permute-start.12 = (bf16[512,128]{1,0:T(8,128)(2,1)S(1)}, bf16[512,128]{1,0:T(8,128)(2,1)S(1)}, u32[]{:S(2)}, u32[]{:S(2)}) collective-permute-start(bf16[512,128]{1,0:T(8,128)(2,1)S(1)} %get-tuple-element.141), channel_id=1, source_target_pairs={{0,2},{1,3},{2,4},{3,5},{4,6},{5,7},{6,8},{7,9},{8,10},{9,11},{10,... | collective-permute-start | bytes 393224 | tf_op jit(solution)/shard_map/ppermute | solution.py:389
  26.7 11.4 %collective-permute-start.17 = (bf16[512,128]{1,0:T(8,128)(2,1)S(1)}, bf16[512,128]{1,0:T(8,128)(2,1)S(1)}, u32[]{:S(2)}, u32[]{:S(2)}) collective-permute-start(bf16[512,128]{1,0:T(8,128)(2,1)S(1)} %get-tuple-element.146), channel_id=1, source_target_pairs={{0,2},{1,3},{2,4},{3,5},{4,6},{5,7},{6,8},{7,9},{8,10},{9,11},{10,... | collective-permute-start | bytes 393224 | tf_op jit(solution)/shard_map/ppermute | solution.py:389
  34.6 3.9 %collective-permute-start.13 = (bf16[48,1152]{1,0:T(8,128)(2,1)S(1)}, bf16[48,1152]{1,0:T(8,128)(2,1)S(1)}, u32[]{:S(2)}, u32[]{:S(2)}) collective-permute-start(bf16[48,1152]{1,0:T(8,128)(2,1)S(1)} %get-tuple-element.142), channel_id=1, source_target_pairs={{0,1},{1,0},{2,3},{3,2},{4,5},{5,4},{6,7},{7,6},{8,9},{9,8},{10,11... | collective-permute-start | bytes 331784 | tf_op jit(solution)/shard_map/ppermute | solution.py:384
  38.1 8.0 %collective-permute-start.23 = (bf16[512,128]{1,0:T(8,128)(2,1)S(1)}, bf16[512,128]{1,0:T(8,128)(2,1)S(1)}, u32[]{:S(2)}, u32[]{:S(2)}) collective-permute-start(bf16[512,128]{1,0:T(8,128)(2,1)S(1)} %get-tuple-element.156), channel_id=1, source_target_pairs={{0,2},{1,3},{2,4},{3,5},{4,6},{5,7},{6,8},{7,9},{8,10},{9,11},{10,... | collective-permute-start | bytes 393224 | tf_op jit(solution)/shard_map/ppermute | solution.py:389
  39.4 8.4 %collective-permute-start.18 = (bf16[48,1152]{1,0:T(8,128)(2,1)S(1)}, bf16[48,1152]{1,0:T(8,128)(2,1)S(1)}, u32[]{:S(2)}, u32[]{:S(2)}) collective-permute-start(bf16[48,1152]{1,0:T(8,128)(2,1)S(1)} %add_convert_fusion.4), channel_id=1, source_target_pairs={{0,8},{1,9},{2,10},{3,11},{4,12},{5,13},{6,14},{7,15},{8,0},{9,1},... | collective-permute-start | bytes 331784 | tf_op jit(solution)/shard_map/ppermute | solution.py:384
  40.0 7.9 %collective-permute-start.19 = (bf16[48,1152]{1,0:T(8,128)(2,1)S(1)}, bf16[48,1152]{1,0:T(8,128)(2,1)S(1)}, u32[]{:S(2)}, u32[]{:S(2)}) collective-permute-start(bf16[48,1152]{1,0:T(8,128)(2,1)S(1)} %add_convert_fusion.3), channel_id=1, source_target_pairs={{0,16},{1,17},{2,18},{3,19},{4,20},{5,21},{6,22},{7,23},{8,24},{9,... | collective-permute-start | bytes 331784 | tf_op jit(solution)/shard_map/ppermute | solution.py:384
  42.8 7.4 %collective-permute-start.20 = (bf16[48,1152]{1,0:T(8,128)(2,1)S(1)}, bf16[48,1152]{1,0:T(8,128)(2,1)S(1)}, u32[]{:S(2)}, u32[]{:S(2)}) collective-permute-start(bf16[48,1152]{1,0:T(8,128)(2,1)S(1)} %add_convert_fusion.2), channel_id=1, source_target_pairs={{0,24},{1,25},{2,26},{3,27},{4,28},{5,29},{6,30},{7,31},{8,16},{9,... | collective-permute-start | bytes 331784 | tf_op jit(solution)/shard_map/ppermute | solution.py:384
  45.1 13.4 %collective-permute-start.32 = (bf16[512,128]{1,0:T(8,128)(2,1)S(1)}, bf16[512,128]{1,0:T(8,128)(2,1)S(1)}, u32[]{:S(2)}, u32[]{:S(2)}) collective-permute-start(bf16[512,128]{1,0:T(8,128)(2,1)S(1)} %get-tuple-element.162), channel_id=1, source_target_pairs={{0,2},{1,3},{2,4},{3,5},{4,6},{5,7},{6,8},{7,9},{8,10},{9,11},{10,... | collective-permute-start | bytes 393224 | tf_op jit(solution)/shard_map/ppermute | solution.py:389
  46.1 4.1 %collective-permute-start.21 = (bf16[512,128]{1,0:T(8,128)(2,1)S(1)}, bf16[512,128]{1,0:T(8,128)(2,1)S(1)}, u32[]{:S(2)}, u32[]{:S(2)}) collective-permute-start(bf16[512,128]{1,0:T(8,128)(2,1)S(1)} %collective-permute-done.12.refs_0_), channel_id=1, source_target_pairs={{0,1},{1,0},{2,3},{3,2},{4,5},{5,4},{6,7},{7,6},{8,9},{9,8},{10,11... | collective-permute-start | bytes 393224 | tf_op jit(solution)/shard_map/ppermute | solution.py:384
  50.3 8.8 %collective-permute-start.27 = (bf16[48,1152]{1,0:T(8,128)(2,1)S(1)}, bf16[48,1152]{1,0:T(8,128)(2,1)S(1)}, u32[]{:S(2)}, u32[]{:S(2)}) collective-permute-start(bf16[48,1152]{1,0:T(8,128)(2,1)S(1)} %add_convert_fusion.1), channel_id=1, source_target_pairs={{0,4},{1,5},{2,6},{3,7},{4,0},{5,1},{6,2},{7,3},{8,12},{9,13},{10,... | collective-permute-start | bytes 331784 | tf_op jit(solution)/shard_map/ppermute | solution.py:384
  53.6 5.7 %collective-permute-start.26 = (bf16[48,1152]{1,0:T(8,128)(2,1)S(1)}, bf16[48,1152]{1,0:T(8,128)(2,1)S(1)}, u32[]{:S(2)}, u32[]{:S(2)}) collective-permute-start(bf16[48,1152]{1,0:T(8,128)(2,1)S(1)} %add_convert_fusion.1), channel_id=1, source_target_pairs={{0,2},{1,3},{2,0},{3,1},{4,6},{5,7},{6,4},{7,5},{8,10},{9,11},{10,... | collective-permute-start | bytes 331784 | tf_op jit(solution)/shard_map/ppermute | solution.py:384
  55.1 5.3 %collective-permute-start.25 = (bf16[48,1152]{1,0:T(8,128)(2,1)S(1)}, bf16[48,1152]{1,0:T(8,128)(2,1)S(1)}, u32[]{:S(2)}, u32[]{:S(2)}) collective-permute-start(bf16[48,1152]{1,0:T(8,128)(2,1)S(1)} %add_convert_fusion.1), channel_id=1, source_target_pairs={{0,6},{1,7},{2,4},{3,5},{4,2},{5,3},{6,0},{7,1},{8,14},{9,15},{10,... | collective-permute-start | bytes 331784 | tf_op jit(solution)/shard_map/ppermute | solution.py:384
  55.1 8.7 %collective-permute-start.31 = (bf16[2,512,128]{2,1,0:T(8,128)(2,1)S(1)}, bf16[2,512,128]{2,1,0:T(8,128)(2,1)S(1)}, u32[]{:S(2)}, u32[]{:S(2)}) collective-permute-start(bf16[2,512,128]{2,1,0:T(8,128)(2,1)S(1)} %get-tuple-element.161), channel_id=1, source_target_pairs={{0,1},{1,4},{2,3},{3,6},{4,5},{5,8},{6,7},{7,10},{8,9},{9,12},{10,... | collective-permute-start | bytes 786440 | tf_op jit(solution)/shard_map/ppermute | solution.py:426
  58.5 5.3 %collective-permute-start.33 = (bf16[512,128]{1,0:T(8,128)(2,1)S(1)}, bf16[512,128]{1,0:T(8,128)(2,1)S(1)}, u32[]{:S(2)}, u32[]{:S(2)}) collective-permute-start(bf16[512,128]{1,0:T(8,128)(2,1)S(1)} %collective-permute-done.32.refs_3_), channel_id=1, source_target_pairs={{0,1},{1,0},{2,3},{3,2},{4,5},{5,4},{6,7},{7,6},{8,9},{9,8},{10,11... | collective-permute-start | bytes 393224 | tf_op jit(solution)/shard_map/ppermute | solution.py:384
  60.4 8.0 %collective-permute-start.30 = (bf16[48,1152]{1,0:T(8,128)(2,1)S(1)}, bf16[48,1152]{1,0:T(8,128)(2,1)S(1)}, u32[]{:S(2)}, u32[]{:S(2)}) collective-permute-start(bf16[48,1152]{1,0:T(8,128)(2,1)S(1)} %add_convert_fusion.refs_0_), channel_id=1, source_target_pairs={{0,24},{1,25},{2,26},{3,27},{4,28},{5,29},{6,30},{7,31},{8,16},{9,... | collective-permute-start | bytes 331784 | tf_op jit(solution)/shard_map/ppermute | solution.py:384
  60.5 7.9 %collective-permute-start.29 = (bf16[48,1152]{1,0:T(8,128)(2,1)S(1)}, bf16[48,1152]{1,0:T(8,128)(2,1)S(1)}, u32[]{:S(2)}, u32[]{:S(2)}) collective-permute-start(bf16[48,1152]{1,0:T(8,128)(2,1)S(1)} %add_convert_fusion.refs_0_), channel_id=1, source_target_pairs={{0,16},{1,17},{2,18},{3,19},{4,20},{5,21},{6,22},{7,23},{8,24},{9,... | collective-permute-start | bytes 331784 | tf_op jit(solution)/shard_map/ppermute | solution.py:384
  60.6 7.8 %collective-permute-start.28 = (bf16[48,1152]{1,0:T(8,128)(2,1)S(1)}, bf16[48,1152]{1,0:T(8,128)(2,1)S(1)}, u32[]{:S(2)}, u32[]{:S(2)}) collective-permute-start(bf16[48,1152]{1,0:T(8,128)(2,1)S(1)} %add_convert_fusion.refs_0_), channel_id=1, source_target_pairs={{0,8},{1,9},{2,10},{3,11},{4,12},{5,13},{6,14},{7,15},{8,0},{9,1},... | collective-permute-start | bytes 331784 | tf_op jit(solution)/shard_map/ppermute | solution.py:384
  65.3 6.4 %collective-permute-start.34 = (bf16[48,1152]{1,0:T(8,128)(2,1)S(1)}, bf16[48,1152]{1,0:T(8,128)(2,1)S(1)}, u32[]{:S(2)}, u32[]{:S(2)}) collective-permute-start(bf16[48,1152]{1,0:T(8,128)(2,1)S(1)} %add_convert_fusion.refs_0_), channel_id=1, source_target_pairs={{0,1},{1,0},{2,3},{3,2},{4,5},{5,4},{6,7},{7,6},{8,9},{9,8},{10,11... | collective-permute-start | bytes 331784 | tf_op jit(solution)/shard_map/ppermute | solution.py:384
  (16 other events, 48.4 us)

commit v6 on v5

--- a/solution.py
+++ b/solution.py
@@ -17,8 +17,8 @@
 ANY = pl.BlockSpec(memory_space=pl.ANY)
 VM = pl.BlockSpec(memory_space=pltpu.VMEM)
 SM = pl.BlockSpec(memory_space=pltpu.SMEM)
-Y_BITS = (8, 16, 24)
-Z_BITS = (2, 4, 6)
+NEAR = (2, 8, 10)
+FAR = (6, 24, 30)
 
 
 def shape(dims, dtype=BF16):
@@ -230,7 +230,7 @@
 
     acc[...] = total + jnp.dot(xt[last], pd[...], preferred_element_type=F32)
     me = lax.axis_index("brick")
-    core, y = lax.rem(me, 2), lax.div(me, 8)
+    core, y = lax.rem(me, 2), label_of(me)
     for k in range(4):
         row = lax.bitwise_xor(y, k) * 48
         mine = pl.multiple_of(core * 192 + row, 16)
@@ -341,7 +341,7 @@
 def finish_kernel(scale, *refs):
     mine, other, (out_hbm, halves, out, sems) = refs[:4], refs[4:8], refs[8:]
     me = lax.axis_index("brick")
-    core, y = lax.rem(me, 2), lax.div(me, 8)
+    core, y = lax.rem(me, 2), label_of(me)
     for k in range(4):
         at = lax.bitwise_xor(y, k)
         halves[core, at] = mine[k][...]
@@ -377,6 +377,12 @@
         compiler_params=params(),
         name="finish_weights",
     )(*mine, *other)
+
+
+def label_of(me):
+    z, y = lax.rem(lax.div(me, 2), 4), lax.div(me, 8)
+    z, y = lax.bitwise_xor(z, lax.div(z, 2)), lax.bitwise_xor(y, lax.div(y, 2))
+    return lax.rem(z, 2) + 2 * lax.rem(y, 2)
 
 
 def swap(block, bits):
@@ -427,16 +433,17 @@
 
     part = [mine.astype(F32) + theirs.astype(F32) for mine, theirs in zip(keep, from_core)]
     total = part[0]
-    for block, bits in zip(part[1:], Y_BITS):
+    for k in (2, 3, 1):
+        block, bits = part[k], NEAR[k - 1]
         total = total + swap(block.astype(BF16), bits).astype(F32)
     total = total.astype(BF16)
     passed = [swap(block, 1) for block in came]
     total, passed = lax.optimization_barrier([total, passed])
     full = total.astype(F32)
-    for bits in (6, 2, 4):
+    for bits in (24, 6, 30):
         full = full + swap(total, bits).astype(F32)
     full = full.astype(BF16)
-    got = [swap(full, bits) for bits in Y_BITS]
+    got = [swap(full, bits) for bits in NEAR]
     came.append(shifted(gin, 2))
     passed.append(swap(came[3], 1))
     skip_grads = slots_step(trainer, stays, arrived, came, passed)

time: 74.5 us -> 73.4 us (0.985); the launches traced: 74.2 us -> 72.1 us
  starting transfers between devices: 44.6 us -> 41.6 us
  waiting for transfers between devices: 15.8 us -> 16.8 us
    ppermute x21, starting transfers between devices: 25.6 us -> 23.1 us  [swap(): return lax.ppermute(block, 'brick', pairs)]
  transfers between devices with their start and end apart: 38 -> 38, of which waited for: 12 -> 16; matrix products, arithmetic and copies ran while one was open for 0% -> 0% of each run, Pallas kernels for 12% -> 13%
where the time goes in v6:
time: 73.4 us; the launch traced here: 72.1 us
  starting transfers between devices  41.6 us (57%)
  waiting for transfers between devices  16.8 us (23%)
  Pallas kernels  12.2 us (17%)
  between operations  1.17 us (2%)
    ppermute x21, starting transfers between devices, swap(): return lax.ppermute(block, 'brick', pairs)  23.1 us
    ppermute x12, waiting for transfers between devices, shards(): above[slot + WORK] = lax.ppermute(gin, 'section', [(sender, sender - 1)])  11.6 us
    ppermute x12, starting transfers between devices, shards(): above[slot + WORK] = lax.ppermute(gin, 'section', [(sender, sender - 1)])  10.7 us
    ppermute x4, starting transfers between devices, shifted(): lax.ppermute(block, 'brick', [(i, (i + distance) % n) for i in range(n)])  4.86 us
    ppermute x21, waiting for transfers between devices, swap(): return lax.ppermute(block, 'brick', pairs)  4.57 us
    pallas_call x14, Pallas kernels, tick_step(): pl.pallas_call(functools.partial(tick_kernel, slot), in_specs=[VM] * (6 +...  2.98 us
    ppermute x1, starting transfers between devices, shards(): arrived = lax.ppermute(leaves, 'brick', across)  2.92 us
    pallas_call x1, Pallas kernels, late_step(): pl.pallas_call(functools.partial(late_kernel, slot), in_specs=[VM] * 9, o...  2.79 us
  transfers between devices with their start and end apart: 38, of which 16 were waited for; matrix products, arithmetic and copies ran while one was open for 0% of the time, Pallas kernels for 13%

profile of v6, /device:TPU:1, one launch (start us, length us, event | category | flops | bytes accessed | tf_op | source)
XLA Modules:
  0.0 72.1 jit_solution(10552363193496033269)
XLA Ops:
  0.6 1.6 %tick_first.1 = (bf16[512,128]{1,0:T(8,128)(2,1)S(1)}, bf16[4,512,128]{2,1,0:T(8,128)(2,1)S(1)}, bf16[4,512,128]{2,1,0:T(8,128)(2,1)S(1)}, bf16[384,1152]{1,0:T(...) custom-call(s32[2,2]{1,0:T(2,128)} %c_hbm.1, ...), custom_call_target="tpu_custom_call" | custom-call | tf_op jit(solution)/shard_map/tick_first/pallas_call | solution.py:132
  8.6 1.3 %collective-permute-start.9 = (bf16[512,128]{1,0:T(8,128)(2,1)S(1)}, bf16[512,128]{1,0:T(8,128)(2,1)S(1)}, u32[]{:S(2)}, u32[]{:S(2)}) collective-permute-start(bf16[512,128]{1,0:T(8,128)(2,1)S(1)} %get-tuple-element.124), channel_id=1, source_target_pairs={{32,0},{33,1},{34,2},{35,3},{36,4},{37,5},{38,6},{39,7},{40,8},{41... | collective-permute-start | bytes 393224 | tf_op jit(solution)/shard_map/ppermute | solution.py:421
  9.9 1.3 %collective-permute-start.10 = (bf16[512,128]{1,0:T(8,128)(2,1)S(1)}, bf16[512,128]{1,0:T(8,128)(2,1)S(1)}, u32[]{:S(2)}, u32[]{:S(2)}) collective-permute-start(bf16[512,128]{1,0:T(8,128)(2,1)S(1)} %get-tuple-element.127), channel_id=1, source_target_pairs={{32,0},{33,1},{34,2},{35,3},{36,4},{37,5},{38,6},{39,7},{40,8},{41... | collective-permute-start | bytes 393224 | tf_op jit(solution)/shard_map/ppermute | solution.py:421
  11.2 1.3 %collective-permute-start.11 = (bf16[512,128]{1,0:T(8,128)(2,1)S(1)}, bf16[512,128]{1,0:T(8,128)(2,1)S(1)}, u32[]{:S(2)}, u32[]{:S(2)}) collective-permute-start(bf16[512,128]{1,0:T(8,128)(2,1)S(1)} %get-tuple-element.130), channel_id=1, source_target_pairs={{32,0},{33,1},{34,2},{35,3},{36,4},{37,5},{38,6},{39,7},{40,8},{41... | collective-permute-start | bytes 393224 | tf_op jit(solution)/shard_map/ppermute | solution.py:421
  12.6 1.3 %collective-permute-start.8 = (bf16[512,128]{1,0:T(8,128)(2,1)S(1)}, bf16[512,128]{1,0:T(8,128)(2,1)S(1)}, u32[]{:S(2)}, u32[]{:S(2)}) collective-permute-start(bf16[512,128]{1,0:T(8,128)(2,1)S(1)} %get-tuple-element.121), channel_id=1, source_target_pairs={{32,0},{33,1},{34,2},{35,3},{36,4},{37,5},{38,6},{39,7},{40,8},{41... | collective-permute-start | bytes 393224 | tf_op jit(solution)/shard_map/ppermute | solution.py:421
  13.9 6.9 %collective-permute-done.9.rest_2_ = bf16[512,128]{1,0:T(8,128)(2,1)S(1)} collective-permute-done((bf16[512,128]{1,0:T(8,128)(2,1)S(1)}, bf16[512,128]{1,0:T(8,128)(2,1)S(1)}, u32[]{:S(2)}, u32[]{:S(2)}) %collective-permute-start.9) | collective-permute-done | bytes 131104 | tf_op jit(solution)/shard_map/ppermute | solution.py:421
  20.8 0.9 %tick12.1 = (bf16[4,512,128]{2,1,0:T(8,128)(2,1)S(1)}, bf16[4,512,128]{2,1,0:T(8,128)(2,1)S(1)}, bf16[512,128]{1,0:T(8,128)(2,1)S(1)}, bf16[512,1152]{1,0:T(8,128)(2,1)S(1)}) custom-call(f32[4,8,128]{2,1,0:T(8,128)S(1)} %get-tuple-element.87.shares, bf16[4,512,128]{2,1,0:T(8,128)(2,1)S(1)} %get-tuple-element.88.p_ref, ...), custom_call_target="tpu_custom_call", output_to_operand_aliasing={{0}: (4, {}), {1}: (5, {})} | custom-call | flops 1 | bytes 262144 | tf_op jit(solution)/shard_map/tick12/pallas_call | solution.py:182
  21.8 1.7 %collective-permute-start.12 = (bf16[512,128]{1,0:T(8,128)(2,1)S(1)}, bf16[512,128]{1,0:T(8,128)(2,1)S(1)}, u32[]{:S(2)}, u32[]{:S(2)}) collective-permute-start(bf16[512,128]{1,0:T(8,128)(2,1)S(1)} %get-tuple-element.141), channel_id=1, source_target_pairs={{0,2},{1,3},{2,4},{3,5},{4,6},{5,7},{6,8},{7,9},{8,10},{9,11},{10,... | collective-permute-start | bytes 393224 | tf_op jit(solution)/shard_map/ppermute | solution.py:395
  23.5 2.3 %collective-permute-done.10.rest_2_ = bf16[512,128]{1,0:T(8,128)(2,1)S(1)} collective-permute-done((bf16[512,128]{1,0:T(8,128)(2,1)S(1)}, bf16[512,128]{1,0:T(8,128)(2,1)S(1)}, u32[]{:S(2)}, u32[]{:S(2)}) %collective-permute-start.10) | collective-permute-done | bytes 131104 | tf_op jit(solution)/shard_map/ppermute | solution.py:421
  26.7 1.9 %collective-permute-start.17 = (bf16[512,128]{1,0:T(8,128)(2,1)S(1)}, bf16[512,128]{1,0:T(8,128)(2,1)S(1)}, u32[]{:S(2)}, u32[]{:S(2)}) collective-permute-start(bf16[512,128]{1,0:T(8,128)(2,1)S(1)} %get-tuple-element.146), channel_id=1, source_target_pairs={{0,2},{1,3},{2,4},{3,5},{4,6},{5,7},{6,8},{7,9},{8,10},{9,11},{10,... | collective-permute-start | bytes 393224 | tf_op jit(solution)/shard_map/ppermute | solution.py:395
  28.5 0.9 %tick14.1 = (bf16[4,512,128]{2,1,0:T(8,128)(2,1)S(1)}, bf16[4,512,128]{2,1,0:T(8,128)(2,1)S(1)}, bf16[512,128]{1,0:T(8,128)(2,1)S(1)}, bf16[512,1152]{1,0:T(8,128)(2,1)S(1)}) custom-call(f32[4,8,128]{2,1,0:T(8,128)S(1)} %get-tuple-element.87.shares, bf16[4,512,128]{2,1,0:T(8,128)(2,1)S(1)} %get-tuple-element.88.p_ref, ...), custom_call_target="tpu_custom_call", output_to_operand_aliasing={{0}: (4, {}), {1}: (5, {})} | custom-call | flops 1 | bytes 262144 | tf_op jit(solution)/shard_map/tick14/pallas_call | solution.py:182
  29.5 2.4 %collective-permute-done.8.above_ref = bf16[512,128]{1,0:T(8,128)(2,1)S(1)} collective-permute-done((bf16[512,128]{1,0:T(8,128)(2,1)S(1)}, bf16[512,128]{1,0:T(8,128)(2,1)S(1)}, u32[]{:S(2)}, u32[]{:S(2)}) %collective-permute-start.8) | collective-permute-done | bytes 131104 | tf_op jit(solution)/shard_map/ppermute | solution.py:421
  31.8 2.8 %weight_terms.1 = (bf16[48,1152]{1,0:T(8,128)(2,1)S(1)}, bf16[48,1152]{1,0:T(8,128)(2,1)S(1)}, bf16[48,1152]{1,0:T(8,128)(2,1)S(1)}, bf16[48,1152]{1,0:T(8,128)(...) custom-call(f32[4,8,128]{2,1,0:T(8,128)S(1)} %get-tuple-element.87.s, ...), custom_call_target="tpu_custom_call" | custom-call | flops 905969664 | bytes 7340032 | tf_op jit(solution)/shard_map/weight_terms/pallas_call | solution.py:243
  34.6 2.9 %collective-permute-start.13 = (bf16[48,1152]{1,0:T(8,128)(2,1)S(1)}, bf16[48,1152]{1,0:T(8,128)(2,1)S(1)}, u32[]{:S(2)}, u32[]{:S(2)}) collective-permute-start(bf16[48,1152]{1,0:T(8,128)(2,1)S(1)} %get-tuple-element.142), channel_id=1, source_target_pairs={{0,1},{1,0},{2,3},{3,2},{4,5},{5,4},{6,7},{7,6},{8,9},{9,8},{10,11... | collective-permute-start | bytes 331784 | tf_op jit(solution)/shard_map/ppermute | solution.py:390
  40.0 1.6 %collective-permute-start.19 = (bf16[48,1152]{1,0:T(8,128)(2,1)S(1)}, bf16[48,1152]{1,0:T(8,128)(2,1)S(1)}, u32[]{:S(2)}, u32[]{:S(2)}) collective-permute-start(bf16[48,1152]{1,0:T(8,128)(2,1)S(1)} %add_convert_fusion.3), channel_id=1, source_target_pairs={{0,10},{1,11},{2,8},{3,9},{4,14},{5,15},{6,12},{7,13},{8,2},{9,3},... | collective-permute-start | bytes 331784 | tf_op jit(solution)/shard_map/ppermute | solution.py:390
  42.4 1.5 %last_grad.1 = (bf16[512,128]{1,0:T(8,128)(2,1)S(1)}, bf16[2,512,128]{2,1,0:T(8,128)(2,1)S(1)}, bf16[2,512,128]{2,1,0:T(8,128)(2,1)S(1)}) custom-call(s32[2,64]{1,0:T(2,128)S(1)} %copy-done.1, bf16[4,512,128]{2,1,0:T(8,128)(2,1)S(1)} %get-tuple-element.158.gins, bf16[512,1152]{1,0:T(8,128)(2,1)S(1)} %get-tuple-element.159.pd, ...), custom_call_target="tpu_custom_call" | custom-call | flops 452984832 | bytes 4194304 | tf_op jit(solution)/shard_map/last_grad/pallas_call | solution.py:284
  45.5 2.4 %collective-permute-start.21 = (bf16[512,128]{1,0:T(8,128)(2,1)S(1)}, bf16[512,128]{1,0:T(8,128)(2,1)S(1)}, u32[]{:S(2)}, u32[]{:S(2)}) collective-permute-start(bf16[512,128]{1,0:T(8,128)(2,1)S(1)} %collective-permute-done.12.refs_0_), channel_id=1, source_target_pairs={{0,1},{1,0},{2,3},{3,2},{4,5},{5,4},{6,7},{7,6},{8,9},{9,8},{10,11... | collective-permute-start | bytes 393224 | tf_op jit(solution)/shard_map/ppermute | solution.py:390
  49.4 4.0 %collective-permute-start.27 = (bf16[48,1152]{1,0:T(8,128)(2,1)S(1)}, bf16[48,1152]{1,0:T(8,128)(2,1)S(1)}, u32[]{:S(2)}, u32[]{:S(2)}) collective-permute-start(bf16[48,1152]{1,0:T(8,128)(2,1)S(1)} %add_convert_fusion.1), channel_id=1, source_target_pairs={{0,30},{1,31},{2,28},{3,29},{4,26},{5,27},{6,24},{7,25},{8,22},{9,... | collective-permute-start | bytes 331784 | tf_op jit(solution)/shard_map/ppermute | solution.py:390
  54.5 2.9 %collective-permute-start.31 = (bf16[2,512,128]{2,1,0:T(8,128)(2,1)S(1)}, bf16[2,512,128]{2,1,0:T(8,128)(2,1)S(1)}, u32[]{:S(2)}, u32[]{:S(2)}) collective-permute-start(bf16[2,512,128]{2,1,0:T(8,128)(2,1)S(1)} %get-tuple-element.161), channel_id=1, source_target_pairs={{0,1},{1,4},{2,3},{3,6},{4,5},{5,8},{6,7},{7,10},{8,9},{9,12},{10,... | collective-permute-start | bytes 786440 | tf_op jit(solution)/shard_map/ppermute | solution.py:432
  57.4 1.3 %collective-permute-done.26 = bf16[48,1152]{1,0:T(8,128)(2,1)S(1)} collective-permute-done((bf16[48,1152]{1,0:T(8,128)(2,1)S(1)}, bf16[48,1152]{1,0:T(8,128)(2,1)S(1)}, u32[]{:S(2)}, u32[]{:S(2)}) %collective-permute-start.26) | collective-permute-done | bytes 110624 | tf_op jit(solution)/shard_map/ppermute | solution.py:390
  59.6 2.3 %collective-permute-start.29 = (bf16[48,1152]{1,0:T(8,128)(2,1)S(1)}, bf16[48,1152]{1,0:T(8,128)(2,1)S(1)}, u32[]{:S(2)}, u32[]{:S(2)}) collective-permute-start(bf16[48,1152]{1,0:T(8,128)(2,1)S(1)} %add_convert_fusion.refs_0_), channel_id=1, source_target_pairs={{0,8},{1,9},{2,10},{3,11},{4,12},{5,13},{6,14},{7,15},{8,0},{9,1},... | collective-permute-start | bytes 331784 | tf_op jit(solution)/shard_map/ppermute | solution.py:390
  61.9 1.6 %slots.1 = bf16[2,4,512,128]{3,2,1,0:T(8,128)(2,1)} custom-call(s32[2,64]{1,0:T(2,128)S(1)} %copy-done.1, bf16[2,512,128]{2,1,0:T(8,128)(2,1)S(1)} %get-tuple-element.160.stays, bf16[2,512,128]{2,1,0:T(8,128)(2,1)S(1)} %collective-permute-done.31.arrived, bf16[512,128]{1,0:T(8,128)(2,1)S(1)} %collective-permute-done.12.refs_0_, ...), custom_call_target="tpu_custom_call" | custom-call | tf_op jit(solution)/shard_map/slots/pallas_call | solution.py:326
  63.5 5.2 %collective-permute-start.34 = (bf16[48,1152]{1,0:T(8,128)(2,1)S(1)}, bf16[48,1152]{1,0:T(8,128)(2,1)S(1)}, u32[]{:S(2)}, u32[]{:S(2)}) collective-permute-start(bf16[48,1152]{1,0:T(8,128)(2,1)S(1)} %add_convert_fusion.refs_0_), channel_id=1, source_target_pairs={{0,1},{1,0},{2,3},{3,2},{4,5},{5,4},{6,7},{7,6},{8,9},{9,8},{10,11... | collective-permute-start | bytes 331784 | tf_op jit(solution)/shard_map/ppermute | solution.py:390
  70.6 1.4 %finish_weights.1 = f32[3456,128]{1,0:T(8,128)} custom-call(bf16[48,1152]{1,0:T(8,128)(2,1)S(1)} %add_convert_fusion.refs_0_, bf16[48,1152]{1,0:T(8,128)(2,1)S(1)} %collective-permute-done.28.refs_1_, bf16[48,1152]{1,0:T(8,128)(2,1)S(1)} %collective-permute-done.29.refs_2_, bf16[48,1152]{1,0:T(8,128)(2,1)S(1)} %collective-permute-done.30.refs_3_, ...), custom_call_target="tpu_custom_call" | custom-call | tf_op jit(solution)/shard_map/finish_weights/pallas_call | solution.py:367
  (81 shorter events, 17.4 us)
Async XLA Ops:
  4.3 3.5 %collective-permute-start.3 = (bf16[512,128]{1,0:T(8,128)(2,1)S(1)}, bf16[512,128]{1,0:T(8,128)(2,1)S(1)}, u32[]{:S(2)}, u32[]{:S(2)}) collective-permute-start(bf16[512,128]{1,0:T(8,128)(2,1)S(1)} %get-tuple-element.108), channel_id=1, source_target_pairs={{96,64},{97,65},{98,66},{99,67},{100,68},{101,69},{102,70},{103,71... | collective-permute-start | bytes 393224 | tf_op jit(solution)/shard_map/ppermute | solution.py:421
  7.1 4.1 %collective-permute-start.6 = (bf16[512,128]{1,0:T(8,128)(2,1)S(1)}, bf16[512,128]{1,0:T(8,128)(2,1)S(1)}, u32[]{:S(2)}, u32[]{:S(2)}) collective-permute-start(bf16[512,128]{1,0:T(8,128)(2,1)S(1)} %get-tuple-element.117), channel_id=1, source_target_pairs={{64,32},{65,33},{66,34},{67,35},{68,36},{69,37},{70,38},{71,39},{7... | collective-permute-start | bytes 393224 | tf_op jit(solution)/shard_map/ppermute | solution.py:421
  7.9 4.7 %collective-permute-start.7 = (bf16[512,128]{1,0:T(8,128)(2,1)S(1)}, bf16[512,128]{1,0:T(8,128)(2,1)S(1)}, u32[]{:S(2)}, u32[]{:S(2)}) collective-permute-start(bf16[512,128]{1,0:T(8,128)(2,1)S(1)} %get-tuple-element.120), channel_id=1, source_target_pairs={{64,32},{65,33},{66,34},{67,35},{68,36},{69,37},{70,38},{71,39},{7... | collective-permute-start | bytes 393224 | tf_op jit(solution)/shard_map/ppermute | solution.py:421
  8.6 12.3 %collective-permute-start.9 = (bf16[512,128]{1,0:T(8,128)(2,1)S(1)}, bf16[512,128]{1,0:T(8,128)(2,1)S(1)}, u32[]{:S(2)}, u32[]{:S(2)}) collective-permute-start(bf16[512,128]{1,0:T(8,128)(2,1)S(1)} %get-tuple-element.124), channel_id=1, source_target_pairs={{32,0},{33,1},{34,2},{35,3},{36,4},{37,5},{38,6},{39,7},{40,8},{41... | collective-permute-start | bytes 393224 | tf_op jit(solution)/shard_map/ppermute | solution.py:421
  9.9 15.8 %collective-permute-start.10 = (bf16[512,128]{1,0:T(8,128)(2,1)S(1)}, bf16[512,128]{1,0:T(8,128)(2,1)S(1)}, u32[]{:S(2)}, u32[]{:S(2)}) collective-permute-start(bf16[512,128]{1,0:T(8,128)(2,1)S(1)} %get-tuple-element.127), channel_id=1, source_target_pairs={{32,0},{33,1},{34,2},{35,3},{36,4},{37,5},{38,6},{39,7},{40,8},{41... | collective-permute-start | bytes 393224 | tf_op jit(solution)/shard_map/ppermute | solution.py:421
  11.2 17.3 %collective-permute-start.11 = (bf16[512,128]{1,0:T(8,128)(2,1)S(1)}, bf16[512,128]{1,0:T(8,128)(2,1)S(1)}, u32[]{:S(2)}, u32[]{:S(2)}) collective-permute-start(bf16[512,128]{1,0:T(8,128)(2,1)S(1)} %get-tuple-element.130), channel_id=1, source_target_pairs={{32,0},{33,1},{34,2},{35,3},{36,4},{37,5},{38,6},{39,7},{40,8},{41... | collective-permute-start | bytes 393224 | tf_op jit(solution)/shard_map/ppermute | solution.py:421
  12.6 19.2 %collective-permute-start.8 = (bf16[512,128]{1,0:T(8,128)(2,1)S(1)}, bf16[512,128]{1,0:T(8,128)(2,1)S(1)}, u32[]{:S(2)}, u32[]{:S(2)}) collective-permute-start(bf16[512,128]{1,0:T(8,128)(2,1)S(1)} %get-tuple-element.121), channel_id=1, source_target_pairs={{32,0},{33,1},{34,2},{35,3},{36,4},{37,5},{38,6},{39,7},{40,8},{41... | collective-permute-start | bytes 393224 | tf_op jit(solution)/shard_map/ppermute | solution.py:421
  21.8 12.9 %collective-permute-start.12 = (bf16[512,128]{1,0:T(8,128)(2,1)S(1)}, bf16[512,128]{1,0:T(8,128)(2,1)S(1)}, u32[]{:S(2)}, u32[]{:S(2)}) collective-permute-start(bf16[512,128]{1,0:T(8,128)(2,1)S(1)} %get-tuple-element.141), channel_id=1, source_target_pairs={{0,2},{1,3},{2,4},{3,5},{4,6},{5,7},{6,8},{7,9},{8,10},{9,11},{10,... | collective-permute-start | bytes 393224 | tf_op jit(solution)/shard_map/ppermute | solution.py:395
  26.7 11.4 %collective-permute-start.17 = (bf16[512,128]{1,0:T(8,128)(2,1)S(1)}, bf16[512,128]{1,0:T(8,128)(2,1)S(1)}, u32[]{:S(2)}, u32[]{:S(2)}) collective-permute-start(bf16[512,128]{1,0:T(8,128)(2,1)S(1)} %get-tuple-element.146), channel_id=1, source_target_pairs={{0,2},{1,3},{2,4},{3,5},{4,6},{5,7},{6,8},{7,9},{8,10},{9,11},{10,... | collective-permute-start | bytes 393224 | tf_op jit(solution)/shard_map/ppermute | solution.py:395
  34.6 3.9 %collective-permute-start.13 = (bf16[48,1152]{1,0:T(8,128)(2,1)S(1)}, bf16[48,1152]{1,0:T(8,128)(2,1)S(1)}, u32[]{:S(2)}, u32[]{:S(2)}) collective-permute-start(bf16[48,1152]{1,0:T(8,128)(2,1)S(1)} %get-tuple-element.142), channel_id=1, source_target_pairs={{0,1},{1,0},{2,3},{3,2},{4,5},{5,4},{6,7},{7,6},{8,9},{9,8},{10,11... | collective-permute-start | bytes 331784 | tf_op jit(solution)/shard_map/ppermute | solution.py:390
  38.1 7.4 %collective-permute-start.23 = (bf16[512,128]{1,0:T(8,128)(2,1)S(1)}, bf16[512,128]{1,0:T(8,128)(2,1)S(1)}, u32[]{:S(2)}, u32[]{:S(2)}) collective-permute-start(bf16[512,128]{1,0:T(8,128)(2,1)S(1)} %get-tuple-element.156), channel_id=1, source_target_pairs={{0,2},{1,3},{2,4},{3,5},{4,6},{5,7},{6,8},{7,9},{8,10},{9,11},{10,... | collective-permute-start | bytes 393224 | tf_op jit(solution)/shard_map/ppermute | solution.py:395
  39.4 8.4 %collective-permute-start.18 = (bf16[48,1152]{1,0:T(8,128)(2,1)S(1)}, bf16[48,1152]{1,0:T(8,128)(2,1)S(1)}, u32[]{:S(2)}, u32[]{:S(2)}) collective-permute-start(bf16[48,1152]{1,0:T(8,128)(2,1)S(1)} %add_convert_fusion.4), channel_id=1, source_target_pairs={{0,8},{1,9},{2,10},{3,11},{4,12},{5,13},{6,14},{7,15},{8,0},{9,1},... | collective-permute-start | bytes 331784 | tf_op jit(solution)/shard_map/ppermute | solution.py:390
  40.0 7.9 %collective-permute-start.19 = (bf16[48,1152]{1,0:T(8,128)(2,1)S(1)}, bf16[48,1152]{1,0:T(8,128)(2,1)S(1)}, u32[]{:S(2)}, u32[]{:S(2)}) collective-permute-start(bf16[48,1152]{1,0:T(8,128)(2,1)S(1)} %add_convert_fusion.3), channel_id=1, source_target_pairs={{0,10},{1,11},{2,8},{3,9},{4,14},{5,15},{6,12},{7,13},{8,2},{9,3},... | collective-permute-start | bytes 331784 | tf_op jit(solution)/shard_map/ppermute | solution.py:390
  41.6 6.7 %collective-permute-start.20 = (bf16[48,1152]{1,0:T(8,128)(2,1)S(1)}, bf16[48,1152]{1,0:T(8,128)(2,1)S(1)}, u32[]{:S(2)}, u32[]{:S(2)}) collective-permute-start(bf16[48,1152]{1,0:T(8,128)(2,1)S(1)} %add_convert_fusion.2), channel_id=1, source_target_pairs={{0,2},{1,3},{2,0},{3,1},{4,6},{5,7},{6,4},{7,5},{8,10},{9,11},{10,... | collective-permute-start | bytes 331784 | tf_op jit(solution)/shard_map/ppermute | solution.py:390
  43.9 13.4 %collective-permute-start.32 = (bf16[512,128]{1,0:T(8,128)(2,1)S(1)}, bf16[512,128]{1,0:T(8,128)(2,1)S(1)}, u32[]{:S(2)}, u32[]{:S(2)}) collective-permute-start(bf16[512,128]{1,0:T(8,128)(2,1)S(1)} %get-tuple-element.162), channel_id=1, source_target_pairs={{0,2},{1,3},{2,4},{3,5},{4,6},{5,7},{6,8},{7,9},{8,10},{9,11},{10,... | collective-permute-start | bytes 393224 | tf_op jit(solution)/shard_map/ppermute | solution.py:395
  49.4 8.0 %collective-permute-start.27 = (bf16[48,1152]{1,0:T(8,128)(2,1)S(1)}, bf16[48,1152]{1,0:T(8,128)(2,1)S(1)}, u32[]{:S(2)}, u32[]{:S(2)}) collective-permute-start(bf16[48,1152]{1,0:T(8,128)(2,1)S(1)} %add_convert_fusion.1), channel_id=1, source_target_pairs={{0,30},{1,31},{2,28},{3,29},{4,26},{5,27},{6,24},{7,25},{8,22},{9,... | collective-permute-start | bytes 331784 | tf_op jit(solution)/shard_map/ppermute | solution.py:390
  53.4 5.3 %collective-permute-start.26 = (bf16[48,1152]{1,0:T(8,128)(2,1)S(1)}, bf16[48,1152]{1,0:T(8,128)(2,1)S(1)}, u32[]{:S(2)}, u32[]{:S(2)}) collective-permute-start(bf16[48,1152]{1,0:T(8,128)(2,1)S(1)} %add_convert_fusion.1), channel_id=1, source_target_pairs={{0,6},{1,7},{2,4},{3,5},{4,2},{5,3},{6,0},{7,1},{8,14},{9,15},{10,... | collective-permute-start | bytes 331784 | tf_op jit(solution)/shard_map/ppermute | solution.py:390
  54.1 4.8 %collective-permute-start.25 = (bf16[48,1152]{1,0:T(8,128)(2,1)S(1)}, bf16[48,1152]{1,0:T(8,128)(2,1)S(1)}, u32[]{:S(2)}, u32[]{:S(2)}) collective-permute-start(bf16[48,1152]{1,0:T(8,128)(2,1)S(1)} %add_convert_fusion.1), channel_id=1, source_target_pairs={{0,24},{1,25},{2,26},{3,27},{4,28},{5,29},{6,30},{7,31},{8,16},{9,... | collective-permute-start | bytes 331784 | tf_op jit(solution)/shard_map/ppermute | solution.py:390
  54.5 7.5 %collective-permute-start.31 = (bf16[2,512,128]{2,1,0:T(8,128)(2,1)S(1)}, bf16[2,512,128]{2,1,0:T(8,128)(2,1)S(1)}, u32[]{:S(2)}, u32[]{:S(2)}) collective-permute-start(bf16[2,512,128]{2,1,0:T(8,128)(2,1)S(1)} %get-tuple-element.161), channel_id=1, source_target_pairs={{0,1},{1,4},{2,3},{3,6},{4,5},{5,8},{6,7},{7,10},{8,9},{9,12},{10,... | collective-permute-start | bytes 786440 | tf_op jit(solution)/shard_map/ppermute | solution.py:432
  57.4 4.5 %collective-permute-start.33 = (bf16[512,128]{1,0:T(8,128)(2,1)S(1)}, bf16[512,128]{1,0:T(8,128)(2,1)S(1)}, u32[]{:S(2)}, u32[]{:S(2)}) collective-permute-start(bf16[512,128]{1,0:T(8,128)(2,1)S(1)} %collective-permute-done.32.refs_3_), channel_id=1, source_target_pairs={{0,1},{1,0},{2,3},{3,2},{4,5},{5,4},{6,7},{7,6},{8,9},{9,8},{10,11... | collective-permute-start | bytes 393224 | tf_op jit(solution)/shard_map/ppermute | solution.py:390
  59.0 9.7 %collective-permute-start.30 = (bf16[48,1152]{1,0:T(8,128)(2,1)S(1)}, bf16[48,1152]{1,0:T(8,128)(2,1)S(1)}, u32[]{:S(2)}, u32[]{:S(2)}) collective-permute-start(bf16[48,1152]{1,0:T(8,128)(2,1)S(1)} %add_convert_fusion.refs_0_), channel_id=1, source_target_pairs={{0,10},{1,11},{2,8},{3,9},{4,14},{5,15},{6,12},{7,13},{8,2},{9,3},... | collective-permute-start | bytes 331784 | tf_op jit(solution)/shard_map/ppermute | solution.py:390
  59.6 9.1 %collective-permute-start.29 = (bf16[48,1152]{1,0:T(8,128)(2,1)S(1)}, bf16[48,1152]{1,0:T(8,128)(2,1)S(1)}, u32[]{:S(2)}, u32[]{:S(2)}) collective-permute-start(bf16[48,1152]{1,0:T(8,128)(2,1)S(1)} %add_convert_fusion.refs_0_), channel_id=1, source_target_pairs={{0,8},{1,9},{2,10},{3,11},{4,12},{5,13},{6,14},{7,15},{8,0},{9,1},... | collective-permute-start | bytes 331784 | tf_op jit(solution)/shard_map/ppermute | solution.py:390
  61.9 6.8 %collective-permute-start.28 = (bf16[48,1152]{1,0:T(8,128)(2,1)S(1)}, bf16[48,1152]{1,0:T(8,128)(2,1)S(1)}, u32[]{:S(2)}, u32[]{:S(2)}) collective-permute-start(bf16[48,1152]{1,0:T(8,128)(2,1)S(1)} %add_convert_fusion.refs_0_), channel_id=1, source_target_pairs={{0,2},{1,3},{2,0},{3,1},{4,6},{5,7},{6,4},{7,5},{8,10},{9,11},{10,... | collective-permute-start | bytes 331784 | tf_op jit(solution)/shard_map/ppermute | solution.py:390
  63.5 6.2 %collective-permute-start.34 = (bf16[48,1152]{1,0:T(8,128)(2,1)S(1)}, bf16[48,1152]{1,0:T(8,128)(2,1)S(1)}, u32[]{:S(2)}, u32[]{:S(2)}) collective-permute-start(bf16[48,1152]{1,0:T(8,128)(2,1)S(1)} %add_convert_fusion.refs_0_), channel_id=1, source_target_pairs={{0,1},{1,0},{2,3},{3,2},{4,5},{5,4},{6,7},{7,6},{8,9},{9,8},{10,11... | collective-permute-start | bytes 331784 | tf_op jit(solution)/shard_map/ppermute | solution.py:390
  (16 other events, 42.8 us)

commit v7 on v6

--- a/solution.py
+++ b/solution.py
@@ -338,45 +338,55 @@
     )(trainer, stays, arrived, *came, *passed)
 
 
-def finish_kernel(scale, *refs):
-    mine, other, (out_hbm, halves, out, sems) = refs[:4], refs[4:8], refs[8:]
+def finish_kernel(scale, other, *refs):
+    pieces, (out_hbm, rows, whole, parts, sems) = refs[:4], refs[-5:]
     me = lax.axis_index("brick")
-    core, y = lax.rem(me, 2), label_of(me)
+    core, label = lax.rem(me, 2), label_of(me)
+    half = 1 - core if other else core
     for k in range(4):
-        at = lax.bitwise_xor(y, k)
-        halves[core, at] = mine[k][...]
-        halves[1 - core, at] = other[k][...]
+        at = pl.multiple_of(lax.bitwise_xor(label, k) * 48, 16)
+        rows[pl.ds(at, 48), :] = pieces[k][...]
     size = 9 * C
-    copies = []
-    for u in range(3):
-        for i in range(8):
-            group = u * 8 + i
-            half, part, row = group // 12, group % 12 // 3, group % 3 * 16
-            rows = halves[half, part, row : row + 16].astype(F32) * scale
-            for tap in range(9):
-                to = (u * 9 + tap) * C + i * 16
-                out[to : to + 16, :] = rows[:, tap * C : (tap + 1) * C]
-        at = slice(u * size, (u + 1) * size)
-        copies.append(pltpu.make_async_copy(out.at[at], out_hbm.at[at], sems.at[u]))
+    to = pl.multiple_of(2 * half * size, size)
+    copies = [pltpu.make_async_copy(whole, out_hbm.at[pl.ds(to, size)], sems.at[9])]
+    for i in range(8):
+        block = rows[pl.ds(pl.multiple_of((i + 4 * half) * 16, 16), 16), :].astype(F32) * scale
+        for tap in range(9):
+            at = tap * C + i * 16
+            whole[at : at + 16, :] = block[:, tap * C : (tap + 1) * C]
+    copies[0].start()
+    for i in range(4):
+        at = pl.multiple_of((i + 8 - 8 * half) * 16, 16)
+        block = rows[pl.ds(at, 16), :].astype(F32) * scale
+        for tap in range(9):
+            parts[tap, i * 16 : (i + 1) * 16, :] = block[:, tap * C : (tap + 1) * C]
+    for tap in range(9):
+        to = pl.multiple_of(size + tap * C + half * 64, 64)
+        copies.append(
+            pltpu.make_async_copy(parts.at[tap], out_hbm.at[pl.ds(to, 64)], sems.at[tap])
+        )
         copies[-1].start()
     for copy in copies:
         copy.wait()
 
 
-def finish_step(scale, mine, other):
-    return pl.pallas_call(
-        functools.partial(finish_kernel, scale),
-        in_specs=[VM] * 8,
+def finish_step(scale, pieces, before=None):
+    other = before is not None
+    return pl.pallas_call(
+        functools.partial(finish_kernel, scale, other),
+        in_specs=[VM] * 4 + [ANY] * other,
         out_specs=ANY,
         out_shape=shape((TAPS * C, C), F32),
         scratch_shapes=[
-            pltpu.VMEM((2, 4, 48, 9 * C), BF16),
-            pltpu.VMEM((TAPS * C, C), F32),
-            pltpu.SemaphoreType.DMA((3,)),
+            pltpu.VMEM((192, 9 * C), BF16),
+            pltpu.VMEM((9 * C, C), F32),
+            pltpu.VMEM((9, 64, C), F32),
+            pltpu.SemaphoreType.DMA((10,)),
         ],
-        compiler_params=params(),
-        name="finish_weights",
-    )(*mine, *other)
+        input_output_aliases={4: 0} if other else {},
+        compiler_params=params(),
+        name="finish_other" if other else "finish_own",
+    )(*pieces, *([before] if other else []))
 
 
 def label_of(me):
@@ -440,10 +450,11 @@
     passed = [swap(block, 1) for block in came]
     total, passed = lax.optimization_barrier([total, passed])
     full = total.astype(F32)
-    for bits in (24, 6, 30):
+    for bits in (24, 30, 6):
         full = full + swap(total, bits).astype(F32)
     full = full.astype(BF16)
-    got = [swap(full, bits) for bits in NEAR]
+    late = {bits: swap(full, bits) for bits in (8, 2, 10)}
+    got = [late[bits] for bits in NEAR]
     came.append(shifted(gin, 2))
     passed.append(swap(came[3], 1))
     skip_grads = slots_step(trainer, stays, arrived, came, passed)
@@ -452,7 +463,7 @@
     mine = [full] + got
     other = [swap(block, 1) for block in mine]
     scale = 1.0 / math.sqrt(WORK * peers * VOX)
-    weight_grads = finish_step(scale, mine, other)
+    weight_grads = finish_step(scale, other, finish_step(scale, mine))
     return skip_grads, weight_grads[None]
 
 

time: 73.4 us -> 73.1 us (level)
  Pallas kernels: 12.2 us -> 13 us
    pallas_call x1 -> x2, Pallas kernels: 1.37 us -> 2.17 us  [finish_step(): pl.pallas_call(functools.partial(finish_kernel, scale, other), in_specs=[...]
    ppermute x21, waiting for transfers between devices: 4.57 us -> 3.82 us  [swap(): return lax.ppermute(block, 'brick', pairs)]
  transfers between devices with their start and end apart: 38 -> 38, of which waited for: 16 -> 12; matrix products, arithmetic and copies ran while one was open for 0% -> 0% of each run, Pallas kernels for 13% -> 14%
where the time goes in v7:
time: 73.1 us; the launch traced here: 71.6 us
  starting transfers between devices  41 us (56%)
  waiting for transfers between devices  16.1 us (22%)
  Pallas kernels  13 us (18%)
  between operations  1.2 us (2%)
    ppermute x21, starting transfers between devices, swap(): return lax.ppermute(block, 'brick', pairs)  22.5 us
    ppermute x12, waiting for transfers between devices, shards(): above[slot + WORK] = lax.ppermute(gin, 'section', [(sender, sender - 1)])  11.6 us
    ppermute x12, starting transfers between devices, shards(): above[slot + WORK] = lax.ppermute(gin, 'section', [(sender, sender - 1)])  10.7 us
    ppermute x4, starting transfers between devices, shifted(): lax.ppermute(block, 'brick', [(i, (i + distance) % n) for i in range(n)])  4.86 us
    ppermute x21, waiting for transfers between devices, swap(): return lax.ppermute(block, 'brick', pairs)  3.82 us
    pallas_call x14, Pallas kernels, tick_step(): pl.pallas_call(functools.partial(tick_kernel, slot), in_specs=[VM] * (6 +...  2.98 us
    ppermute x1, starting transfers between devices, shards(): arrived = lax.ppermute(leaves, 'brick', across)  2.92 us
    pallas_call x1, Pallas kernels, late_step(): pl.pallas_call(functools.partial(late_kernel, slot), in_specs=[VM] * 9, o...  2.79 us
  transfers between devices with their start and end apart: 38, of which 12 were waited for; matrix products, arithmetic and copies ran while one was open for 0% of the time, Pallas kernels for 14%

profile of v7, /device:TPU:1, one launch (start us, length us, event | category | flops | bytes accessed | tf_op | source)
XLA Modules:
  0.0 71.6 jit_solution(16788249949350534114)
XLA Ops:
  0.6 1.6 %tick_first.1 = (bf16[512,128]{1,0:T(8,128)(2,1)S(1)}, bf16[4,512,128]{2,1,0:T(8,128)(2,1)S(1)}, bf16[4,512,128]{2,1,0:T(8,128)(2,1)S(1)}, bf16[384,1152]{1,0:T(...) custom-call(s32[2,2]{1,0:T(2,128)} %c_hbm.1, ...), custom_call_target="tpu_custom_call" | custom-call | tf_op jit(solution)/shard_map/tick_first/pallas_call | solution.py:132
  8.6 1.3 %collective-permute-start.9 = (bf16[512,128]{1,0:T(8,128)(2,1)S(1)}, bf16[512,128]{1,0:T(8,128)(2,1)S(1)}, u32[]{:S(2)}, u32[]{:S(2)}) collective-permute-start(bf16[512,128]{1,0:T(8,128)(2,1)S(1)} %get-tuple-element.124), channel_id=1, source_target_pairs={{32,0},{33,1},{34,2},{35,3},{36,4},{37,5},{38,6},{39,7},{40,8},{41... | collective-permute-start | bytes 393224 | tf_op jit(solution)/shard_map/ppermute | solution.py:431
  9.9 1.3 %collective-permute-start.10 = (bf16[512,128]{1,0:T(8,128)(2,1)S(1)}, bf16[512,128]{1,0:T(8,128)(2,1)S(1)}, u32[]{:S(2)}, u32[]{:S(2)}) collective-permute-start(bf16[512,128]{1,0:T(8,128)(2,1)S(1)} %get-tuple-element.127), channel_id=1, source_target_pairs={{32,0},{33,1},{34,2},{35,3},{36,4},{37,5},{38,6},{39,7},{40,8},{41... | collective-permute-start | bytes 393224 | tf_op jit(solution)/shard_map/ppermute | solution.py:431
  11.2 1.3 %collective-permute-start.11 = (bf16[512,128]{1,0:T(8,128)(2,1)S(1)}, bf16[512,128]{1,0:T(8,128)(2,1)S(1)}, u32[]{:S(2)}, u32[]{:S(2)}) collective-permute-start(bf16[512,128]{1,0:T(8,128)(2,1)S(1)} %get-tuple-element.130), channel_id=1, source_target_pairs={{32,0},{33,1},{34,2},{35,3},{36,4},{37,5},{38,6},{39,7},{40,8},{41... | collective-permute-start | bytes 393224 | tf_op jit(solution)/shard_map/ppermute | solution.py:431
  12.6 1.3 %collective-permute-start.8 = (bf16[512,128]{1,0:T(8,128)(2,1)S(1)}, bf16[512,128]{1,0:T(8,128)(2,1)S(1)}, u32[]{:S(2)}, u32[]{:S(2)}) collective-permute-start(bf16[512,128]{1,0:T(8,128)(2,1)S(1)} %get-tuple-element.121), channel_id=1, source_target_pairs={{32,0},{33,1},{34,2},{35,3},{36,4},{37,5},{38,6},{39,7},{40,8},{41... | collective-permute-start | bytes 393224 | tf_op jit(solution)/shard_map/ppermute | solution.py:431
  13.9 6.9 %collective-permute-done.9.rest_2_ = bf16[512,128]{1,0:T(8,128)(2,1)S(1)} collective-permute-done((bf16[512,128]{1,0:T(8,128)(2,1)S(1)}, bf16[512,128]{1,0:T(8,128)(2,1)S(1)}, u32[]{:S(2)}, u32[]{:S(2)}) %collective-permute-start.9) | collective-permute-done | bytes 131104 | tf_op jit(solution)/shard_map/ppermute | solution.py:431
  21.8 1.7 %collective-permute-start.12 = (bf16[512,128]{1,0:T(8,128)(2,1)S(1)}, bf16[512,128]{1,0:T(8,128)(2,1)S(1)}, u32[]{:S(2)}, u32[]{:S(2)}) collective-permute-start(bf16[512,128]{1,0:T(8,128)(2,1)S(1)} %get-tuple-element.141), channel_id=1, source_target_pairs={{0,2},{1,3},{2,4},{3,5},{4,6},{5,7},{6,8},{7,9},{8,10},{9,11},{10,... | collective-permute-start | bytes 393224 | tf_op jit(solution)/shard_map/ppermute | solution.py:405
  23.5 2.3 %collective-permute-done.10.rest_2_ = bf16[512,128]{1,0:T(8,128)(2,1)S(1)} collective-permute-done((bf16[512,128]{1,0:T(8,128)(2,1)S(1)}, bf16[512,128]{1,0:T(8,128)(2,1)S(1)}, u32[]{:S(2)}, u32[]{:S(2)}) %collective-permute-start.10) | collective-permute-done | bytes 131104 | tf_op jit(solution)/shard_map/ppermute | solution.py:431
  26.7 1.9 %collective-permute-start.17 = (bf16[512,128]{1,0:T(8,128)(2,1)S(1)}, bf16[512,128]{1,0:T(8,128)(2,1)S(1)}, u32[]{:S(2)}, u32[]{:S(2)}) collective-permute-start(bf16[512,128]{1,0:T(8,128)(2,1)S(1)} %get-tuple-element.146), channel_id=1, source_target_pairs={{0,2},{1,3},{2,4},{3,5},{4,6},{5,7},{6,8},{7,9},{8,10},{9,11},{10,... | collective-permute-start | bytes 393224 | tf_op jit(solution)/shard_map/ppermute | solution.py:405
  29.5 2.4 %collective-permute-done.8.above_ref = bf16[512,128]{1,0:T(8,128)(2,1)S(1)} collective-permute-done((bf16[512,128]{1,0:T(8,128)(2,1)S(1)}, bf16[512,128]{1,0:T(8,128)(2,1)S(1)}, u32[]{:S(2)}, u32[]{:S(2)}) %collective-permute-start.8) | collective-permute-done | bytes 131104 | tf_op jit(solution)/shard_map/ppermute | solution.py:431
  31.8 2.8 %weight_terms.1 = (bf16[48,1152]{1,0:T(8,128)(2,1)S(1)}, bf16[48,1152]{1,0:T(8,128)(2,1)S(1)}, bf16[48,1152]{1,0:T(8,128)(2,1)S(1)}, bf16[48,1152]{1,0:T(8,128)(...) custom-call(f32[4,8,128]{2,1,0:T(8,128)S(1)} %get-tuple-element.87.s, ...), custom_call_target="tpu_custom_call" | custom-call | flops 905969664 | bytes 7340032 | tf_op jit(solution)/shard_map/weight_terms/pallas_call | solution.py:243
  34.6 2.9 %collective-permute-start.13 = (bf16[48,1152]{1,0:T(8,128)(2,1)S(1)}, bf16[48,1152]{1,0:T(8,128)(2,1)S(1)}, u32[]{:S(2)}, u32[]{:S(2)}) collective-permute-start(bf16[48,1152]{1,0:T(8,128)(2,1)S(1)} %get-tuple-element.142), channel_id=1, source_target_pairs={{0,1},{1,0},{2,3},{3,2},{4,5},{5,4},{6,7},{7,6},{8,9},{9,8},{10,11... | collective-permute-start | bytes 331784 | tf_op jit(solution)/shard_map/ppermute | solution.py:400
  40.0 1.6 %collective-permute-start.19 = (bf16[48,1152]{1,0:T(8,128)(2,1)S(1)}, bf16[48,1152]{1,0:T(8,128)(2,1)S(1)}, u32[]{:S(2)}, u32[]{:S(2)}) collective-permute-start(bf16[48,1152]{1,0:T(8,128)(2,1)S(1)} %add_convert_fusion.3), channel_id=1, source_target_pairs={{0,10},{1,11},{2,8},{3,9},{4,14},{5,15},{6,12},{7,13},{8,2},{9,3},... | collective-permute-start | bytes 331784 | tf_op jit(solution)/shard_map/ppermute | solution.py:400
  42.4 1.5 %last_grad.1 = (bf16[512,128]{1,0:T(8,128)(2,1)S(1)}, bf16[2,512,128]{2,1,0:T(8,128)(2,1)S(1)}, bf16[2,512,128]{2,1,0:T(8,128)(2,1)S(1)}) custom-call(s32[2,64]{1,0:T(2,128)S(1)} %copy-done.1, bf16[4,512,128]{2,1,0:T(8,128)(2,1)S(1)} %get-tuple-element.158.gins, bf16[512,1152]{1,0:T(8,128)(2,1)S(1)} %get-tuple-element.159.pd, ...), custom_call_target="tpu_custom_call" | custom-call | flops 452984832 | bytes 4194304 | tf_op jit(solution)/shard_map/last_grad/pallas_call | solution.py:284
  45.5 2.4 %collective-permute-start.21 = (bf16[512,128]{1,0:T(8,128)(2,1)S(1)}, bf16[512,128]{1,0:T(8,128)(2,1)S(1)}, u32[]{:S(2)}, u32[]{:S(2)}) collective-permute-start(bf16[512,128]{1,0:T(8,128)(2,1)S(1)} %collective-permute-done.12.refs_0_), channel_id=1, source_target_pairs={{0,1},{1,0},{2,3},{3,2},{4,5},{5,4},{6,7},{7,6},{8,9},{9,8},{10,11... | collective-permute-start | bytes 393224 | tf_op jit(solution)/shard_map/ppermute | solution.py:400
  49.4 1.5 %collective-permute-start.27 = (bf16[48,1152]{1,0:T(8,128)(2,1)S(1)}, bf16[48,1152]{1,0:T(8,128)(2,1)S(1)}, u32[]{:S(2)}, u32[]{:S(2)}) collective-permute-start(bf16[48,1152]{1,0:T(8,128)(2,1)S(1)} %add_convert_fusion.1), channel_id=1, source_target_pairs={{0,6},{1,7},{2,4},{3,5},{4,2},{5,3},{6,0},{7,1},{8,14},{9,15},{10,... | collective-permute-start | bytes 331784 | tf_op jit(solution)/shard_map/ppermute | solution.py:400
  50.9 3.2 %collective-permute-start.26 = (bf16[48,1152]{1,0:T(8,128)(2,1)S(1)}, bf16[48,1152]{1,0:T(8,128)(2,1)S(1)}, u32[]{:S(2)}, u32[]{:S(2)}) collective-permute-start(bf16[48,1152]{1,0:T(8,128)(2,1)S(1)} %add_convert_fusion.1), channel_id=1, source_target_pairs={{0,30},{1,31},{2,28},{3,29},{4,26},{5,27},{6,24},{7,25},{8,22},{9,... | collective-permute-start | bytes 331784 | tf_op jit(solution)/shard_map/ppermute | solution.py:400
  54.5 2.9 %collective-permute-start.31 = (bf16[2,512,128]{2,1,0:T(8,128)(2,1)S(1)}, bf16[2,512,128]{2,1,0:T(8,128)(2,1)S(1)}, u32[]{:S(2)}, u32[]{:S(2)}) collective-permute-start(bf16[2,512,128]{2,1,0:T(8,128)(2,1)S(1)} %get-tuple-element.161), channel_id=1, source_target_pairs={{0,1},{1,4},{2,3},{3,6},{4,5},{5,8},{6,7},{7,10},{8,9},{9,12},{10,... | collective-permute-start | bytes 786440 | tf_op jit(solution)/shard_map/ppermute | solution.py:442
  57.8 1.5 %collective-permute-done.25 = bf16[48,1152]{1,0:T(8,128)(2,1)S(1)} collective-permute-done((bf16[48,1152]{1,0:T(8,128)(2,1)S(1)}, bf16[48,1152]{1,0:T(8,128)(2,1)S(1)}, u32[]{:S(2)}, u32[]{:S(2)}) %collective-permute-start.25) | collective-permute-done | bytes 110624 | tf_op jit(solution)/shard_map/ppermute | solution.py:400
  59.6 1.7 %collective-permute-start.29 = (bf16[48,1152]{1,0:T(8,128)(2,1)S(1)}, bf16[48,1152]{1,0:T(8,128)(2,1)S(1)}, u32[]{:S(2)}, u32[]{:S(2)}) collective-permute-start(bf16[48,1152]{1,0:T(8,128)(2,1)S(1)} %add_convert_fusion.refs_0_), channel_id=1, source_target_pairs={{0,8},{1,9},{2,10},{3,11},{4,12},{5,13},{6,14},{7,15},{8,0},{9,1},... | collective-permute-start | bytes 331784 | tf_op jit(solution)/shard_map/ppermute | solution.py:400
  62.2 1.6 %slots.1 = bf16[2,4,512,128]{3,2,1,0:T(8,128)(2,1)} custom-call(s32[2,64]{1,0:T(2,128)S(1)} %copy-done.1, bf16[2,512,128]{2,1,0:T(8,128)(2,1)S(1)} %get-tuple-element.160.stays, bf16[2,512,128]{2,1,0:T(8,128)(2,1)S(1)} %collective-permute-done.31.arrived, bf16[512,128]{1,0:T(8,128)(2,1)S(1)} %collective-permute-done.12.refs_0_, ...), custom_call_target="tpu_custom_call" | custom-call | tf_op jit(solution)/shard_map/slots/pallas_call | solution.py:326
  63.7 4.4 %collective-permute-start.34 = (bf16[48,1152]{1,0:T(8,128)(2,1)S(1)}, bf16[48,1152]{1,0:T(8,128)(2,1)S(1)}, u32[]{:S(2)}, u32[]{:S(2)}) collective-permute-start(bf16[48,1152]{1,0:T(8,128)(2,1)S(1)} %add_convert_fusion.refs_0_), channel_id=1, source_target_pairs={{0,1},{1,0},{2,3},{3,2},{4,5},{5,4},{6,7},{7,6},{8,9},{9,8},{10,11... | collective-permute-start | bytes 331784 | tf_op jit(solution)/shard_map/ppermute | solution.py:400
  69.3 1.1 %finish_own.1.refs_4_ = f32[3456,128]{1,0:T(8,128)} custom-call(bf16[48,1152]{1,0:T(8,128)(2,1)S(1)} %add_convert_fusion.refs_0_, bf16[48,1152]{1,0:T(8,128)(2,1)S(1)} %collective-permute-done.28.refs_1_, bf16[48,1152]{1,0:T(8,128)(2,1)S(1)} %collective-permute-done.29.refs_2_, bf16[48,1152]{1,0:T(8,128)(2,1)S(1)} %collective-permute-done.30.refs_3_), custom_call_target="tpu_custom_call" | custom-call | tf_op jit(solution)/shard_map/finish_own/pallas_call | solution.py:375
  70.4 1.1 %finish_other.1 = f32[3456,128]{1,0:T(8,128)} custom-call(bf16[48,1152]{1,0:T(8,128)(2,1)S(1)} %collective-permute-done.34.refs_0_, bf16[48,1152]{1,0:T(8,128)(2,1)S(1)} %collective-permute-done.35.refs_1_, bf16[48,1152]{1,0:T(8,128)(2,1)S(1)} %collective-permute-done.36.refs_2_, ...), custom_call_target="tpu_custom_call", output_to_operand_aliasing={{}: (4, {})} | custom-call | tf_op jit(solution)/shard_map/finish_other/pallas_call | solution.py:375
  (82 shorter events, 18.3 us)
Async XLA Ops:
  4.3 3.5 %collective-permute-start.3 = (bf16[512,128]{1,0:T(8,128)(2,1)S(1)}, bf16[512,128]{1,0:T(8,128)(2,1)S(1)}, u32[]{:S(2)}, u32[]{:S(2)}) collective-permute-start(bf16[512,128]{1,0:T(8,128)(2,1)S(1)} %get-tuple-element.108), channel_id=1, source_target_pairs={{96,64},{97,65},{98,66},{99,67},{100,68},{101,69},{102,70},{103,71... | collective-permute-start | bytes 393224 | tf_op jit(solution)/shard_map/ppermute | solution.py:431
  7.1 4.1 %collective-permute-start.6 = (bf16[512,128]{1,0:T(8,128)(2,1)S(1)}, bf16[512,128]{1,0:T(8,128)(2,1)S(1)}, u32[]{:S(2)}, u32[]{:S(2)}) collective-permute-start(bf16[512,128]{1,0:T(8,128)(2,1)S(1)} %get-tuple-element.117), channel_id=1, source_target_pairs={{64,32},{65,33},{66,34},{67,35},{68,36},{69,37},{70,38},{71,39},{7... | collective-permute-start | bytes 393224 | tf_op jit(solution)/shard_map/ppermute | solution.py:431
  7.9 4.7 %collective-permute-start.7 = (bf16[512,128]{1,0:T(8,128)(2,1)S(1)}, bf16[512,128]{1,0:T(8,128)(2,1)S(1)}, u32[]{:S(2)}, u32[]{:S(2)}) collective-permute-start(bf16[512,128]{1,0:T(8,128)(2,1)S(1)} %get-tuple-element.120), channel_id=1, source_target_pairs={{64,32},{65,33},{66,34},{67,35},{68,36},{69,37},{70,38},{71,39},{7... | collective-permute-start | bytes 393224 | tf_op jit(solution)/shard_map/ppermute | solution.py:431
  8.6 12.3 %collective-permute-start.9 = (bf16[512,128]{1,0:T(8,128)(2,1)S(1)}, bf16[512,128]{1,0:T(8,128)(2,1)S(1)}, u32[]{:S(2)}, u32[]{:S(2)}) collective-permute-start(bf16[512,128]{1,0:T(8,128)(2,1)S(1)} %get-tuple-element.124), channel_id=1, source_target_pairs={{32,0},{33,1},{34,2},{35,3},{36,4},{37,5},{38,6},{39,7},{40,8},{41... | collective-permute-start | bytes 393224 | tf_op jit(solution)/shard_map/ppermute | solution.py:431
  9.9 15.8 %collective-permute-start.10 = (bf16[512,128]{1,0:T(8,128)(2,1)S(1)}, bf16[512,128]{1,0:T(8,128)(2,1)S(1)}, u32[]{:S(2)}, u32[]{:S(2)}) collective-permute-start(bf16[512,128]{1,0:T(8,128)(2,1)S(1)} %get-tuple-element.127), channel_id=1, source_target_pairs={{32,0},{33,1},{34,2},{35,3},{36,4},{37,5},{38,6},{39,7},{40,8},{41... | collective-permute-start | bytes 393224 | tf_op jit(solution)/shard_map/ppermute | solution.py:431
  11.2 17.3 %collective-permute-start.11 = (bf16[512,128]{1,0:T(8,128)(2,1)S(1)}, bf16[512,128]{1,0:T(8,128)(2,1)S(1)}, u32[]{:S(2)}, u32[]{:S(2)}) collective-permute-start(bf16[512,128]{1,0:T(8,128)(2,1)S(1)} %get-tuple-element.130), channel_id=1, source_target_pairs={{32,0},{33,1},{34,2},{35,3},{36,4},{37,5},{38,6},{39,7},{40,8},{41... | collective-permute-start | bytes 393224 | tf_op jit(solution)/shard_map/ppermute | solution.py:431
  12.6 19.2 %collective-permute-start.8 = (bf16[512,128]{1,0:T(8,128)(2,1)S(1)}, bf16[512,128]{1,0:T(8,128)(2,1)S(1)}, u32[]{:S(2)}, u32[]{:S(2)}) collective-permute-start(bf16[512,128]{1,0:T(8,128)(2,1)S(1)} %get-tuple-element.121), channel_id=1, source_target_pairs={{32,0},{33,1},{34,2},{35,3},{36,4},{37,5},{38,6},{39,7},{40,8},{41... | collective-permute-start | bytes 393224 | tf_op jit(solution)/shard_map/ppermute | solution.py:431
  21.8 12.9 %collective-permute-start.12 = (bf16[512,128]{1,0:T(8,128)(2,1)S(1)}, bf16[512,128]{1,0:T(8,128)(2,1)S(1)}, u32[]{:S(2)}, u32[]{:S(2)}) collective-permute-start(bf16[512,128]{1,0:T(8,128)(2,1)S(1)} %get-tuple-element.141), channel_id=1, source_target_pairs={{0,2},{1,3},{2,4},{3,5},{4,6},{5,7},{6,8},{7,9},{8,10},{9,11},{10,... | collective-permute-start | bytes 393224 | tf_op jit(solution)/shard_map/ppermute | solution.py:405
  26.7 11.4 %collective-permute-start.17 = (bf16[512,128]{1,0:T(8,128)(2,1)S(1)}, bf16[512,128]{1,0:T(8,128)(2,1)S(1)}, u32[]{:S(2)}, u32[]{:S(2)}) collective-permute-start(bf16[512,128]{1,0:T(8,128)(2,1)S(1)} %get-tuple-element.146), channel_id=1, source_target_pairs={{0,2},{1,3},{2,4},{3,5},{4,6},{5,7},{6,8},{7,9},{8,10},{9,11},{10,... | collective-permute-start | bytes 393224 | tf_op jit(solution)/shard_map/ppermute | solution.py:405
  34.6 3.9 %collective-permute-start.13 = (bf16[48,1152]{1,0:T(8,128)(2,1)S(1)}, bf16[48,1152]{1,0:T(8,128)(2,1)S(1)}, u32[]{:S(2)}, u32[]{:S(2)}) collective-permute-start(bf16[48,1152]{1,0:T(8,128)(2,1)S(1)} %get-tuple-element.142), channel_id=1, source_target_pairs={{0,1},{1,0},{2,3},{3,2},{4,5},{5,4},{6,7},{7,6},{8,9},{9,8},{10,11... | collective-permute-start | bytes 331784 | tf_op jit(solution)/shard_map/ppermute | solution.py:400
  38.1 7.4 %collective-permute-start.23 = (bf16[512,128]{1,0:T(8,128)(2,1)S(1)}, bf16[512,128]{1,0:T(8,128)(2,1)S(1)}, u32[]{:S(2)}, u32[]{:S(2)}) collective-permute-start(bf16[512,128]{1,0:T(8,128)(2,1)S(1)} %get-tuple-element.156), channel_id=1, source_target_pairs={{0,2},{1,3},{2,4},{3,5},{4,6},{5,7},{6,8},{7,9},{8,10},{9,11},{10,... | collective-permute-start | bytes 393224 | tf_op jit(solution)/shard_map/ppermute | solution.py:405
  39.4 8.4 %collective-permute-start.18 = (bf16[48,1152]{1,0:T(8,128)(2,1)S(1)}, bf16[48,1152]{1,0:T(8,128)(2,1)S(1)}, u32[]{:S(2)}, u32[]{:S(2)}) collective-permute-start(bf16[48,1152]{1,0:T(8,128)(2,1)S(1)} %add_convert_fusion.4), channel_id=1, source_target_pairs={{0,8},{1,9},{2,10},{3,11},{4,12},{5,13},{6,14},{7,15},{8,0},{9,1},... | collective-permute-start | bytes 331784 | tf_op jit(solution)/shard_map/ppermute | solution.py:400
  40.0 7.9 %collective-permute-start.19 = (bf16[48,1152]{1,0:T(8,128)(2,1)S(1)}, bf16[48,1152]{1,0:T(8,128)(2,1)S(1)}, u32[]{:S(2)}, u32[]{:S(2)}) collective-permute-start(bf16[48,1152]{1,0:T(8,128)(2,1)S(1)} %add_convert_fusion.3), channel_id=1, source_target_pairs={{0,10},{1,11},{2,8},{3,9},{4,14},{5,15},{6,12},{7,13},{8,2},{9,3},... | collective-permute-start | bytes 331784 | tf_op jit(solution)/shard_map/ppermute | solution.py:400
  41.6 6.7 %collective-permute-start.20 = (bf16[48,1152]{1,0:T(8,128)(2,1)S(1)}, bf16[48,1152]{1,0:T(8,128)(2,1)S(1)}, u32[]{:S(2)}, u32[]{:S(2)}) collective-permute-start(bf16[48,1152]{1,0:T(8,128)(2,1)S(1)} %add_convert_fusion.2), channel_id=1, source_target_pairs={{0,2},{1,3},{2,0},{3,1},{4,6},{5,7},{6,4},{7,5},{8,10},{9,11},{10,... | collective-permute-start | bytes 331784 | tf_op jit(solution)/shard_map/ppermute | solution.py:400
  43.9 13.4 %collective-permute-start.32 = (bf16[512,128]{1,0:T(8,128)(2,1)S(1)}, bf16[512,128]{1,0:T(8,128)(2,1)S(1)}, u32[]{:S(2)}, u32[]{:S(2)}) collective-permute-start(bf16[512,128]{1,0:T(8,128)(2,1)S(1)} %get-tuple-element.162), channel_id=1, source_target_pairs={{0,2},{1,3},{2,4},{3,5},{4,6},{5,7},{6,8},{7,9},{8,10},{9,11},{10,... | collective-permute-start | bytes 393224 | tf_op jit(solution)/shard_map/ppermute | solution.py:405
  49.4 8.0 %collective-permute-start.27 = (bf16[48,1152]{1,0:T(8,128)(2,1)S(1)}, bf16[48,1152]{1,0:T(8,128)(2,1)S(1)}, u32[]{:S(2)}, u32[]{:S(2)}) collective-permute-start(bf16[48,1152]{1,0:T(8,128)(2,1)S(1)} %add_convert_fusion.1), channel_id=1, source_target_pairs={{0,6},{1,7},{2,4},{3,5},{4,2},{5,3},{6,0},{7,1},{8,14},{9,15},{10,... | collective-permute-start | bytes 331784 | tf_op jit(solution)/shard_map/ppermute | solution.py:400
  50.9 6.9 %collective-permute-start.26 = (bf16[48,1152]{1,0:T(8,128)(2,1)S(1)}, bf16[48,1152]{1,0:T(8,128)(2,1)S(1)}, u32[]{:S(2)}, u32[]{:S(2)}) collective-permute-start(bf16[48,1152]{1,0:T(8,128)(2,1)S(1)} %add_convert_fusion.1), channel_id=1, source_target_pairs={{0,30},{1,31},{2,28},{3,29},{4,26},{5,27},{6,24},{7,25},{8,22},{9,... | collective-permute-start | bytes 331784 | tf_op jit(solution)/shard_map/ppermute | solution.py:400
  54.1 5.3 %collective-permute-start.25 = (bf16[48,1152]{1,0:T(8,128)(2,1)S(1)}, bf16[48,1152]{1,0:T(8,128)(2,1)S(1)}, u32[]{:S(2)}, u32[]{:S(2)}) collective-permute-start(bf16[48,1152]{1,0:T(8,128)(2,1)S(1)} %add_convert_fusion.1), channel_id=1, source_target_pairs={{0,24},{1,25},{2,26},{3,27},{4,28},{5,29},{6,30},{7,31},{8,16},{9,... | collective-permute-start | bytes 331784 | tf_op jit(solution)/shard_map/ppermute | solution.py:400
  54.5 7.7 %collective-permute-start.31 = (bf16[2,512,128]{2,1,0:T(8,128)(2,1)S(1)}, bf16[2,512,128]{2,1,0:T(8,128)(2,1)S(1)}, u32[]{:S(2)}, u32[]{:S(2)}) collective-permute-start(bf16[2,512,128]{2,1,0:T(8,128)(2,1)S(1)} %get-tuple-element.161), channel_id=1, source_target_pairs={{0,1},{1,4},{2,3},{3,6},{4,5},{5,8},{6,7},{7,10},{8,9},{9,12},{10,... | collective-permute-start | bytes 786440 | tf_op jit(solution)/shard_map/ppermute | solution.py:442
  57.4 4.8 %collective-permute-start.33 = (bf16[512,128]{1,0:T(8,128)(2,1)S(1)}, bf16[512,128]{1,0:T(8,128)(2,1)S(1)}, u32[]{:S(2)}, u32[]{:S(2)}) collective-permute-start(bf16[512,128]{1,0:T(8,128)(2,1)S(1)} %collective-permute-done.32.refs_3_), channel_id=1, source_target_pairs={{0,1},{1,0},{2,3},{3,2},{4,5},{5,4},{6,7},{7,6},{8,9},{9,8},{10,11... | collective-permute-start | bytes 393224 | tf_op jit(solution)/shard_map/ppermute | solution.py:400
  59.4 8.7 %collective-permute-start.30 = (bf16[48,1152]{1,0:T(8,128)(2,1)S(1)}, bf16[48,1152]{1,0:T(8,128)(2,1)S(1)}, u32[]{:S(2)}, u32[]{:S(2)}) collective-permute-start(bf16[48,1152]{1,0:T(8,128)(2,1)S(1)} %add_convert_fusion.refs_0_), channel_id=1, source_target_pairs={{0,10},{1,11},{2,8},{3,9},{4,14},{5,15},{6,12},{7,13},{8,2},{9,3},... | collective-permute-start | bytes 331784 | tf_op jit(solution)/shard_map/ppermute | solution.py:400
  59.6 8.6 %collective-permute-start.29 = (bf16[48,1152]{1,0:T(8,128)(2,1)S(1)}, bf16[48,1152]{1,0:T(8,128)(2,1)S(1)}, u32[]{:S(2)}, u32[]{:S(2)}) collective-permute-start(bf16[48,1152]{1,0:T(8,128)(2,1)S(1)} %add_convert_fusion.refs_0_), channel_id=1, source_target_pairs={{0,8},{1,9},{2,10},{3,11},{4,12},{5,13},{6,14},{7,15},{8,0},{9,1},... | collective-permute-start | bytes 331784 | tf_op jit(solution)/shard_map/ppermute | solution.py:400
  61.3 6.9 %collective-permute-start.28 = (bf16[48,1152]{1,0:T(8,128)(2,1)S(1)}, bf16[48,1152]{1,0:T(8,128)(2,1)S(1)}, u32[]{:S(2)}, u32[]{:S(2)}) collective-permute-start(bf16[48,1152]{1,0:T(8,128)(2,1)S(1)} %add_convert_fusion.refs_0_), channel_id=1, source_target_pairs={{0,2},{1,3},{2,0},{3,1},{4,6},{5,7},{6,4},{7,5},{8,10},{9,11},{10,... | collective-permute-start | bytes 331784 | tf_op jit(solution)/shard_map/ppermute | solution.py:400
  63.7 6.6 %collective-permute-start.34 = (bf16[48,1152]{1,0:T(8,128)(2,1)S(1)}, bf16[48,1152]{1,0:T(8,128)(2,1)S(1)}, u32[]{:S(2)}, u32[]{:S(2)}) collective-permute-start(bf16[48,1152]{1,0:T(8,128)(2,1)S(1)} %add_convert_fusion.refs_0_), channel_id=1, source_target_pairs={{0,1},{1,0},{2,3},{3,2},{4,5},{5,4},{6,7},{7,6},{8,9},{9,8},{10,11... | collective-permute-start | bytes 331784 | tf_op jit(solution)/shard_map/ppermute | solution.py:400
  (16 other events, 44.1 us)

commit v8 on v7

--- a/solution.py
+++ b/solution.py
@@ -261,37 +261,50 @@
     return jnp.where(trainer[micro, 2 * owner + 1] == to, second, first)
 
 
-def last_kernel(slot, trainer, gins, pd, wn, gin, stays, leaves):
-    active = working(slot)
-
-    @pl.when(active)
+def last_kernel(slot, gins, pd, wn, gin):
+    @pl.when(working(slot))
     def _():
         gin[...] = input_grad(pd[...], wn[...])
 
-    @pl.when(jnp.logical_not(active))
+    @pl.when(jnp.logical_not(working(slot)))
     def _():
         gin[...] = gins[WORK - 1]
 
-    me = lax.axis_index("brick")
-    core = lax.rem(me, 2)
-    for micro in range(2):
-        first, second = gins.at[2 * micro], gins.at[1] if micro == 0 else gin
-        stays[micro] = choose(trainer, micro, me, 0, first[...], second[...])
-        leaves[micro] = choose(trainer, micro, me, 1 + 2 * core, first[...], second[...])
-
-
-def last_step(slot, trainer, gins, pd, wn):
+
+def last_step(slot, gins, pd, wn):
     return pl.pallas_call(
         functools.partial(last_kernel, slot),
-        in_specs=[SM] + [VM] * 3,
-        out_specs=[VM] * 3,
-        out_shape=[shape((VOX, C)), shape((2, VOX, C)), shape((2, VOX, C))],
+        in_specs=[VM] * 3,
+        out_specs=VM,
+        out_shape=shape((VOX, C)),
         compiler_params=params(),
         cost_estimate=pl.CostEstimate(
             flops=2 * VOX * TAPS * C * C, bytes_accessed=4 << 20, transcendentals=0
         ),
         name="last_grad",
-    )(trainer, vmem(gins), pd, vmem(wn))
+    )(vmem(gins), pd, vmem(wn))
+
+
+def select_kernel(trainer, gins, gin, stays, leaves):
+    me = lax.axis_index("brick")
+    core = lax.rem(me, 2)
+    for micro in range(2):
+        first = gins[2 * micro]
+        second = gins[1] if micro == 0 else gin[...]
+        stays[micro] = choose(trainer, micro, me, 0, first, second)
+        leaves[micro] = choose(trainer, micro, me, 1 + 2 * core, first, second)
+
+
+def select_step(trainer, gins, gin):
+    return pl.pallas_call(
+        select_kernel,
+        in_specs=[SM] + [VM] * 2,
+        out_specs=[VM] * 2,
+        out_shape=[shape((2, VOX, C))] * 2,
+        compiler_params=params(),
+        cost_estimate=pl.CostEstimate(flops=1, bytes_accessed=1 << 20, transcendentals=0),
+        name="select",
+    )(trainer, vmem(gins), gin)
 
 
 def slots_kernel(trainer, stays, arrived, *refs):
@@ -436,7 +449,8 @@
     keep, send = halves[:4], halves[4:]
     send, came[0] = lax.optimization_barrier([send, came[0]])
     from_core = [swap(block, 1) for block in send]
-    gin, stays, leaves = last_step(last, trainer, gins, pd, wn)
+    gin = last_step(last, gins, pd, wn)
+    stays, leaves = select_step(trainer, gins, gin)
     from_core, came[1] = lax.optimization_barrier([from_core, came[1]])
     across = [(i, (i + 1 + 2 * (i % 2)) % peers) for i in range(peers)]
     arrived = lax.ppermute(leaves, "brick", across)

time: 73.1 us -> 73.1 us (level)
    ppermute x21, waiting for transfers between devices: 3.82 us -> 3.03 us  [swap(): return lax.ppermute(block, 'brick', pairs)]
    pallas_call x1 -> x2, Pallas kernels: 1.53 us -> 1.52 us  [the longest x1 0.82 us: last_step(): pl.pallas_call(functools.partial(last_kernel, slot), in_specs=[VM] * 3, o...]
  transfers between devices with their start and end apart: 38 -> 38, of which waited for: 12 -> 11; matrix products, arithmetic and copies ran while one was open for 0% -> 0% of each run, Pallas kernels for 14% -> 14%
where the time goes in v8:
time: 73.1 us; the launch traced here: 71.8 us
  starting transfers between devices  41.2 us (56%)
  waiting for transfers between devices  16 us (22%)
  Pallas kernels  12.9 us (18%)
  between operations  1.22 us (2%)
    ppermute x21, starting transfers between devices, swap(): return lax.ppermute(block, 'brick', pairs)  22.7 us
    ppermute x12, waiting for transfers between devices, shards(): above[slot + WORK] = lax.ppermute(gin, 'section', [(sender, sender - 1)])  11.6 us
    ppermute x12, starting transfers between devices, shards(): above[slot + WORK] = lax.ppermute(gin, 'section', [(sender, sender - 1)])  10.7 us
    ppermute x4, starting transfers between devices, shifted(): lax.ppermute(block, 'brick', [(i, (i + distance) % n) for i in range(n)])  4.86 us
    ppermute x21, waiting for transfers between devices, swap(): return lax.ppermute(block, 'brick', pairs)  3.03 us
    ppermute x1, starting transfers between devices, shards(): arrived = lax.ppermute(leaves, 'brick', across)  2.99 us
    pallas_call x14, Pallas kernels, tick_step(): pl.pallas_call(functools.partial(tick_kernel, slot), in_specs=[VM] * (6 +...  2.97 us
    pallas_call x1, Pallas kernels, late_step(): pl.pallas_call(functools.partial(late_kernel, slot), in_specs=[VM] * 9, o...  2.79 us
  transfers between devices with their start and end apart: 38, of which 11 were waited for; matrix products, arithmetic and copies ran while one was open for 0% of the time, Pallas kernels for 14%

profile of v8, /device:TPU:1, one launch (start us, length us, event | category | flops | bytes accessed | tf_op | source)
XLA Modules:
  0.0 71.8 jit_solution(2821148593662557378)
XLA Ops:
  0.6 1.6 %tick_first.1 = (bf16[512,128]{1,0:T(8,128)(2,1)S(1)}, bf16[4,512,128]{2,1,0:T(8,128)(2,1)S(1)}, bf16[4,512,128]{2,1,0:T(8,128)(2,1)S(1)}, bf16[384,1152]{1,0:T(...) custom-call(s32[2,2]{1,0:T(2,128)} %c_hbm.1, ...), custom_call_target="tpu_custom_call" | custom-call | tf_op jit(solution)/shard_map/tick_first/pallas_call | solution.py:132
  8.6 1.3 %collective-permute-start.9 = (bf16[512,128]{1,0:T(8,128)(2,1)S(1)}, bf16[512,128]{1,0:T(8,128)(2,1)S(1)}, u32[]{:S(2)}, u32[]{:S(2)}) collective-permute-start(bf16[512,128]{1,0:T(8,128)(2,1)S(1)} %get-tuple-element.123), channel_id=1, source_target_pairs={{32,0},{33,1},{34,2},{35,3},{36,4},{37,5},{38,6},{39,7},{40,8},{41... | collective-permute-start | bytes 393224 | tf_op jit(solution)/shard_map/ppermute | solution.py:444
  9.9 1.3 %collective-permute-start.10 = (bf16[512,128]{1,0:T(8,128)(2,1)S(1)}, bf16[512,128]{1,0:T(8,128)(2,1)S(1)}, u32[]{:S(2)}, u32[]{:S(2)}) collective-permute-start(bf16[512,128]{1,0:T(8,128)(2,1)S(1)} %get-tuple-element.126), channel_id=1, source_target_pairs={{32,0},{33,1},{34,2},{35,3},{36,4},{37,5},{38,6},{39,7},{40,8},{41... | collective-permute-start | bytes 393224 | tf_op jit(solution)/shard_map/ppermute | solution.py:444
  11.2 1.3 %collective-permute-start.11 = (bf16[512,128]{1,0:T(8,128)(2,1)S(1)}, bf16[512,128]{1,0:T(8,128)(2,1)S(1)}, u32[]{:S(2)}, u32[]{:S(2)}) collective-permute-start(bf16[512,128]{1,0:T(8,128)(2,1)S(1)} %get-tuple-element.129), channel_id=1, source_target_pairs={{32,0},{33,1},{34,2},{35,3},{36,4},{37,5},{38,6},{39,7},{40,8},{41... | collective-permute-start | bytes 393224 | tf_op jit(solution)/shard_map/ppermute | solution.py:444
  12.6 1.3 %collective-permute-start.8 = (bf16[512,128]{1,0:T(8,128)(2,1)S(1)}, bf16[512,128]{1,0:T(8,128)(2,1)S(1)}, u32[]{:S(2)}, u32[]{:S(2)}) collective-permute-start(bf16[512,128]{1,0:T(8,128)(2,1)S(1)} %get-tuple-element.120), channel_id=1, source_target_pairs={{32,0},{33,1},{34,2},{35,3},{36,4},{37,5},{38,6},{39,7},{40,8},{41... | collective-permute-start | bytes 393224 | tf_op jit(solution)/shard_map/ppermute | solution.py:444
  13.9 6.9 %collective-permute-done.9.rest_2_ = bf16[512,128]{1,0:T(8,128)(2,1)S(1)} collective-permute-done((bf16[512,128]{1,0:T(8,128)(2,1)S(1)}, bf16[512,128]{1,0:T(8,128)(2,1)S(1)}, u32[]{:S(2)}, u32[]{:S(2)}) %collective-permute-start.9) | collective-permute-done | bytes 131104 | tf_op jit(solution)/shard_map/ppermute | solution.py:444
  21.8 1.7 %collective-permute-start.12 = (bf16[512,128]{1,0:T(8,128)(2,1)S(1)}, bf16[512,128]{1,0:T(8,128)(2,1)S(1)}, u32[]{:S(2)}, u32[]{:S(2)}) collective-permute-start(bf16[512,128]{1,0:T(8,128)(2,1)S(1)} %get-tuple-element.140), channel_id=1, source_target_pairs={{0,2},{1,3},{2,4},{3,5},{4,6},{5,7},{6,8},{7,9},{8,10},{9,11},{10,... | collective-permute-start | bytes 393224 | tf_op jit(solution)/shard_map/ppermute | solution.py:418
  23.5 2.3 %collective-permute-done.10.rest_2_ = bf16[512,128]{1,0:T(8,128)(2,1)S(1)} collective-permute-done((bf16[512,128]{1,0:T(8,128)(2,1)S(1)}, bf16[512,128]{1,0:T(8,128)(2,1)S(1)}, u32[]{:S(2)}, u32[]{:S(2)}) %collective-permute-start.10) | collective-permute-done | bytes 131104 | tf_op jit(solution)/shard_map/ppermute | solution.py:444
  26.7 1.9 %collective-permute-start.17 = (bf16[512,128]{1,0:T(8,128)(2,1)S(1)}, bf16[512,128]{1,0:T(8,128)(2,1)S(1)}, u32[]{:S(2)}, u32[]{:S(2)}) collective-permute-start(bf16[512,128]{1,0:T(8,128)(2,1)S(1)} %get-tuple-element.145), channel_id=1, source_target_pairs={{0,2},{1,3},{2,4},{3,5},{4,6},{5,7},{6,8},{7,9},{8,10},{9,11},{10,... | collective-permute-start | bytes 393224 | tf_op jit(solution)/shard_map/ppermute | solution.py:418
  29.5 2.4 %collective-permute-done.8.above_ref = bf16[512,128]{1,0:T(8,128)(2,1)S(1)} collective-permute-done((bf16[512,128]{1,0:T(8,128)(2,1)S(1)}, bf16[512,128]{1,0:T(8,128)(2,1)S(1)}, u32[]{:S(2)}, u32[]{:S(2)}) %collective-permute-start.8) | collective-permute-done | bytes 131104 | tf_op jit(solution)/shard_map/ppermute | solution.py:444
  31.8 2.8 %weight_terms.1 = (bf16[48,1152]{1,0:T(8,128)(2,1)S(1)}, bf16[48,1152]{1,0:T(8,128)(2,1)S(1)}, bf16[48,1152]{1,0:T(8,128)(2,1)S(1)}, bf16[48,1152]{1,0:T(8,128)(...) custom-call(f32[4,8,128]{2,1,0:T(8,128)S(1)} %get-tuple-element.86.s, ...), custom_call_target="tpu_custom_call" | custom-call | flops 905969664 | bytes 7340032 | tf_op jit(solution)/shard_map/weight_terms/pallas_call | solution.py:243
  34.6 2.9 %collective-permute-start.13 = (bf16[48,1152]{1,0:T(8,128)(2,1)S(1)}, bf16[48,1152]{1,0:T(8,128)(2,1)S(1)}, u32[]{:S(2)}, u32[]{:S(2)}) collective-permute-start(bf16[48,1152]{1,0:T(8,128)(2,1)S(1)} %get-tuple-element.141), channel_id=1, source_target_pairs={{0,1},{1,0},{2,3},{3,2},{4,5},{5,4},{6,7},{7,6},{8,9},{9,8},{10,11... | collective-permute-start | bytes 331784 | tf_op jit(solution)/shard_map/ppermute | solution.py:413
  40.0 1.6 %collective-permute-start.19 = (bf16[48,1152]{1,0:T(8,128)(2,1)S(1)}, bf16[48,1152]{1,0:T(8,128)(2,1)S(1)}, u32[]{:S(2)}, u32[]{:S(2)}) collective-permute-start(bf16[48,1152]{1,0:T(8,128)(2,1)S(1)} %add_convert_fusion.3), channel_id=1, source_target_pairs={{0,10},{1,11},{2,8},{3,9},{4,14},{5,15},{6,12},{7,13},{8,2},{9,3},... | collective-permute-start | bytes 331784 | tf_op jit(solution)/shard_map/ppermute | solution.py:413
  44.1 1.4 %collective-permute-done.23.refs_2_ = bf16[512,128]{1,0:T(8,128)(2,1)S(1)} collective-permute-done((bf16[512,128]{1,0:T(8,128)(2,1)S(1)}, bf16[512,128]{1,0:T(8,128)(2,1)S(1)}, u32[]{:S(2)}, u32[]{:S(2)}) %collective-permute-start.23) | collective-permute-done | bytes 131104 | tf_op jit(solution)/shard_map/ppermute | solution.py:418
  45.5 2.4 %collective-permute-start.21 = (bf16[512,128]{1,0:T(8,128)(2,1)S(1)}, bf16[512,128]{1,0:T(8,128)(2,1)S(1)}, u32[]{:S(2)}, u32[]{:S(2)}) collective-permute-start(bf16[512,128]{1,0:T(8,128)(2,1)S(1)} %collective-permute-done.12.refs_0_), channel_id=1, source_target_pairs={{0,1},{1,0},{2,3},{3,2},{4,5},{5,4},{6,7},{7,6},{8,9},{9,8},{10,11... | collective-permute-start | bytes 393224 | tf_op jit(solution)/shard_map/ppermute | solution.py:413
  49.4 1.5 %collective-permute-start.27 = (bf16[48,1152]{1,0:T(8,128)(2,1)S(1)}, bf16[48,1152]{1,0:T(8,128)(2,1)S(1)}, u32[]{:S(2)}, u32[]{:S(2)}) collective-permute-start(bf16[48,1152]{1,0:T(8,128)(2,1)S(1)} %add_convert_fusion.1), channel_id=1, source_target_pairs={{0,6},{1,7},{2,4},{3,5},{4,2},{5,3},{6,0},{7,1},{8,14},{9,15},{10,... | collective-permute-start | bytes 331784 | tf_op jit(solution)/shard_map/ppermute | solution.py:413
  50.9 3.2 %collective-permute-start.26 = (bf16[48,1152]{1,0:T(8,128)(2,1)S(1)}, bf16[48,1152]{1,0:T(8,128)(2,1)S(1)}, u32[]{:S(2)}, u32[]{:S(2)}) collective-permute-start(bf16[48,1152]{1,0:T(8,128)(2,1)S(1)} %add_convert_fusion.1), channel_id=1, source_target_pairs={{0,30},{1,31},{2,28},{3,29},{4,26},{5,27},{6,24},{7,25},{8,22},{9,... | collective-permute-start | bytes 331784 | tf_op jit(solution)/shard_map/ppermute | solution.py:413
  55.2 3.0 %collective-permute-start.31 = (bf16[2,512,128]{2,1,0:T(8,128)(2,1)S(1)}, bf16[2,512,128]{2,1,0:T(8,128)(2,1)S(1)}, u32[]{:S(2)}, u32[]{:S(2)}) collective-permute-start(bf16[2,512,128]{2,1,0:T(8,128)(2,1)S(1)} %get-tuple-element.160), channel_id=1, source_target_pairs={{0,1},{1,4},{2,3},{3,6},{4,5},{5,8},{6,7},{7,10},{8,9},{9,12},{10,... | collective-permute-start | bytes 786440 | tf_op jit(solution)/shard_map/ppermute | solution.py:456
  58.2 1.2 %collective-permute-done.25 = bf16[48,1152]{1,0:T(8,128)(2,1)S(1)} collective-permute-done((bf16[48,1152]{1,0:T(8,128)(2,1)S(1)}, bf16[48,1152]{1,0:T(8,128)(2,1)S(1)}, u32[]{:S(2)}, u32[]{:S(2)}) %collective-permute-start.25) | collective-permute-done | bytes 110624 | tf_op jit(solution)/shard_map/ppermute | solution.py:413
  59.6 1.7 %collective-permute-start.29 = (bf16[48,1152]{1,0:T(8,128)(2,1)S(1)}, bf16[48,1152]{1,0:T(8,128)(2,1)S(1)}, u32[]{:S(2)}, u32[]{:S(2)}) collective-permute-start(bf16[48,1152]{1,0:T(8,128)(2,1)S(1)} %add_convert_fusion.refs_0_), channel_id=1, source_target_pairs={{0,8},{1,9},{2,10},{3,11},{4,12},{5,13},{6,14},{7,15},{8,0},{9,1},... | collective-permute-start | bytes 331784 | tf_op jit(solution)/shard_map/ppermute | solution.py:413
  62.2 1.6 %slots.1 = bf16[2,4,512,128]{3,2,1,0:T(8,128)(2,1)} custom-call(s32[2,64]{1,0:T(2,128)S(1)} %copy-done.1, bf16[2,512,128]{2,1,0:T(8,128)(2,1)S(1)} %get-tuple-element.159.stays, bf16[2,512,128]{2,1,0:T(8,128)(2,1)S(1)} %collective-permute-done.31.arrived, bf16[512,128]{1,0:T(8,128)(2,1)S(1)} %collective-permute-done.12.refs_0_, ...), custom_call_target="tpu_custom_call" | custom-call | tf_op jit(solution)/shard_map/slots/pallas_call | solution.py:339
  63.7 4.6 %collective-permute-start.34 = (bf16[48,1152]{1,0:T(8,128)(2,1)S(1)}, bf16[48,1152]{1,0:T(8,128)(2,1)S(1)}, u32[]{:S(2)}, u32[]{:S(2)}) collective-permute-start(bf16[48,1152]{1,0:T(8,128)(2,1)S(1)} %add_convert_fusion.refs_0_), channel_id=1, source_target_pairs={{0,1},{1,0},{2,3},{3,2},{4,5},{5,4},{6,7},{7,6},{8,9},{9,8},{10,11... | collective-permute-start | bytes 331784 | tf_op jit(solution)/shard_map/ppermute | solution.py:413
  69.4 1.1 %finish_own.1.refs_4_ = f32[3456,128]{1,0:T(8,128)} custom-call(bf16[48,1152]{1,0:T(8,128)(2,1)S(1)} %add_convert_fusion.refs_0_, bf16[48,1152]{1,0:T(8,128)(2,1)S(1)} %collective-permute-done.28.refs_1_, bf16[48,1152]{1,0:T(8,128)(2,1)S(1)} %collective-permute-done.29.refs_2_, bf16[48,1152]{1,0:T(8,128)(2,1)S(1)} %collective-permute-done.30.refs_3_), custom_call_target="tpu_custom_call" | custom-call | tf_op jit(solution)/shard_map/finish_own/pallas_call | solution.py:388
  70.5 1.1 %finish_other.1 = f32[3456,128]{1,0:T(8,128)} custom-call(bf16[48,1152]{1,0:T(8,128)(2,1)S(1)} %collective-permute-done.34.refs_0_, bf16[48,1152]{1,0:T(8,128)(2,1)S(1)} %collective-permute-done.35.refs_1_, bf16[48,1152]{1,0:T(8,128)(2,1)S(1)} %collective-permute-done.36.refs_2_, ...), custom_call_target="tpu_custom_call", output_to_operand_aliasing={{}: (4, {})} | custom-call | tf_op jit(solution)/shard_map/finish_other/pallas_call | solution.py:388
  (83 shorter events, 18.7 us)
Async XLA Ops:
  4.3 3.5 %collective-permute-start.3 = (bf16[512,128]{1,0:T(8,128)(2,1)S(1)}, bf16[512,128]{1,0:T(8,128)(2,1)S(1)}, u32[]{:S(2)}, u32[]{:S(2)}) collective-permute-start(bf16[512,128]{1,0:T(8,128)(2,1)S(1)} %get-tuple-element.107), channel_id=1, source_target_pairs={{96,64},{97,65},{98,66},{99,67},{100,68},{101,69},{102,70},{103,71... | collective-permute-start | bytes 393224 | tf_op jit(solution)/shard_map/ppermute | solution.py:444
  7.1 4.1 %collective-permute-start.6 = (bf16[512,128]{1,0:T(8,128)(2,1)S(1)}, bf16[512,128]{1,0:T(8,128)(2,1)S(1)}, u32[]{:S(2)}, u32[]{:S(2)}) collective-permute-start(bf16[512,128]{1,0:T(8,128)(2,1)S(1)} %get-tuple-element.116), channel_id=1, source_target_pairs={{64,32},{65,33},{66,34},{67,35},{68,36},{69,37},{70,38},{71,39},{7... | collective-permute-start | bytes 393224 | tf_op jit(solution)/shard_map/ppermute | solution.py:444
  7.9 4.7 %collective-permute-start.7 = (bf16[512,128]{1,0:T(8,128)(2,1)S(1)}, bf16[512,128]{1,0:T(8,128)(2,1)S(1)}, u32[]{:S(2)}, u32[]{:S(2)}) collective-permute-start(bf16[512,128]{1,0:T(8,128)(2,1)S(1)} %get-tuple-element.119), channel_id=1, source_target_pairs={{64,32},{65,33},{66,34},{67,35},{68,36},{69,37},{70,38},{71,39},{7... | collective-permute-start | bytes 393224 | tf_op jit(solution)/shard_map/ppermute | solution.py:444
  8.6 12.3 %collective-permute-start.9 = (bf16[512,128]{1,0:T(8,128)(2,1)S(1)}, bf16[512,128]{1,0:T(8,128)(2,1)S(1)}, u32[]{:S(2)}, u32[]{:S(2)}) collective-permute-start(bf16[512,128]{1,0:T(8,128)(2,1)S(1)} %get-tuple-element.123), channel_id=1, source_target_pairs={{32,0},{33,1},{34,2},{35,3},{36,4},{37,5},{38,6},{39,7},{40,8},{41... | collective-permute-start | bytes 393224 | tf_op jit(solution)/shard_map/ppermute | solution.py:444
  9.9 15.8 %collective-permute-start.10 = (bf16[512,128]{1,0:T(8,128)(2,1)S(1)}, bf16[512,128]{1,0:T(8,128)(2,1)S(1)}, u32[]{:S(2)}, u32[]{:S(2)}) collective-permute-start(bf16[512,128]{1,0:T(8,128)(2,1)S(1)} %get-tuple-element.126), channel_id=1, source_target_pairs={{32,0},{33,1},{34,2},{35,3},{36,4},{37,5},{38,6},{39,7},{40,8},{41... | collective-permute-start | bytes 393224 | tf_op jit(solution)/shard_map/ppermute | solution.py:444
  11.2 17.3 %collective-permute-start.11 = (bf16[512,128]{1,0:T(8,128)(2,1)S(1)}, bf16[512,128]{1,0:T(8,128)(2,1)S(1)}, u32[]{:S(2)}, u32[]{:S(2)}) collective-permute-start(bf16[512,128]{1,0:T(8,128)(2,1)S(1)} %get-tuple-element.129), channel_id=1, source_target_pairs={{32,0},{33,1},{34,2},{35,3},{36,4},{37,5},{38,6},{39,7},{40,8},{41... | collective-permute-start | bytes 393224 | tf_op jit(solution)/shard_map/ppermute | solution.py:444
  12.6 19.2 %collective-permute-start.8 = (bf16[512,128]{1,0:T(8,128)(2,1)S(1)}, bf16[512,128]{1,0:T(8,128)(2,1)S(1)}, u32[]{:S(2)}, u32[]{:S(2)}) collective-permute-start(bf16[512,128]{1,0:T(8,128)(2,1)S(1)} %get-tuple-element.120), channel_id=1, source_target_pairs={{32,0},{33,1},{34,2},{35,3},{36,4},{37,5},{38,6},{39,7},{40,8},{41... | collective-permute-start | bytes 393224 | tf_op jit(solution)/shard_map/ppermute | solution.py:444
  21.8 12.9 %collective-permute-start.12 = (bf16[512,128]{1,0:T(8,128)(2,1)S(1)}, bf16[512,128]{1,0:T(8,128)(2,1)S(1)}, u32[]{:S(2)}, u32[]{:S(2)}) collective-permute-start(bf16[512,128]{1,0:T(8,128)(2,1)S(1)} %get-tuple-element.140), channel_id=1, source_target_pairs={{0,2},{1,3},{2,4},{3,5},{4,6},{5,7},{6,8},{7,9},{8,10},{9,11},{10,... | collective-permute-start | bytes 393224 | tf_op jit(solution)/shard_map/ppermute | solution.py:418
  26.7 11.4 %collective-permute-start.17 = (bf16[512,128]{1,0:T(8,128)(2,1)S(1)}, bf16[512,128]{1,0:T(8,128)(2,1)S(1)}, u32[]{:S(2)}, u32[]{:S(2)}) collective-permute-start(bf16[512,128]{1,0:T(8,128)(2,1)S(1)} %get-tuple-element.145), channel_id=1, source_target_pairs={{0,2},{1,3},{2,4},{3,5},{4,6},{5,7},{6,8},{7,9},{8,10},{9,11},{10,... | collective-permute-start | bytes 393224 | tf_op jit(solution)/shard_map/ppermute | solution.py:418
  34.6 3.9 %collective-permute-start.13 = (bf16[48,1152]{1,0:T(8,128)(2,1)S(1)}, bf16[48,1152]{1,0:T(8,128)(2,1)S(1)}, u32[]{:S(2)}, u32[]{:S(2)}) collective-permute-start(bf16[48,1152]{1,0:T(8,128)(2,1)S(1)} %get-tuple-element.141), channel_id=1, source_target_pairs={{0,1},{1,0},{2,3},{3,2},{4,5},{5,4},{6,7},{7,6},{8,9},{9,8},{10,11... | collective-permute-start | bytes 331784 | tf_op jit(solution)/shard_map/ppermute | solution.py:413
  38.1 7.4 %collective-permute-start.23 = (bf16[512,128]{1,0:T(8,128)(2,1)S(1)}, bf16[512,128]{1,0:T(8,128)(2,1)S(1)}, u32[]{:S(2)}, u32[]{:S(2)}) collective-permute-start(bf16[512,128]{1,0:T(8,128)(2,1)S(1)} %get-tuple-element.155), channel_id=1, source_target_pairs={{0,2},{1,3},{2,4},{3,5},{4,6},{5,7},{6,8},{7,9},{8,10},{9,11},{10,... | collective-permute-start | bytes 393224 | tf_op jit(solution)/shard_map/ppermute | solution.py:418
  39.4 8.4 %collective-permute-start.18 = (bf16[48,1152]{1,0:T(8,128)(2,1)S(1)}, bf16[48,1152]{1,0:T(8,128)(2,1)S(1)}, u32[]{:S(2)}, u32[]{:S(2)}) collective-permute-start(bf16[48,1152]{1,0:T(8,128)(2,1)S(1)} %add_convert_fusion.4), channel_id=1, source_target_pairs={{0,8},{1,9},{2,10},{3,11},{4,12},{5,13},{6,14},{7,15},{8,0},{9,1},... | collective-permute-start | bytes 331784 | tf_op jit(solution)/shard_map/ppermute | solution.py:413
  40.0 7.9 %collective-permute-start.19 = (bf16[48,1152]{1,0:T(8,128)(2,1)S(1)}, bf16[48,1152]{1,0:T(8,128)(2,1)S(1)}, u32[]{:S(2)}, u32[]{:S(2)}) collective-permute-start(bf16[48,1152]{1,0:T(8,128)(2,1)S(1)} %add_convert_fusion.3), channel_id=1, source_target_pairs={{0,10},{1,11},{2,8},{3,9},{4,14},{5,15},{6,12},{7,13},{8,2},{9,3},... | collective-permute-start | bytes 331784 | tf_op jit(solution)/shard_map/ppermute | solution.py:413
  41.6 6.7 %collective-permute-start.20 = (bf16[48,1152]{1,0:T(8,128)(2,1)S(1)}, bf16[48,1152]{1,0:T(8,128)(2,1)S(1)}, u32[]{:S(2)}, u32[]{:S(2)}) collective-permute-start(bf16[48,1152]{1,0:T(8,128)(2,1)S(1)} %add_convert_fusion.2), channel_id=1, source_target_pairs={{0,2},{1,3},{2,0},{3,1},{4,6},{5,7},{6,4},{7,5},{8,10},{9,11},{10,... | collective-permute-start | bytes 331784 | tf_op jit(solution)/shard_map/ppermute | solution.py:413
  43.2 14.9 %collective-permute-start.32 = (bf16[512,128]{1,0:T(8,128)(2,1)S(1)}, bf16[512,128]{1,0:T(8,128)(2,1)S(1)}, u32[]{:S(2)}, u32[]{:S(2)}) collective-permute-start(bf16[512,128]{1,0:T(8,128)(2,1)S(1)} %last_grad.1.gin), channel_id=1, source_target_pairs={{0,2},{1,3},{2,4},{3,5},{4,6},{5,7},{6,8},{7,9},{8,10},{9,11},{10,... | collective-permute-start | bytes 393224 | tf_op jit(solution)/shard_map/ppermute | solution.py:418
  49.4 8.8 %collective-permute-start.27 = (bf16[48,1152]{1,0:T(8,128)(2,1)S(1)}, bf16[48,1152]{1,0:T(8,128)(2,1)S(1)}, u32[]{:S(2)}, u32[]{:S(2)}) collective-permute-start(bf16[48,1152]{1,0:T(8,128)(2,1)S(1)} %add_convert_fusion.1), channel_id=1, source_target_pairs={{0,6},{1,7},{2,4},{3,5},{4,2},{5,3},{6,0},{7,1},{8,14},{9,15},{10,... | collective-permute-start | bytes 331784 | tf_op jit(solution)/shard_map/ppermute | solution.py:413
  50.9 7.3 %collective-permute-start.26 = (bf16[48,1152]{1,0:T(8,128)(2,1)S(1)}, bf16[48,1152]{1,0:T(8,128)(2,1)S(1)}, u32[]{:S(2)}, u32[]{:S(2)}) collective-permute-start(bf16[48,1152]{1,0:T(8,128)(2,1)S(1)} %add_convert_fusion.1), channel_id=1, source_target_pairs={{0,30},{1,31},{2,28},{3,29},{4,26},{5,27},{6,24},{7,25},{8,22},{9,... | collective-permute-start | bytes 331784 | tf_op jit(solution)/shard_map/ppermute | solution.py:413
  54.1 5.3 %collective-permute-start.25 = (bf16[48,1152]{1,0:T(8,128)(2,1)S(1)}, bf16[48,1152]{1,0:T(8,128)(2,1)S(1)}, u32[]{:S(2)}, u32[]{:S(2)}) collective-permute-start(bf16[48,1152]{1,0:T(8,128)(2,1)S(1)} %add_convert_fusion.1), channel_id=1, source_target_pairs={{0,24},{1,25},{2,26},{3,27},{4,28},{5,29},{6,30},{7,31},{8,16},{9,... | collective-permute-start | bytes 331784 | tf_op jit(solution)/shard_map/ppermute | solution.py:413
  55.2 7.0 %collective-permute-start.31 = (bf16[2,512,128]{2,1,0:T(8,128)(2,1)S(1)}, bf16[2,512,128]{2,1,0:T(8,128)(2,1)S(1)}, u32[]{:S(2)}, u32[]{:S(2)}) collective-permute-start(bf16[2,512,128]{2,1,0:T(8,128)(2,1)S(1)} %get-tuple-element.160), channel_id=1, source_target_pairs={{0,1},{1,4},{2,3},{3,6},{4,5},{5,8},{6,7},{7,10},{8,9},{9,12},{10,... | collective-permute-start | bytes 786440 | tf_op jit(solution)/shard_map/ppermute | solution.py:456
  58.2 4.0 %collective-permute-start.33 = (bf16[512,128]{1,0:T(8,128)(2,1)S(1)}, bf16[512,128]{1,0:T(8,128)(2,1)S(1)}, u32[]{:S(2)}, u32[]{:S(2)}) collective-permute-start(bf16[512,128]{1,0:T(8,128)(2,1)S(1)} %collective-permute-done.32.refs_3_), channel_id=1, source_target_pairs={{0,1},{1,0},{2,3},{3,2},{4,5},{5,4},{6,7},{7,6},{8,9},{9,8},{10,11... | collective-permute-start | bytes 393224 | tf_op jit(solution)/shard_map/ppermute | solution.py:413
  59.4 8.9 %collective-permute-start.30 = (bf16[48,1152]{1,0:T(8,128)(2,1)S(1)}, bf16[48,1152]{1,0:T(8,128)(2,1)S(1)}, u32[]{:S(2)}, u32[]{:S(2)}) collective-permute-start(bf16[48,1152]{1,0:T(8,128)(2,1)S(1)} %add_convert_fusion.refs_0_), channel_id=1, source_target_pairs={{0,10},{1,11},{2,8},{3,9},{4,14},{5,15},{6,12},{7,13},{8,2},{9,3},... | collective-permute-start | bytes 331784 | tf_op jit(solution)/shard_map/ppermute | solution.py:413
  59.6 8.7 %collective-permute-start.29 = (bf16[48,1152]{1,0:T(8,128)(2,1)S(1)}, bf16[48,1152]{1,0:T(8,128)(2,1)S(1)}, u32[]{:S(2)}, u32[]{:S(2)}) collective-permute-start(bf16[48,1152]{1,0:T(8,128)(2,1)S(1)} %add_convert_fusion.refs_0_), channel_id=1, source_target_pairs={{0,8},{1,9},{2,10},{3,11},{4,12},{5,13},{6,14},{7,15},{8,0},{9,1},... | collective-permute-start | bytes 331784 | tf_op jit(solution)/shard_map/ppermute | solution.py:413
  61.3 7.0 %collective-permute-start.28 = (bf16[48,1152]{1,0:T(8,128)(2,1)S(1)}, bf16[48,1152]{1,0:T(8,128)(2,1)S(1)}, u32[]{:S(2)}, u32[]{:S(2)}) collective-permute-start(bf16[48,1152]{1,0:T(8,128)(2,1)S(1)} %add_convert_fusion.refs_0_), channel_id=1, source_target_pairs={{0,2},{1,3},{2,0},{3,1},{4,6},{5,7},{6,4},{7,5},{8,10},{9,11},{10,... | collective-permute-start | bytes 331784 | tf_op jit(solution)/shard_map/ppermute | solution.py:413
  63.7 6.7 %collective-permute-start.34 = (bf16[48,1152]{1,0:T(8,128)(2,1)S(1)}, bf16[48,1152]{1,0:T(8,128)(2,1)S(1)}, u32[]{:S(2)}, u32[]{:S(2)}) collective-permute-start(bf16[48,1152]{1,0:T(8,128)(2,1)S(1)} %add_convert_fusion.refs_0_), channel_id=1, source_target_pairs={{0,1},{1,0},{2,3},{3,2},{4,5},{5,4},{6,7},{7,6},{8,9},{9,8},{10,11... | collective-permute-start | bytes 331784 | tf_op jit(solution)/shard_map/ppermute | solution.py:413
  (16 other events, 45.6 us)
